TPU v7x, 32 devices: a whole 2x2x4 slice. The times are simulated.
32 devices in a mesh: row: 4 (over z), col: 4 (over y, x), section: 2 (over core).
Axes of the slice: x: 2, y: 2, z: 4, core: 2. Of those that a mesh axis runs over, the one named last changes fastest.
Arguments:
- hidden_in: bfloat16 [512, 8192], P(('col', 'section'), 'row'), may hold values from -6 to 6
- norm_gain: float32 [8192], P('row'), may hold values from 0.2 to 4
- gate_weight: bfloat16 [8192, 14336], P('row', ('col', 'section')), may hold values from -0.0625 to 0.0625
- up_weight: bfloat16 [8192, 14336], P('row', ('col', 'section')), may hold values from -0.0625 to 0.0625
- down_weight: bfloat16 [14336, 8192], P(('col', 'section'), 'row'), may hold values from -0.046875 to 0.046875
- proj_weight: bfloat16 [8192, 16384], P('row', ('col', 'section')), may hold values from -0.0625 to 0.0625
- teacher_out: bfloat16 [512, 16384], P(('row', 'col', 'section')), may hold values from -16 to 16
- loss_mask: int32 [512], P('row'), may hold values from 0 to 1, as said below
Outputs:
- loss_value: float32 [], replicated
- grad_gain: float32 [8192], P('row')
- grad_gate: float32 [8192, 14336], P('row', ('col', 'section'))
- grad_up: float32 [8192, 14336], P('row', ('col', 'section'))
- grad_down: float32 [14336, 8192], P(('col', 'section'), 'row')
- grad_proj: float32 [8192, 16384], P('row', ('col', 'section'))
- grad_input: float32 [512, 8192], P(('col', 'section'), 'row')
Inputs may be any that keep to these rules, and one draw needn't show every extreme that they name: `loss_mask`: the last token is always kept.
All inputs are finite; a program needn't handle non-finite values.
Results may differ from a plain program's by a relative error of at most 0.033.
Values may be sent and summed in bfloat16 or wider, within the bound.
No kernel may reach another device: no remote copies, remote signals or barrier semaphores. Data moves between devices by JAX's collectives and lax.ppermute only.
A program may use at most 192 MiB of HBM per device.

v0:
```python
import functools

import jax
import jax.numpy as jnp
from jax import lax
from jax.experimental import pallas as pl
from jax.experimental.pallas import tpu as pltpu
from jax.sharding import PartitionSpec as P

PLANE = ("col", "section")
F32 = jnp.float32
BF16 = jnp.bfloat16


def mm(left, right):
    return jnp.dot(left, right, preferred_element_type=F32)


def mm_t(left, right):
    return lax.dot_general(left, right, (((1,), (1,)), ((), ())), preferred_element_type=F32)


def grad_kernel(places, tile, *refs):
    out_ref, left, right, sems = refs[-4:]
    pieces = refs[:-4]

    @pl.when(pl.program_id(0) == 0)
    def load():
        copies = []
        for i, (piece, (side, row, column)) in enumerate(zip(pieces, places)):
            to = (left, right)[side].at[pl.ds(row, piece.shape[0]), pl.ds(column, piece.shape[1])]
            copies.append(pltpu.make_async_copy(piece, to, sems.at[i]))
        for copy in copies:
            copy.start()
        for copy in copies:
            copy.wait()

    columns = pl.ds(pl.multiple_of(pl.program_id(0) * tile, tile), tile)
    out_ref[...] = lax.dot_general(
        left[:, columns], right[...], (((0,), (0,)), ((), ())), preferred_element_type=F32
    )


def weight_grad(lefts, rights):
    places, pieces, shapes = [], [], []
    for side, grid in enumerate((lefts, rights)):
        row = 0
        for line in grid:
            column = 0
            for piece in line:
                places.append((side, row, column))
                pieces.append(piece)
                column += piece.shape[1]
            row += line[0].shape[0]
        shapes.append((row, column))
    (depth, m), (_, n) = shapes
    tile = 256 if m % 256 == 0 else 128
    return pl.pallas_call(
        functools.partial(grad_kernel, places, tile),
        grid=(m // tile,),
        in_specs=[pl.BlockSpec(memory_space=pl.ANY)] * len(pieces),
        out_specs=pl.BlockSpec((tile, n), lambda i: (i, 0)),
        out_shape=jax.ShapeDtypeStruct((m, n), F32),
        scratch_shapes=[
            pltpu.VMEM((depth, m), BF16),
            pltpu.VMEM((depth, n), BF16),
            pltpu.SemaphoreType.DMA((len(pieces),)),
        ],
        compiler_params=pltpu.CompilerParams(vmem_limit_bytes=14 << 20),
        cost_estimate=pl.CostEstimate(
            flops=2 * depth * m * n,
            bytes_accessed=2 * depth * (m + n) + 4 * m * n,
            transcendentals=0,
        ),
    )(*pieces)


def reverse_bits(value, width):
    out = 0
    for bit in range(width):
        out |= ((value >> bit) & 1) << (width - 1 - bit)
    return out


def after(value, earlier):
    first = earlier[(0,) * earlier.ndim]
    return jnp.where(first == first, value, jnp.zeros_like(value))


def halves(size):
    middle = -(-size // 256) * 128
    return [(0, middle), (middle, size)]


class Plane:
    def __init__(self, size):
        self.size = size
        self.width = (size // 2).bit_length() - 1
        assert 2 << self.width == size
        self.rev = [reverse_bits(k, self.width) for k in range(size // 2)]
        self.perms = []
        for step in range(self.width):
            even, odd = 2 << step, 2 << (self.width - 1 - step)
            self.perms.append([(c, c ^ (odd if c & 1 else even)) for c in range(size)])
        self.swap = [(c, c ^ 1) for c in range(size)]

    def gather(self, block):
        own = block
        for perm in self.perms:
            own = jnp.concatenate([own, lax.ppermute(own, PLANE, perm)], axis=0)
        return own, lax.ppermute(own, PLANE, self.swap)

    def scatter(self, full):
        b = full.shape[0] // self.size
        block = lambda i: full[i * b : (i + 1) * b]
        half = self.size // 2
        mine = jnp.concatenate([block(2 * k) for k in range(half)], axis=0)
        send = jnp.concatenate([block(2 * self.rev[k] + 1) for k in range(half)], axis=0)
        got = lax.ppermute(send, PLANE, self.swap)
        acc = mine.astype(F32) + got.astype(F32)
        for perm in reversed(self.perms):
            half = acc.shape[0] // 2
            got = lax.ppermute(acc[half:].astype(full.dtype), PLANE, perm)
            acc = acc[:half] + got.astype(F32)
        return acc

    def total(self, value):
        for perm in self.perms + [self.swap]:
            value = value + lax.ppermute(value, PLANE, perm)
        return value


class Rows:
    def __init__(self, size, plane):
        self.size = size
        self.ring = [(r, (r + 1) % size) for r in range(size)]
        self.me = lax.axis_index("row")
        c = lax.axis_index(PLANE)
        self.odd = (c & 1) == 1
        self.slots = []
        for back in range(size):
            k = (c >> 1) ^ lax.rem(self.me + (size - back), size)
            flipped = jnp.asarray(plane.rev, jnp.int32)[k]
            self.slots.append((jnp.where(self.odd, flipped, k), jnp.where(self.odd, k, flipped)))

    def parts(self, own, other):
        b = own.shape[0] // self.size
        return [
            [
                lax.dynamic_slice_in_dim(own, at * b, b, 0),
                lax.dynamic_slice_in_dim(other, at_other * b, b, 0),
            ]
            for at, at_other in self.slots
        ]

    def place(self, full, block, back):
        rows = block.shape[0]
        return lax.dynamic_update_slice_in_dim(full, block, self.slots[back][0] * rows, 0)

    def shift(self, value):
        return lax.ppermute(value, "row", self.ring)

    def reduce(self, parts, products):
        got, first = None, None
        for back in range(1, self.size + 1):
            rows = jnp.concatenate(parts[back % self.size], axis=0)
            sums = [product(rows) for product in products]
            if got is not None:
                sums = [s + g.astype(F32) for s, g in zip(sums, got)]
            if back < self.size:
                got = [self.shift(s.astype(BF16)) for s in sums]
                first = got[0] if first is None else first
        return sums, first

    def gather(self, blocks, product, beside=None):
        steps = [blocks]
        for back in range(1, self.size):
            sent = steps[-1]
            if back == 2 and beside is not None:
                sent = sent[:-1] + [after(sent[-1], beside)]
            steps.append([self.shift(b) for b in sent])
        made = [product(step) for step in steps]
        return steps, made, self.placed(made)

    def placed(self, blocks):
        out = jnp.zeros((blocks[0].shape[0] * self.size,) + blocks[0].shape[1:], blocks[0].dtype)
        for back, block in enumerate(blocks):
            out = self.place(out, block, back)
        return out

    def total(self, value):
        step = 1
        while step < self.size:
            value = value + lax.ppermute(value, "row", [(r, r ^ step) for r in range(self.size)])
            step *= 2
        return value

    def own_order(self, value):
        half = value.shape[0] // 2
        return jnp.where(self.odd, jnp.concatenate([value[half:], value[:half]], axis=0), value)


def lines(parts):
    return [[piece] for part in parts for piece in part]


def make_body(n_row, n_plane):
    plane = Plane(n_plane)
    assert n_plane == 2 * n_row

    def body(x, gain, gate_w, up_w, down_w, proj_w, teacher, loss_mask):
        rows = Rows(n_row, plane)
        block = x.shape[0]
        features = x.shape[1] * n_row

        own, other = plane.gather((x.astype(F32) * gain[None, :]).astype(BF16))
        scaled = rows.parts(own, other)
        (gate, up), moved = rows.reduce(scaled, [lambda a: mm(a, gate_w), lambda a: mm(a, up_w)])
        squares = [jnp.sum(jnp.square(p.astype(F32) / gain[None, :]), axis=1) for p in (own, other)]
        squares = rows.total(after(jnp.concatenate(squares), moved))
        inv_all = lax.rsqrt(squares / features + 1e-05)
        inv = jnp.concatenate(rows.parts(*jnp.split(inv_all, 2))[0])[:, None]

        target = lax.all_to_all(
            after(teacher, moved), PLANE, split_axis=1, concat_axis=0, tiled=True
        )
        target = rows.own_order(target).astype(F32)
        keep = rows.own_order(loss_mask.astype(F32))
        inv = after(inv, target)
        gate, up = gate * inv, up * inv
        sigma = jax.nn.sigmoid(gate)
        activated = gate * sigma
        hidden = (activated * up).astype(BF16)
        cuts = halves(hidden.shape[1])
        hiddens, _, ffn = rows.gather(
            [hidden[:, lo:hi] for lo, hi in cuts],
            lambda bs: sum(mm(b, down_w[lo:hi]) for b, (lo, hi) in zip(bs, cuts)).astype(BF16),
        )
        residual = (x.astype(F32) + plane.scatter(ffn)).astype(BF16)
        residuals = rows.parts(*plane.gather(residual))

        ecuts = halves(proj_w.shape[1])
        predicted, _ = rows.reduce(
            residuals, [lambda a, lo=lo, hi=hi: mm(a, proj_w[:, lo:hi]) for lo, hi in ecuts]
        )
        error = [p - target[:, lo:hi] for p, (lo, hi) in zip(predicted, ecuts)]
        masked = [e * keep[:, None] for e in error]

        pred_grads, _, back = rows.gather(
            [m.astype(BF16) for m in masked],
            lambda bs: sum(mm_t(b, proj_w[:, lo:hi]) for b, (lo, hi) in zip(bs, ecuts)).astype(BF16),
        )
        resid_grad = plane.scatter(back).astype(BF16)
        resid_grads = rows.parts(*plane.gather(resid_grad))

        hid_grad, _ = rows.reduce(
            resid_grads, [lambda a, lo=lo, hi=hi: mm_t(a, down_w[lo:hi]) for lo, hi in cuts]
        )
        hid_grad = jnp.concatenate(hid_grad, axis=1)
        gate_grad = hid_grad * up * (sigma * (1.0 + gate * (1.0 - sigma)))
        up_grad = hid_grad * activated
        blocks = [(gate_grad * inv).astype(BF16), (up_grad * inv).astype(BF16)]

        def held(parts):
            return [[after(p, blocks[1]) for p in parts[0]]] + parts[1:]

        grad_proj = weight_grad(lines(held(residuals)), pred_grads)
        grad_down = weight_grad(hiddens, lines(held(resid_grads)))
        grads, made, back = rows.gather(
            blocks,
            lambda b: (mm_t(b[0], gate_w) + mm_t(b[1], up_w)).astype(BF16),
            grad_proj[:1, :1] + grad_down[:1, :1],
        )
        normed_grad = plane.scatter(back)
        inner = jnp.sum(normed_grad * gain[None, :] * x.astype(F32), axis=1)
        loss_sum = 0.5 * sum(jnp.sum(m * e) for m, e in zip(masked, error))
        loss_parts = jnp.stack([loss_sum, jnp.sum(keep)])
        gain_sum = sum(
            jnp.sum(m.astype(F32) * jnp.concatenate(p, axis=0).astype(F32), axis=0)
            for m, p in zip(made, scaled)
        )
        sums = plane.total(jnp.concatenate([gain_sum / gain, loss_parts]))
        grad_gain = sums[:-2]
        sums = rows.total(jnp.concatenate([inner, sums[-2:]]))
        inner = sums[:-2]
        loss_value = sums[-2] / (sums[-1] / n_plane)

        grad_gate = weight_grad(lines(scaled), [g[:1] for g in grads])
        grad_up = weight_grad(lines(scaled), [g[1:] for g in grads])

        inv_own = inv_all[:block]
        grad_input = (
            resid_grad.astype(F32)
            + gain[None, :] * normed_grad
            - x.astype(F32) * (inv_own * inv_own * inner / features)[:, None]
        )
        return (loss_value, grad_gain, grad_gate, grad_up, grad_down, grad_proj, grad_input)

    return body


def solution(mesh):
    in_specs = (
        P(PLANE, "row"),
        P("row"),
        P("row", PLANE),
        P("row", PLANE),
        P(PLANE, "row"),
        P("row", PLANE),
        P(("row", "col", "section"), None),
        P("row"),
    )
    out_specs = (
        P(),
        P("row"),
        P("row", PLANE),
        P("row", PLANE),
        P(PLANE, "row"),
        P("row", PLANE),
        P(PLANE, "row"),
    )
    body = make_body(mesh.shape["row"], mesh.shape["col"] * mesh.shape["section"])
    return jax.shard_map(body, mesh=mesh, in_specs=in_specs, out_specs=out_specs, check_vma=False)
```

profile of v0, /device:TPU:0, one launch (start us, length us, event | category | flops | bytes accessed | tf_op | source)
XLA Modules:
  0.0 469.0 jit_solution(5069444134374095932)
XLA Ops:
  11.2 7.2 %collective-permute-done.1 = bf16[128,2048]{1,0:T(8,128)(2,1)S(1)} collective-permute-done((bf16[128,2048]{1,0:T(8,128)(2,1)S(1)}, bf16[128,2048]{1,0:T(8,128)(2,1)S(1)}, u32[]{:S(2)}, u32[]{:S(2)}) %collective-permute-start.1) | collective-permute-done | bytes 524320 | tf_op jit(solution)/shard_map/ppermute | solution.py:110
  35.4 11.2 %collective-permute-done.3 = bf16[128,1792]{1,0:T(8,128)(2,1)S(1)} collective-permute-done((bf16[128,1792]{1,0:T(8,128)(2,1)S(1)}, bf16[128,1792]{1,0:T(8,128)(2,1)S(1)}, u32[]{:S(2)}, u32[]{:S(2)}) %collective-permute-start.3) | collective-permute-done | bytes 458784 | tf_op jit(solution)/shard_map/ppermute | solution.py:161
  51.8 4.7 collective-permute-done.8
  65.5 7.7 %collective-permute-done.7 = f32[512]{0:T(512)} collective-permute-done((f32[512]{0:T(512)S(1)}, f32[512]{0:T(512)}, u32[]{:S(2)}, u32[]{:S(2)}) %collective-permute-start.7) | collective-permute-done | bytes 2080 | tf_op jit(solution)/shard_map/ppermute | solution.py:194
  90.8 4.5 collective-permute-done.5
  95.4 4.4 fusion.1
  109.5 9.5 %collective-permute-done.12.refs_3_ = bf16[128,896]{1,0:T(8,128)(2,1)S(1)} collective-permute-done((bf16[128,896]{1,0:T(8,128)(2,1)S(1)}, bf16[128,896]{1,0:T(8,128)(2,1)S(1)}, u32[]{:S(2)}, u32[]{:S(2)}) %collective-permute-start.12) | collective-permute-done | bytes 229408 | tf_op jit(solution)/shard_map/ppermute | solution.py:161
  120.6 8.6 %collective-permute-done.14.refs_5_ = bf16[128,896]{1,0:T(8,128)(2,1)S(1)} collective-permute-done((bf16[128,896]{1,0:T(8,128)(2,1)S(1)}, bf16[128,896]{1,0:T(8,128)(2,1)S(1)}, u32[]{:S(2)}, u32[]{:S(2)}) %collective-permute-start.14) | collective-permute-done | bytes 229408 | tf_op jit(solution)/shard_map/ppermute | solution.py:161
  147.6 7.7 %collective-permute-done.18 = bf16[128,2048]{1,0:T(8,128)(2,1)S(1)} collective-permute-done((bf16[128,2048]{1,0:T(8,128)(2,1)S(1)}, bf16[128,2048]{1,0:T(8,128)(2,1)S(1)}, u32[]{:S(2)}, u32[]{:S(2)}) %collective-permute-start.18) | collective-permute-done | bytes 524320 | tf_op jit(solution)/shard_map/ppermute | solution.py:123
  157.1 4.9 %collective-permute-done.19 = bf16[64,2048]{1,0:T(8,128)(2,1)S(1)} collective-permute-done((bf16[64,2048]{1,0:T(8,128)(2,1)S(1)}, bf16[64,2048]{1,0:T(8,128)(2,1)S(1)}, u32[]{:S(2)}, u32[]{:S(2)}) %collective-permute-start.19) | collective-permute-done | bytes 262176 | tf_op jit(solution)/shard_map/ppermute | solution.py:123
  163.6 4.9 %collective-permute-done.20 = bf16[64,2048]{1,0:T(8,128)(2,1)S(1)} collective-permute-done((bf16[64,2048]{1,0:T(8,128)(2,1)S(1)}, bf16[64,2048]{1,0:T(8,128)(2,1)S(1)}, u32[]{:S(2)}, u32[]{:S(2)}) %collective-permute-start.20) | collective-permute-done | bytes 262176 | tf_op jit(solution)/shard_map/ppermute | solution.py:110
  170.1 7.7 %collective-permute-done.21 = bf16[128,2048]{1,0:T(8,128)(2,1)S(1)} collective-permute-done((bf16[128,2048]{1,0:T(8,128)(2,1)S(1)}, bf16[128,2048]{1,0:T(8,128)(2,1)S(1)}, u32[]{:S(2)}, u32[]{:S(2)}) %collective-permute-start.21) | collective-permute-done | bytes 524320 | tf_op jit(solution)/shard_map/ppermute | solution.py:110
  182.3 10.1 %collective-permute-done.23 = bf16[128,1024]{1,0:T(8,128)(2,1)S(1)} collective-permute-done((bf16[128,1024]{1,0:T(8,128)(2,1)S(1)}, bf16[128,1024]{1,0:T(8,128)(2,1)S(1)}, u32[]{:S(2)}, u32[]{:S(2)}) %collective-permute-start.23) | collective-permute-done | bytes 262176 | tf_op jit(solution)/shard_map/ppermute | solution.py:161
  193.3 4.8 %collective-permute-done.26 = bf16[128,1024]{1,0:T(8,128)(2,1)S(1)} collective-permute-done((bf16[128,1024]{1,0:T(8,128)(2,1)S(1)}, bf16[128,1024]{1,0:T(8,128)(2,1)S(1)}, u32[]{:S(2)}, u32[]{:S(2)}) %collective-permute-start.26) | collective-permute-done | bytes 262176 | tf_op jit(solution)/shard_map/ppermute | solution.py:161
  198.9 5.1 %collective-permute-done.24 = bf16[128,1024]{1,0:T(8,128)(2,1)S(1)} collective-permute-done((bf16[128,1024]{1,0:T(8,128)(2,1)S(1)}, bf16[128,1024]{1,0:T(8,128)(2,1)S(1)}, u32[]{:S(2)}, u32[]{:S(2)}) %collective-permute-start.24) | collective-permute-done | bytes 262176 | tf_op jit(solution)/shard_map/ppermute | solution.py:161
  204.8 5.1 %collective-permute-done.27 = bf16[128,1024]{1,0:T(8,128)(2,1)S(1)} collective-permute-done((bf16[128,1024]{1,0:T(8,128)(2,1)S(1)}, bf16[128,1024]{1,0:T(8,128)(2,1)S(1)}, u32[]{:S(2)}, u32[]{:S(2)}) %collective-permute-start.27) | collective-permute-done | bytes 262176 | tf_op jit(solution)/shard_map/ppermute | solution.py:161
  224.7 10.0 %collective-permute-done.30.refs_11_ = bf16[128,1024]{1,0:T(8,128)(2,1)S(1)} collective-permute-done((bf16[128,1024]{1,0:T(8,128)(2,1)S(1)}, bf16[128,1024]{1,0:T(8,128)(2,1)S(1)}, u32[]{:S(2)}, u32[]{:S(2)}) %collective-permute-start.30) | collective-permute-done | bytes 262176 | tf_op jit(solution)/shard_map/ppermute | solution.py:161
  237.8 7.8 %collective-permute-done.32.refs_13_ = bf16[128,1024]{1,0:T(8,128)(2,1)S(1)} collective-permute-done((bf16[128,1024]{1,0:T(8,128)(2,1)S(1)}, bf16[128,1024]{1,0:T(8,128)(2,1)S(1)}, u32[]{:S(2)}, u32[]{:S(2)}) %collective-permute-start.32) | collective-permute-done | bytes 262176 | tf_op jit(solution)/shard_map/ppermute | solution.py:161
  266.1 7.7 %collective-permute-done.36 = bf16[128,2048]{1,0:T(8,128)(2,1)S(1)} collective-permute-done((bf16[128,2048]{1,0:T(8,128)(2,1)S(1)}, bf16[128,2048]{1,0:T(8,128)(2,1)S(1)}, u32[]{:S(2)}, u32[]{:S(2)}) %collective-permute-start.36) | collective-permute-done | bytes 524320 | tf_op jit(solution)/shard_map/ppermute | solution.py:123
  275.5 4.9 %collective-permute-done.37 = bf16[64,2048]{1,0:T(8,128)(2,1)S(1)} collective-permute-done((bf16[64,2048]{1,0:T(8,128)(2,1)S(1)}, bf16[64,2048]{1,0:T(8,128)(2,1)S(1)}, u32[]{:S(2)}, u32[]{:S(2)}) %collective-permute-start.37) | collective-permute-done | bytes 262176 | tf_op jit(solution)/shard_map/ppermute | solution.py:123
  282.0 4.9 %collective-permute-done.38 = bf16[64,2048]{1,0:T(8,128)(2,1)S(1)} collective-permute-done((bf16[64,2048]{1,0:T(8,128)(2,1)S(1)}, bf16[64,2048]{1,0:T(8,128)(2,1)S(1)}, u32[]{:S(2)}, u32[]{:S(2)}) %collective-permute-start.38) | collective-permute-done | bytes 262176 | tf_op jit(solution)/shard_map/ppermute | solution.py:110
  288.5 7.7 %collective-permute-done.39 = bf16[128,2048]{1,0:T(8,128)(2,1)S(1)} collective-permute-done((bf16[128,2048]{1,0:T(8,128)(2,1)S(1)}, bf16[128,2048]{1,0:T(8,128)(2,1)S(1)}, u32[]{:S(2)}, u32[]{:S(2)}) %collective-permute-start.39) | collective-permute-done | bytes 524320 | tf_op jit(solution)/shard_map/ppermute | solution.py:110
  301.9 8.9 %collective-permute-done.41 = bf16[128,896]{1,0:T(8,128)(2,1)S(1)} collective-permute-done((bf16[128,896]{1,0:T(8,128)(2,1)S(1)}, bf16[128,896]{1,0:T(8,128)(2,1)S(1)}, u32[]{:S(2)}, u32[]{:S(2)}) %collective-permute-start.41) | collective-permute-done | bytes 229408 | tf_op jit(solution)/shard_map/ppermute | solution.py:161
  321.3 5.3 %collective-permute-done.45 = bf16[128,896]{1,0:T(8,128)(2,1)S(1)} collective-permute-done((bf16[128,896]{1,0:T(8,128)(2,1)S(1)}, bf16[128,896]{1,0:T(8,128)(2,1)S(1)}, u32[]{:S(2)}, u32[]{:S(2)}) %collective-permute-start.45) | collective-permute-done | bytes 229408 | tf_op jit(solution)/shard_map/ppermute | solution.py:161
  344.9 8.7 %shard_map.172 = f32[1792,2048]{1,0:T(8,128)} custom-call(bf16[128,896]{1,0:T(8,128)(2,1)S(1)} %get-tuple-element.67.refs_0_, bf16[128,896]{1,0:T(8,128)(2,1)S(1)} %get-tuple-element.68.refs_1_, bf16[128,896]{1,0:T(8,128)(2,1)S(1)} %collective-permute-done.11.refs_2_, bf16[128,896]{1,0:T(8,128)(2,1)S(1)} %collective-permute-done.12.refs_3_, ...), custom_call_target="tpu_custom_call" | custom-call | flops 3758096384 | bytes 18612224 | tf_op jit(solution)/shard_map/pallas_call | solution.py:58
  354.9 9.5 %shard_map.171 = f32[2048,2048]{1,0:T(8,128)} custom-call(bf16[64,2048]{1,0:T(8,128)(2,1)S(1)} %get-tuple-element.92.refs_0_, bf16[64,2048]{1,0:T(8,128)(2,1)S(1)} %get-tuple-element.91.refs_1_, bf16[64,2048]{1,0:T(8,128)(2,1)S(1)} %get-tuple-element.48.refs_2_, bf16[64,2048]{1,0:T(8,128)(2,1)S(1)} %get-tuple-element.52.refs_3_, ...), custom_call_target="tpu_custom_call" | custom-call | flops 4294967296 | bytes 20971520 | tf_op jit(solution)/shard_map/pallas_call | solution.py:58
  377.2 5.3 %collective-permute-done.50.refs_10_ = bf16[128,1792]{1,0:T(8,128)(2,1)S(1)} collective-permute-done((bf16[128,1792]{1,0:T(8,128)(2,1)S(1)}, bf16[128,1792]{1,0:T(8,128)(2,1)S(1)}, u32[]{:S(2)}, u32[]{:S(2)}) %collective-permute-start.50) | collective-permute-done | bytes 458784 | tf_op jit(solution)/shard_map/ppermute | solution.py:161
  385.6 6.8 %collective-permute-done.49.refs_10_ = bf16[128,1792]{1,0:T(8,128)(2,1)S(1)} collective-permute-done((bf16[128,1792]{1,0:T(8,128)(2,1)S(1)}, bf16[128,1792]{1,0:T(8,128)(2,1)S(1)}, u32[]{:S(2)}, u32[]{:S(2)}) %collective-permute-start.49) | collective-permute-done | bytes 458784 | tf_op jit(solution)/shard_map/ppermute | solution.py:161
  395.7 6.4 %collective-permute-done.52.refs_11_ = bf16[128,1792]{1,0:T(8,128)(2,1)S(1)} collective-permute-done((bf16[128,1792]{1,0:T(8,128)(2,1)S(1)}, bf16[128,1792]{1,0:T(8,128)(2,1)S(1)}, u32[]{:S(2)}, u32[]{:S(2)}) %collective-permute-start.52) | collective-permute-done | bytes 458784 | tf_op jit(solution)/shard_map/ppermute | solution.py:161
  414.7 7.7 %collective-permute-done.54 = bf16[128,2048]{1,0:T(8,128)(2,1)S(1)} collective-permute-done((bf16[128,2048]{1,0:T(8,128)(2,1)S(1)}, bf16[128,2048]{1,0:T(8,128)(2,1)S(1)}, u32[]{:S(2)}, u32[]{:S(2)}) %collective-permute-start.54) | collective-permute-done | bytes 524320 | tf_op jit(solution)/shard_map/ppermute | solution.py:123
  440.9 9.8 %shard_map.173 = f32[2048,1792]{1,0:T(8,128)} custom-call(bf16[64,2048]{1,0:T(8,128)(2,1)S(1)} %get-tuple-element.55.refs_0_, bf16[64,2048]{1,0:T(8,128)(2,1)S(1)} %get-tuple-element.59.refs_1_, bf16[64,2048]{1,0:T(8,128)(2,1)S(1)} %get-tuple-element.56.refs_2_, bf16[64,2048]{1,0:T(8,128)(2,1)S(1)} %get-tuple-element.60.refs_3_, ...), custom_call_target="tpu_custom_call" | custom-call | flops 3758096384 | bytes 18612224 | tf_op jit(solution)/shard_map/pallas_call | solution.py:58
  453.1 9.8 %shard_map.174 = f32[2048,1792]{1,0:T(8,128)} custom-call(bf16[64,2048]{1,0:T(8,128)(2,1)S(1)} %get-tuple-element.55.refs_0_, bf16[64,2048]{1,0:T(8,128)(2,1)S(1)} %get-tuple-element.59.refs_1_, bf16[64,2048]{1,0:T(8,128)(2,1)S(1)} %get-tuple-element.56.refs_2_, bf16[64,2048]{1,0:T(8,128)(2,1)S(1)} %get-tuple-element.60.refs_3_, ...), custom_call_target="tpu_custom_call" | custom-call | flops 3758096384 | bytes 18612224 | tf_op jit(solution)/shard_map/pallas_call | solution.py:58
  (302 shorter events, 222.7 us)
Async XLA Ops:
  31.0 15.5 %collective-permute-start.3 = (bf16[128,1792]{1,0:T(8,128)(2,1)S(1)}, bf16[128,1792]{1,0:T(8,128)(2,1)S(1)}, u32[]{:S(2)}, u32[]{:S(2)}) collective-permute-start(bf16[128,1792]{1,0:T(8,128)(2,1)S(1)} %convolution_convert_fusion.1), channel_id=1, source_target_pairs={{0,8},{8,16},{16,24},{24,0},{1,9},{9,17},{17,25},{25,1},{2,10},{10... | collective-permute-start | bytes 1376264 | tf_op jit(solution)/shard_map/ppermute | solution.py:161
  33.2 23.3 %collective-permute-start.8 = (bf16[128,1792]{1,0:T(8,128)(2,1)S(1)}, bf16[128,1792]{1,0:T(8,128)(2,1)S(1)}, u32[]{:S(2)}, u32[]{:S(2)}) collective-permute-start(bf16[128,1792]{1,0:T(8,128)(2,1)S(1)} %convolution_convert_fusion), channel_id=1, source_target_pairs={{0,8},{8,16},{16,24},{24,0},{1,9},{9,17},{17,25},{25,1},{2,10},{10... | collective-permute-start | bytes 1376264 | tf_op jit(solution)/shard_map/ppermute | solution.py:161
  49.7 25.4 %collective-permute-start.4 = (bf16[128,1792]{1,0:T(8,128)(2,1)S(1)}, bf16[128,1792]{1,0:T(8,128)(2,1)S(1)}, u32[]{:S(2)}, u32[]{:S(2)}) collective-permute-start(bf16[128,1792]{1,0:T(8,128)(2,1)S(1)} %fusion.7), channel_id=1, source_target_pairs={{0,8},{8,16},{16,24},{24,0},{1,9},{9,17},{17,25},{25,1},{2,10},{10... | collective-permute-start | bytes 1376264 | tf_op jit(solution)/shard_map/ppermute | solution.py:161
  58.4 24.3 %collective-permute-start.9 = (bf16[128,1792]{1,0:T(8,128)(2,1)}, bf16[128,1792]{1,0:T(8,128)(2,1)}, u32[]{:S(2)}, u32[]{:S(2)}) collective-permute-start(bf16[128,1792]{1,0:T(8,128)(2,1)} %fusion.9), channel_id=1, source_target_pairs={{0,8},{8,16},{16,24},{24,0},{1,9},{9,17},{17,25},{25,1},{2,10},{10... | collective-permute-start | bytes 1376264 | tf_op jit(solution)/shard_map/ppermute | solution.py:161
  58.4 14.8 %collective-permute-start.7 = (f32[512]{0:T(512)S(1)}, f32[512]{0:T(512)}, u32[]{:S(2)}, u32[]{:S(2)}) collective-permute-start(f32[512]{0:T(512)S(1)} %add.280), channel_id=1, source_target_pairs={{0,16},{8,24},{16,0},{24,8},{1,17},{9,25},{17,1},{25,9},{2,18},{10... | collective-permute-start | bytes 6152 | tf_op jit(solution)/shard_map/ppermute | solution.py:194
  61.8 25.9 %all-to-all-start = ((bf16[16,8,2048]{2,0,1:T(8,128)(2,1)}), bf16[16,8,2048]{2,0,1:T(8,128)(2,1)S(1)}, u32[]{:S(2)}, u32[]{:S(2)}) async-start(bf16[16,8,2048]{2,0,1:T(8,128)(2,1)} %bitcast.58), calls=%async_computation | async-start | bytes 1048576 | tf_op jit(solution)/shard_map/all_to_all | solution.py:224
  79.3 16.1 %collective-permute-start.5 = (bf16[128,1792]{1,0:T(8,128)(2,1)S(1)}, bf16[128,1792]{1,0:T(8,128)(2,1)}, u32[]{:S(2)}, u32[]{:S(2)}) collective-permute-start(bf16[128,1792]{1,0:T(8,128)(2,1)S(1)} %fusion.6), channel_id=1, source_target_pairs={{0,8},{8,16},{16,24},{24,0},{1,9},{9,17},{17,25},{25,1},{2,10},{10... | collective-permute-start | bytes 1376264 | tf_op jit(solution)/shard_map/ppermute | solution.py:161
  87.0 16.7 %collective-permute-start.10 = (bf16[128,1792]{1,0:T(8,128)(2,1)S(1)}, bf16[128,1792]{1,0:T(8,128)(2,1)}, u32[]{:S(2)}, u32[]{:S(2)}) collective-permute-start(bf16[128,1792]{1,0:T(8,128)(2,1)S(1)} %fusion.8), channel_id=1, source_target_pairs={{0,8},{8,16},{16,24},{24,0},{1,9},{9,17},{17,25},{25,1},{2,10},{10... | collective-permute-start | bytes 1376264 | tf_op jit(solution)/shard_map/ppermute | solution.py:161
  106.2 13.6 %collective-permute-start.11 = (bf16[128,896]{1,0:T(8,128)(2,1)S(1)}, bf16[128,896]{1,0:T(8,128)(2,1)S(1)}, u32[]{:S(2)}, u32[]{:S(2)}) collective-permute-start(bf16[128,896]{1,0:T(8,128)(2,1)S(1)} %get-tuple-element.67.refs_0_), channel_id=1, source_target_pairs={{0,8},{8,16},{16,24},{24,0},{1,9},{9,17},{17,25},{25,1},{2,10},{10... | collective-permute-start | bytes 688136 | tf_op jit(solution)/shard_map/ppermute | solution.py:161
  107.3 11.7 %collective-permute-start.12 = (bf16[128,896]{1,0:T(8,128)(2,1)S(1)}, bf16[128,896]{1,0:T(8,128)(2,1)S(1)}, u32[]{:S(2)}, u32[]{:S(2)}) collective-permute-start(bf16[128,896]{1,0:T(8,128)(2,1)S(1)} %get-tuple-element.68.refs_1_), channel_id=1, source_target_pairs={{0,8},{8,16},{16,24},{24,0},{1,9},{9,17},{17,25},{25,1},{2,10},{10... | collective-permute-start | bytes 688136 | tf_op jit(solution)/shard_map/ppermute | solution.py:161
  119.8 14.3 %collective-permute-start.13 = (bf16[128,896]{1,0:T(8,128)(2,1)S(1)}, bf16[128,896]{1,0:T(8,128)(2,1)S(1)}, u32[]{:S(2)}, u32[]{:S(2)}) collective-permute-start(bf16[128,896]{1,0:T(8,128)(2,1)S(1)} %collective-permute-done.11.refs_2_), channel_id=1, source_target_pairs={{0,8},{8,16},{16,24},{24,0},{1,9},{9,17},{17,25},{25,1},{2,10},{10... | collective-permute-start | bytes 688136 | tf_op jit(solution)/shard_map/ppermute | solution.py:161
  181.5 11.0 %collective-permute-start.23 = (bf16[128,1024]{1,0:T(8,128)(2,1)S(1)}, bf16[128,1024]{1,0:T(8,128)(2,1)S(1)}, u32[]{:S(2)}, u32[]{:S(2)}) collective-permute-start(bf16[128,1024]{1,0:T(8,128)(2,1)S(1)} %convolution_convert_fusion.3), channel_id=1, source_target_pairs={{0,8},{8,16},{16,24},{24,0},{1,9},{9,17},{17,25},{25,1},{2,10},{10... | collective-permute-start | bytes 786440 | tf_op jit(solution)/shard_map/ppermute | solution.py:161
  182.3 15.8 %collective-permute-start.26 = (bf16[128,1024]{1,0:T(8,128)(2,1)S(1)}, bf16[128,1024]{1,0:T(8,128)(2,1)S(1)}, u32[]{:S(2)}, u32[]{:S(2)}) collective-permute-start(bf16[128,1024]{1,0:T(8,128)(2,1)S(1)} %convolution_convert_fusion.2), channel_id=1, source_target_pairs={{0,8},{8,16},{16,24},{24,0},{1,9},{9,17},{17,25},{25,1},{2,10},{10... | collective-permute-start | bytes 786440 | tf_op jit(solution)/shard_map/ppermute | solution.py:161
  193.2 10.8 %collective-permute-start.24 = (bf16[128,1024]{1,0:T(8,128)(2,1)S(1)}, bf16[128,1024]{1,0:T(8,128)(2,1)S(1)}, u32[]{:S(2)}, u32[]{:S(2)}) collective-permute-start(bf16[128,1024]{1,0:T(8,128)(2,1)S(1)} %fusion.29), channel_id=1, source_target_pairs={{0,8},{8,16},{16,24},{24,0},{1,9},{9,17},{17,25},{25,1},{2,10},{10... | collective-permute-start | bytes 786440 | tf_op jit(solution)/shard_map/ppermute | solution.py:161
  198.8 11.1 %collective-permute-start.27 = (bf16[128,1024]{1,0:T(8,128)(2,1)S(1)}, bf16[128,1024]{1,0:T(8,128)(2,1)S(1)}, u32[]{:S(2)}, u32[]{:S(2)}) collective-permute-start(bf16[128,1024]{1,0:T(8,128)(2,1)S(1)} %fusion.31), channel_id=1, source_target_pairs={{0,8},{8,16},{16,24},{24,0},{1,9},{9,17},{17,25},{25,1},{2,10},{10... | collective-permute-start | bytes 786440 | tf_op jit(solution)/shard_map/ppermute | solution.py:161
  204.7 10.7 %collective-permute-start.25 = (bf16[128,1024]{1,0:T(8,128)(2,1)S(1)}, bf16[128,1024]{1,0:T(8,128)(2,1)S(1)}, u32[]{:S(2)}, u32[]{:S(2)}) collective-permute-start(bf16[128,1024]{1,0:T(8,128)(2,1)S(1)} %fusion.28), channel_id=1, source_target_pairs={{0,8},{8,16},{16,24},{24,0},{1,9},{9,17},{17,25},{25,1},{2,10},{10... | collective-permute-start | bytes 786440 | tf_op jit(solution)/shard_map/ppermute | solution.py:161
  221.4 14.9 %collective-permute-start.29 = (bf16[128,1024]{1,0:T(8,128)(2,1)S(1)}, bf16[128,1024]{1,0:T(8,128)(2,1)S(1)}, u32[]{:S(2)}, u32[]{:S(2)}) collective-permute-start(bf16[128,1024]{1,0:T(8,128)(2,1)S(1)} %get-tuple-element.63.refs_8_), channel_id=1, source_target_pairs={{0,8},{8,16},{16,24},{24,0},{1,9},{9,17},{17,25},{25,1},{2,10},{10... | collective-permute-start | bytes 786440 | tf_op jit(solution)/shard_map/ppermute | solution.py:161
  222.9 11.8 %collective-permute-start.30 = (bf16[128,1024]{1,0:T(8,128)(2,1)S(1)}, bf16[128,1024]{1,0:T(8,128)(2,1)S(1)}, u32[]{:S(2)}, u32[]{:S(2)}) collective-permute-start(bf16[128,1024]{1,0:T(8,128)(2,1)S(1)} %get-tuple-element.64.refs_9_), channel_id=1, source_target_pairs={{0,8},{8,16},{16,24},{24,0},{1,9},{9,17},{17,25},{25,1},{2,10},{10... | collective-permute-start | bytes 786440 | tf_op jit(solution)/shard_map/ppermute | solution.py:161
  234.7 10.9 %collective-permute-start.32 = (bf16[128,1024]{1,0:T(8,128)(2,1)S(1)}, bf16[128,1024]{1,0:T(8,128)(2,1)S(1)}, u32[]{:S(2)}, u32[]{:S(2)}) collective-permute-start(bf16[128,1024]{1,0:T(8,128)(2,1)S(1)} %collective-permute-done.30.refs_11_), channel_id=1, source_target_pairs={{0,8},{8,16},{16,24},{24,0},{1,9},{9,17},{17,25},{25,1},{2,10},{10... | collective-permute-start | bytes 786440 | tf_op jit(solution)/shard_map/ppermute | solution.py:161
  236.2 15.0 %collective-permute-start.31 = (bf16[128,1024]{1,0:T(8,128)(2,1)S(1)}, bf16[128,1024]{1,0:T(8,128)(2,1)S(1)}, u32[]{:S(2)}, u32[]{:S(2)}) collective-permute-start(bf16[128,1024]{1,0:T(8,128)(2,1)S(1)} %collective-permute-done.29.refs_10_), channel_id=1, source_target_pairs={{0,8},{8,16},{16,24},{24,0},{1,9},{9,17},{17,25},{25,1},{2,10},{10... | collective-permute-start | bytes 786440 | tf_op jit(solution)/shard_map/ppermute | solution.py:161
  300.5 10.3 %collective-permute-start.41 = (bf16[128,896]{1,0:T(8,128)(2,1)S(1)}, bf16[128,896]{1,0:T(8,128)(2,1)S(1)}, u32[]{:S(2)}, u32[]{:S(2)}) collective-permute-start(bf16[128,896]{1,0:T(8,128)(2,1)S(1)} %convolution_convert_fusion.5), channel_id=1, source_target_pairs={{0,8},{8,16},{16,24},{24,0},{1,9},{9,17},{17,25},{25,1},{2,10},{10... | collective-permute-start | bytes 688136 | tf_op jit(solution)/shard_map/ppermute | solution.py:161
  301.8 13.1 %collective-permute-start.44 = (bf16[128,896]{1,0:T(8,128)(2,1)S(1)}, bf16[128,896]{1,0:T(8,128)(2,1)S(1)}, u32[]{:S(2)}, u32[]{:S(2)}) collective-permute-start(bf16[128,896]{1,0:T(8,128)(2,1)S(1)} %convolution_convert_fusion.4), channel_id=1, source_target_pairs={{0,8},{8,16},{16,24},{24,0},{1,9},{9,17},{17,25},{25,1},{2,10},{10... | collective-permute-start | bytes 688136 | tf_op jit(solution)/shard_map/ppermute | solution.py:161
  316.2 10.4 %collective-permute-start.45 = (bf16[128,896]{1,0:T(8,128)(2,1)S(1)}, bf16[128,896]{1,0:T(8,128)(2,1)S(1)}, u32[]{:S(2)}, u32[]{:S(2)}) collective-permute-start(bf16[128,896]{1,0:T(8,128)(2,1)S(1)} %fusion.35), channel_id=1, source_target_pairs={{0,8},{8,16},{16,24},{24,0},{1,9},{9,17},{17,25},{25,1},{2,10},{10... | collective-permute-start | bytes 688136 | tf_op jit(solution)/shard_map/ppermute | solution.py:161
  339.8 27.4 %collective-permute-start.48 = (bf16[128,1792]{1,0:T(8,128)(2,1)S(1)}, bf16[128,1792]{1,0:T(8,128)(2,1)S(1)}, u32[]{:S(2)}, u32[]{:S(2)}) collective-permute-start(bf16[128,1792]{1,0:T(8,128)(2,1)S(1)} %get-tuple-element.38.refs_8_), channel_id=1, source_target_pairs={{0,8},{8,16},{16,24},{24,0},{1,9},{9,17},{17,25},{25,1},{2,10},{10... | collective-permute-start | bytes 1376264 | tf_op jit(solution)/shard_map/ppermute | solution.py:161
  339.8 30.5 %collective-permute-start.47 = (bf16[128,1792]{1,0:T(8,128)(2,1)S(1)}, bf16[128,1792]{1,0:T(8,128)(2,1)S(1)}, u32[]{:S(2)}, u32[]{:S(2)}) collective-permute-start(bf16[128,1792]{1,0:T(8,128)(2,1)S(1)} %get-tuple-element.37.refs_8_), channel_id=1, source_target_pairs={{0,8},{8,16},{16,24},{24,0},{1,9},{9,17},{17,25},{25,1},{2,10},{10... | collective-permute-start | bytes 1376264 | tf_op jit(solution)/shard_map/ppermute | solution.py:161
  367.2 15.3 %collective-permute-start.50 = (bf16[128,1792]{1,0:T(8,128)(2,1)S(1)}, bf16[128,1792]{1,0:T(8,128)(2,1)S(1)}, u32[]{:S(2)}, u32[]{:S(2)}) collective-permute-start(bf16[128,1792]{1,0:T(8,128)(2,1)S(1)} %broadcast_select_fusion.1), channel_id=1, source_target_pairs={{0,8},{8,16},{16,24},{24,0},{1,9},{9,17},{17,25},{25,1},{2,10},{10... | collective-permute-start | bytes 1376264 | tf_op jit(solution)/shard_map/ppermute | solution.py:161
  370.3 22.0 %collective-permute-start.49 = (bf16[128,1792]{1,0:T(8,128)(2,1)S(1)}, bf16[128,1792]{1,0:T(8,128)(2,1)S(1)}, u32[]{:S(2)}, u32[]{:S(2)}) collective-permute-start(bf16[128,1792]{1,0:T(8,128)(2,1)S(1)} %collective-permute-done.47.refs_9_), channel_id=1, source_target_pairs={{0,8},{8,16},{16,24},{24,0},{1,9},{9,17},{17,25},{25,1},{2,10},{10... | collective-permute-start | bytes 1376264 | tf_op jit(solution)/shard_map/ppermute | solution.py:161
  382.5 19.6 %collective-permute-start.52 = (bf16[128,1792]{1,0:T(8,128)(2,1)S(1)}, bf16[128,1792]{1,0:T(8,128)(2,1)S(1)}, u32[]{:S(2)}, u32[]{:S(2)}) collective-permute-start(bf16[128,1792]{1,0:T(8,128)(2,1)S(1)} %collective-permute-done.50.refs_10_), channel_id=1, source_target_pairs={{0,8},{8,16},{16,24},{24,0},{1,9},{9,17},{17,25},{25,1},{2,10},{10... | collective-permute-start | bytes 1376264 | tf_op jit(solution)/shard_map/ppermute | solution.py:161
  392.4 14.7 %collective-permute-start.51 = (bf16[128,1792]{1,0:T(8,128)(2,1)S(1)}, bf16[128,1792]{1,0:T(8,128)(2,1)S(1)}, u32[]{:S(2)}, u32[]{:S(2)}) collective-permute-start(bf16[128,1792]{1,0:T(8,128)(2,1)S(1)} %collective-permute-done.49.refs_10_), channel_id=1, source_target_pairs={{0,8},{8,16},{16,24},{24,0},{1,9},{9,17},{17,25},{25,1},{2,10},{10... | collective-permute-start | bytes 1376264 | tf_op jit(solution)/shard_map/ppermute | solution.py:161
  424.2 12.1 %collective-permute-start.55 = (bf16[64,2048]{1,0:T(8,128)(2,1)}, bf16[64,2048]{1,0:T(8,128)(2,1)}, u32[]{:S(2)}, u32[]{:S(2)}) collective-permute-start(bf16[64,2048]{1,0:T(8,128)(2,1)} %slice.428), channel_id=1, source_target_pairs={{0,2},{1,5},{2,0},{3,7},{4,6},{5,1},{6,4},{7,3},{8,10},{9,13},{10,... | collective-permute-start | bytes 786440 | tf_op jit(solution)/shard_map/ppermute | solution.py:123
  437.8 12.9 %collective-permute-start.59 = (f32[66]{0:T(128)S(1)}, f32[66]{0:T(128)S(1)}, u32[]{:S(2)}, u32[]{:S(2)}) collective-permute-start(f32[66]{0:T(128)S(1)} %pad_maximum_fusion.46), channel_id=1, source_target_pairs={{0,8},{8,0},{16,24},{24,16},{1,9},{9,1},{17,25},{25,17},{2,10},{10... | collective-permute-start | bytes 800 | tf_op jit(solution)/shard_map/ppermute | solution.py:194
  450.8 12.8 %collective-permute-start.60 = (f32[66]{0:T(128)S(1)}, f32[66]{0:T(128)S(1)}, u32[]{:S(2)}, u32[]{:S(2)}) collective-permute-start(f32[66]{0:T(128)S(1)} %fusion.164), channel_id=1, source_target_pairs={{0,16},{8,24},{16,0},{24,8},{1,17},{9,25},{17,1},{25,9},{2,18},{10... | collective-permute-start | bytes 800 | tf_op jit(solution)/shard_map/ppermute | solution.py:194
  (66 other events, 591.5 us)
where the time goes:
time: 478 us; the launch traced here: 469 us
  waiting for transfers between devices  257 us (54%)
  matrix products  78.6 us (16%)
  starting transfers between devices  51.3 us (11%)
  Pallas kernels  37.9 us (8%)
  between operations  17 us (4%)
  local copies, waits for them, and re-layouts  16.7 us (3%)
  other arithmetic  10.4 us (2%)
    ppermute x36, waiting for transfers between devices, shift(): return lax.ppermute(value, 'row', self.ring)  161 us
    dot_general x24, matrix products, mm_t(): lax.dot_general(left, right, (((1,), (1,)), ((), ())), preferred_element_...  42.2 us
    pallas_call x4, Pallas kernels, weight_grad(): pl.pallas_call(functools.partial(grad_kernel, places, tile), grid=(m // t...  37.9 us
    ppermute x6, waiting for transfers between devices, gather(): own = jnp.concatenate([own, lax.ppermute(own, PLANE, perm)], axis=0)  36.7 us
    dot_general x24, matrix products, mm(): return jnp.dot(left, right, preferred_element_type=F32)  36.4 us
    ppermute x6, waiting for transfers between devices, scatter(): got = lax.ppermute(acc[half:].astype(full.dtype), PLANE, perm)  32.9 us
    ppermute x36, starting transfers between devices, shift(): return lax.ppermute(value, 'row', self.ring)  19.6 us
    ppermute x6, starting transfers between devices, gather(): own = jnp.concatenate([own, lax.ppermute(own, PLANE, perm)], axis=0)  11.3 us
  transfers between devices with their start and end apart: 62, of which 50 were waited for; matrix products, arithmetic and copies ran while one was open for 16% of the time, Pallas kernels for 8%

commit v1 on v0

--- a/solution.py
+++ b/solution.py
@@ -21,8 +21,8 @@
 
 
 def grad_kernel(places, tile, *refs):
-    out_ref, left, right, sems = refs[-4:]
-    pieces = refs[:-4]
+    pieces = refs[: len(places)]
+    out_ref, _, left, right, sems = refs[-5:]
 
     @pl.when(pl.program_id(0) == 0)
     def load():
@@ -41,7 +41,7 @@
     )
 
 
-def weight_grad(lefts, rights):
+def weight_grad(lefts, rights, through, *earlier):
     places, pieces, shapes = [], [], []
     for side, grid in enumerate((lefts, rights)):
         row = 0
@@ -55,12 +55,17 @@
         shapes.append((row, column))
     (depth, m), (_, n) = shapes
     tile = 256 if m % 256 == 0 else 128
+    operands = pieces + list(earlier) + [through]
     return pl.pallas_call(
         functools.partial(grad_kernel, places, tile),
         grid=(m // tile,),
-        in_specs=[pl.BlockSpec(memory_space=pl.ANY)] * len(pieces),
-        out_specs=pl.BlockSpec((tile, n), lambda i: (i, 0)),
-        out_shape=jax.ShapeDtypeStruct((m, n), F32),
+        in_specs=[pl.BlockSpec(memory_space=pl.ANY)] * len(operands),
+        out_specs=[pl.BlockSpec((tile, n), lambda i: (i, 0)), pl.BlockSpec(memory_space=pl.ANY)],
+        out_shape=[
+            jax.ShapeDtypeStruct((m, n), F32),
+            jax.ShapeDtypeStruct(through.shape, through.dtype),
+        ],
+        input_output_aliases={len(operands) - 1: 1},
         scratch_shapes=[
             pltpu.VMEM((depth, m), BF16),
             pltpu.VMEM((depth, n), BF16),
@@ -72,7 +77,7 @@
             bytes_accessed=2 * depth * (m + n) + 4 * m * n,
             transcendentals=0,
         ),
-    )(*pieces)
+    )(*operands)
 
 
 def reverse_bits(value, width):
@@ -110,7 +115,7 @@
             own = jnp.concatenate([own, lax.ppermute(own, PLANE, perm)], axis=0)
         return own, lax.ppermute(own, PLANE, self.swap)
 
-    def scatter(self, full):
+    def scatter(self, full, beside=()):
         b = full.shape[0] // self.size
         block = lambda i: full[i * b : (i + 1) * b]
         half = self.size // 2
@@ -118,10 +123,13 @@
         send = jnp.concatenate([block(2 * self.rev[k] + 1) for k in range(half)], axis=0)
         got = lax.ppermute(send, PLANE, self.swap)
         acc = mine.astype(F32) + got.astype(F32)
-        for perm in reversed(self.perms):
+        for i, perm in enumerate(reversed(self.perms)):
             half = acc.shape[0] // 2
-            got = lax.ppermute(acc[half:].astype(full.dtype), PLANE, perm)
-            acc = acc[:half] + got.astype(F32)
+            kept, sent = acc[:half], acc[half:].astype(full.dtype)
+            got = lax.ppermute(sent, PLANE, perm)
+            if i < len(beside):
+                kept = beside[i](kept, sent)
+            acc = kept + got.astype(F32)
         return acc
 
     def total(self, value):
@@ -160,15 +168,18 @@
     def shift(self, value):
         return lax.ppermute(value, "row", self.ring)
 
-    def reduce(self, parts, products):
+    def reduce(self, parts, products, beside=None):
         got, first = None, None
         for back in range(1, self.size + 1):
             rows = jnp.concatenate(parts[back % self.size], axis=0)
             sums = [product(rows) for product in products]
+            if back == 2 and beside is not None:
+                sums[-1] = beside(sums[-1], sent[-1])
             if got is not None:
                 sums = [s + g.astype(F32) for s, g in zip(sums, got)]
             if back < self.size:
-                got = [self.shift(s.astype(BF16)) for s in sums]
+                sent = [s.astype(BF16) for s in sums]
+                got = [self.shift(s) for s in sent]
                 first = got[0] if first is None else first
         return sums, first
 
@@ -188,6 +199,14 @@
             out = self.place(out, block, back)
         return out
 
+    def sum_direct(self, value):
+        total = value
+        for step in range(1, self.size):
+            total = total + lax.ppermute(
+                value, "row", [(r, r ^ step) for r in range(self.size)]
+            )
+        return total
+
     def total(self, value):
         step = 1
         while step < self.size:
@@ -217,7 +236,7 @@
         scaled = rows.parts(own, other)
         (gate, up), moved = rows.reduce(scaled, [lambda a: mm(a, gate_w), lambda a: mm(a, up_w)])
         squares = [jnp.sum(jnp.square(p.astype(F32) / gain[None, :]), axis=1) for p in (own, other)]
-        squares = rows.total(after(jnp.concatenate(squares), moved))
+        squares = rows.sum_direct(after(jnp.concatenate(squares), moved))
         inv_all = lax.rsqrt(squares / features + 1e-05)
         inv = jnp.concatenate(rows.parts(*jnp.split(inv_all, 2))[0])[:, None]
 
@@ -253,28 +272,39 @@
         resid_grad = plane.scatter(back).astype(BF16)
         resid_grads = rows.parts(*plane.gather(resid_grad))
 
+        found = {}
+
+        def grad(name, lefts, rights, through, *earlier):
+            found[name], through = weight_grad(lefts, rights, through, *earlier)
+            return through
+
         hid_grad, _ = rows.reduce(
-            resid_grads, [lambda a, lo=lo, hi=hi: mm_t(a, down_w[lo:hi]) for lo, hi in cuts]
+            resid_grads,
+            [lambda a, lo=lo, hi=hi: mm_t(a, down_w[lo:hi]) for lo, hi in cuts],
+            lambda own, sent: grad("down", hiddens, lines(resid_grads), own, sent),
         )
         hid_grad = jnp.concatenate(hid_grad, axis=1)
         gate_grad = hid_grad * up * (sigma * (1.0 + gate * (1.0 - sigma)))
         up_grad = hid_grad * activated
         blocks = [(gate_grad * inv).astype(BF16), (up_grad * inv).astype(BF16)]
 
-        def held(parts):
-            return [[after(p, blocks[1]) for p in parts[0]]] + parts[1:]
-
-        grad_proj = weight_grad(lines(held(residuals)), pred_grads)
-        grad_down = weight_grad(hiddens, lines(held(resid_grads)))
+        last = grad("proj", lines(residuals), pred_grads, keep, blocks[1])
         grads, made, back = rows.gather(
             blocks,
             lambda b: (mm_t(b[0], gate_w) + mm_t(b[1], up_w)).astype(BF16),
-            grad_proj[:1, :1] + grad_down[:1, :1],
-        )
-        normed_grad = plane.scatter(back)
+            last,
+        )
+        gates, ups = [g[:1] for g in grads], [g[1:] for g in grads]
+        normed_grad = plane.scatter(
+            back,
+            (
+                lambda kept, sent: grad("gate", lines(scaled), gates, kept, sent),
+                lambda kept, sent: grad("up", lines(scaled), ups, kept, sent),
+            ),
+        )
         inner = jnp.sum(normed_grad * gain[None, :] * x.astype(F32), axis=1)
         loss_sum = 0.5 * sum(jnp.sum(m * e) for m, e in zip(masked, error))
-        loss_parts = jnp.stack([loss_sum, jnp.sum(keep)])
+        loss_parts = jnp.stack([loss_sum, jnp.sum(last)])
         gain_sum = sum(
             jnp.sum(m.astype(F32) * jnp.concatenate(p, axis=0).astype(F32), axis=0)
             for m, p in zip(made, scaled)
@@ -285,16 +315,21 @@
         inner = sums[:-2]
         loss_value = sums[-2] / (sums[-1] / n_plane)
 
-        grad_gate = weight_grad(lines(scaled), [g[:1] for g in grads])
-        grad_up = weight_grad(lines(scaled), [g[1:] for g in grads])
-
         inv_own = inv_all[:block]
         grad_input = (
             resid_grad.astype(F32)
             + gain[None, :] * normed_grad
             - x.astype(F32) * (inv_own * inv_own * inner / features)[:, None]
         )
-        return (loss_value, grad_gain, grad_gate, grad_up, grad_down, grad_proj, grad_input)
+        return (
+            loss_value,
+            grad_gain,
+            found["gate"],
+            found["up"],
+            found["down"],
+            found["proj"],
+            grad_input,
+        )
 
     return body
 

time: 478 us -> 474 us (level)
  matrix products: 78.6 us -> 104 us
  waiting for transfers between devices: 257 us -> 237 us
  starting transfers between devices: 51.3 us -> 45 us
    dot_general x24, matrix products: 42.2 us -> 66 us  [mm_t(): lax.dot_general(left, right, (((1,), (1,)), ((), ())), preferred_element_...]
    ppermute x36, waiting for transfers between devices: 161 us -> 148 us  [shift(): return lax.ppermute(value, 'row', self.ring)]
    ppermute x6 -> x9, waiting for transfers between devices: 32.9 us -> 25.8 us  [the longest x6 25.8 us: scatter(): got = lax.ppermute(sent, PLANE, perm)]
    ppermute x4 -> x2, starting transfers between devices: 4.9 us -> 0.01 us  [total(): lax.ppermute(value, 'row', [(r, r ^ step) for r in range(self.size)])]
    ppermute x6 -> x9, starting transfers between devices: 9.21 us -> 12.9 us  [the longest x6 8.46 us: scatter(): got = lax.ppermute(sent, PLANE, perm)]
  transfers between devices with their start and end apart: 62 -> 63, of which waited for: 50 -> 49; matrix products, arithmetic and copies ran while one was open for 16% -> 20% of each run, Pallas kernels for 8% -> 8%
where the time goes in v1:
time: 474 us; the launch traced here: 465 us
  waiting for transfers between devices  237 us (50%)
  matrix products  104 us (22%)
  starting transfers between devices  45 us (9%)
  Pallas kernels  37.9 us (8%)
  local copies, waits for them, and re-layouts  15.7 us (3%)
  between operations  14.4 us (3%)
  other arithmetic  11.1 us (2%)
    ppermute x36, waiting for transfers between devices, shift(): return lax.ppermute(value, 'row', self.ring)  148 us
    dot_general x24, matrix products, mm_t(): lax.dot_general(left, right, (((1,), (1,)), ((), ())), preferred_element_...  66 us
    dot_general x24, matrix products, mm(): return jnp.dot(left, right, preferred_element_type=F32)  38 us
    pallas_call x4, Pallas kernels, weight_grad(): pl.pallas_call(functools.partial(grad_kernel, places, tile), grid=(m // t...  37.9 us
    ppermute x6, waiting for transfers between devices, gather(): own = jnp.concatenate([own, lax.ppermute(own, PLANE, perm)], axis=0)  37.3 us
    ppermute x6, waiting for transfers between devices, scatter(): got = lax.ppermute(sent, PLANE, perm)  25.8 us
    ppermute x36, starting transfers between devices, shift(): return lax.ppermute(value, 'row', self.ring)  15 us
    ppermute x6, starting transfers between devices, gather(): own = jnp.concatenate([own, lax.ppermute(own, PLANE, perm)], axis=0)  10.7 us
  transfers between devices with their start and end apart: 63, of which 49 were waited for; matrix products, arithmetic and copies ran while one was open for 20% of the time, Pallas kernels for 8%

profile of v1, /device:TPU:0, one launch (start us, length us, event | category | flops | bytes accessed | tf_op | source)
XLA Modules:
  0.0 464.8 jit_solution(278080752527125316)
XLA Ops:
  4.7 4.4 collective-permute-done
  11.2 7.2 %collective-permute-done.1 = bf16[128,2048]{1,0:T(8,128)(2,1)S(1)} collective-permute-done((bf16[128,2048]{1,0:T(8,128)(2,1)S(1)}, bf16[128,2048]{1,0:T(8,128)(2,1)S(1)}, u32[]{:S(2)}, u32[]{:S(2)}) %collective-permute-start.1) | collective-permute-done | bytes 524320 | tf_op jit(solution)/shard_map/ppermute | solution.py:115
  24.7 4.4 convolution_convert_fusion.1
  35.4 9.2 %collective-permute-done.3 = bf16[128,1792]{1,0:T(8,128)(2,1)S(1)} collective-permute-done((bf16[128,1792]{1,0:T(8,128)(2,1)S(1)}, bf16[128,1792]{1,0:T(8,128)(2,1)S(1)}, u32[]{:S(2)}, u32[]{:S(2)}) %collective-permute-start.3) | collective-permute-done | bytes 458784 | tf_op jit(solution)/shard_map/ppermute | solution.py:169
  66.2 5.0 %fusion.6 = bf16[128,1792]{1,0:T(8,128)(2,1)} fusion(bf16[2048,1792]{1,0:T(8,128)(2,1)} %param.14, bf16[128,1792]{1,0:T(8,128)(2,1)} %collective-permute-done.4, bf16[64,2048]{1,0:T(8,128)(2,1)S(1)} %get-tuple-element.74.refs_7_, bf16[64,2048]{1,0:T(8,128)(2,1)S(1)} %get-tuple-element.70.refs_6_), kind=kOutput, calls=%fused_computation.24 | convolution fusion | flops 941260800 | bytes 8781824 | tf_op jit(solution)/shard_map/dot_general | solution.py:16
  77.2 4.4 fusion.8
  81.7 5.4 %collective-permute-done.5 = bf16[128,1792]{1,0:T(8,128)(2,1)} collective-permute-done((bf16[128,1792]{1,0:T(8,128)(2,1)}, bf16[128,1792]{1,0:T(8,128)(2,1)}, u32[]{:S(2)}, u32[]{:S(2)}) %collective-permute-start.5) | collective-permute-done | bytes 458784 | tf_op jit(solution)/shard_map/ppermute | solution.py:169
  89.5 7.1 %collective-permute-done.11 = bf16[128,1792]{1,0:T(8,128)(2,1)S(1)} collective-permute-done((bf16[128,1792]{1,0:T(8,128)(2,1)S(1)}, bf16[128,1792]{1,0:T(8,128)(2,1)S(1)}, u32[]{:S(2)}, u32[]{:S(2)}) %collective-permute-start.11) | collective-permute-done | bytes 458784 | tf_op jit(solution)/shard_map/ppermute | solution.py:169
  100.9 11.4 %collective-permute-done.13.refs_3_ = bf16[128,896]{1,0:T(8,128)(2,1)S(1)} collective-permute-done((bf16[128,896]{1,0:T(8,128)(2,1)S(1)}, bf16[128,896]{1,0:T(8,128)(2,1)S(1)}, u32[]{:S(2)}, u32[]{:S(2)}) %collective-permute-start.13) | collective-permute-done | bytes 229408 | tf_op jit(solution)/shard_map/ppermute | solution.py:169
  113.8 8.8 %collective-permute-done.15.refs_5_ = bf16[128,896]{1,0:T(8,128)(2,1)S(1)} collective-permute-done((bf16[128,896]{1,0:T(8,128)(2,1)S(1)}, bf16[128,896]{1,0:T(8,128)(2,1)S(1)}, u32[]{:S(2)}, u32[]{:S(2)}) %collective-permute-start.15) | collective-permute-done | bytes 229408 | tf_op jit(solution)/shard_map/ppermute | solution.py:169
  128.2 4.6 collective-permute-done.17.refs_7_
  140.9 7.8 %collective-permute-done.19 = bf16[128,2048]{1,0:T(8,128)(2,1)S(1)} collective-permute-done((bf16[128,2048]{1,0:T(8,128)(2,1)S(1)}, bf16[128,2048]{1,0:T(8,128)(2,1)S(1)}, u32[]{:S(2)}, u32[]{:S(2)}) %collective-permute-start.19) | collective-permute-done | bytes 524320 | tf_op jit(solution)/shard_map/ppermute | solution.py:129
  150.3 5.0 %collective-permute-done.20 = bf16[64,2048]{1,0:T(8,128)(2,1)S(1)} collective-permute-done((bf16[64,2048]{1,0:T(8,128)(2,1)S(1)}, bf16[64,2048]{1,0:T(8,128)(2,1)S(1)}, u32[]{:S(2)}, u32[]{:S(2)}) %collective-permute-start.20) | collective-permute-done | bytes 262176 | tf_op jit(solution)/shard_map/ppermute | solution.py:129
  156.9 5.0 %collective-permute-done.21 = bf16[64,2048]{1,0:T(8,128)(2,1)S(1)} collective-permute-done((bf16[64,2048]{1,0:T(8,128)(2,1)S(1)}, bf16[64,2048]{1,0:T(8,128)(2,1)S(1)}, u32[]{:S(2)}, u32[]{:S(2)}) %collective-permute-start.21) | collective-permute-done | bytes 262176 | tf_op jit(solution)/shard_map/ppermute | solution.py:115
  163.4 7.8 %collective-permute-done.22 = bf16[128,2048]{1,0:T(8,128)(2,1)S(1)} collective-permute-done((bf16[128,2048]{1,0:T(8,128)(2,1)S(1)}, bf16[128,2048]{1,0:T(8,128)(2,1)S(1)}, u32[]{:S(2)}, u32[]{:S(2)}) %collective-permute-start.22) | collective-permute-done | bytes 524320 | tf_op jit(solution)/shard_map/ppermute | solution.py:115
  175.7 10.1 %collective-permute-done.24 = bf16[128,1024]{1,0:T(8,128)(2,1)S(1)} collective-permute-done((bf16[128,1024]{1,0:T(8,128)(2,1)S(1)}, bf16[128,1024]{1,0:T(8,128)(2,1)S(1)}, u32[]{:S(2)}, u32[]{:S(2)}) %collective-permute-start.24) | collective-permute-done | bytes 262176 | tf_op jit(solution)/shard_map/ppermute | solution.py:169
  186.7 4.8 %collective-permute-done.27 = bf16[128,1024]{1,0:T(8,128)(2,1)S(1)} collective-permute-done((bf16[128,1024]{1,0:T(8,128)(2,1)S(1)}, bf16[128,1024]{1,0:T(8,128)(2,1)S(1)}, u32[]{:S(2)}, u32[]{:S(2)}) %collective-permute-start.27) | collective-permute-done | bytes 262176 | tf_op jit(solution)/shard_map/ppermute | solution.py:169
  192.3 5.1 %collective-permute-done.25 = bf16[128,1024]{1,0:T(8,128)(2,1)S(1)} collective-permute-done((bf16[128,1024]{1,0:T(8,128)(2,1)S(1)}, bf16[128,1024]{1,0:T(8,128)(2,1)S(1)}, u32[]{:S(2)}, u32[]{:S(2)}) %collective-permute-start.25) | collective-permute-done | bytes 262176 | tf_op jit(solution)/shard_map/ppermute | solution.py:169
  198.2 5.1 %collective-permute-done.28 = bf16[128,1024]{1,0:T(8,128)(2,1)S(1)} collective-permute-done((bf16[128,1024]{1,0:T(8,128)(2,1)S(1)}, bf16[128,1024]{1,0:T(8,128)(2,1)S(1)}, u32[]{:S(2)}, u32[]{:S(2)}) %collective-permute-start.28) | collective-permute-done | bytes 262176 | tf_op jit(solution)/shard_map/ppermute | solution.py:169
  220.4 9.3 %collective-permute-done.31.refs_11_ = bf16[128,1024]{1,0:T(8,128)(2,1)S(1)} collective-permute-done((bf16[128,1024]{1,0:T(8,128)(2,1)S(1)}, bf16[128,1024]{1,0:T(8,128)(2,1)S(1)}, u32[]{:S(2)}, u32[]{:S(2)}) %collective-permute-start.31) | collective-permute-done | bytes 262176 | tf_op jit(solution)/shard_map/ppermute | solution.py:169
  263.8 7.8 %collective-permute-done.37 = bf16[128,2048]{1,0:T(8,128)(2,1)S(1)} collective-permute-done((bf16[128,2048]{1,0:T(8,128)(2,1)S(1)}, bf16[128,2048]{1,0:T(8,128)(2,1)S(1)}, u32[]{:S(2)}, u32[]{:S(2)}) %collective-permute-start.37) | collective-permute-done | bytes 524320 | tf_op jit(solution)/shard_map/ppermute | solution.py:129
  273.2 5.1 %collective-permute-done.38 = bf16[64,2048]{1,0:T(8,128)(2,1)S(1)} collective-permute-done((bf16[64,2048]{1,0:T(8,128)(2,1)S(1)}, bf16[64,2048]{1,0:T(8,128)(2,1)S(1)}, u32[]{:S(2)}, u32[]{:S(2)}) %collective-permute-start.38) | collective-permute-done | bytes 262176 | tf_op jit(solution)/shard_map/ppermute | solution.py:129
  279.7 5.1 %collective-permute-done.39 = bf16[64,2048]{1,0:T(8,128)(2,1)S(1)} collective-permute-done((bf16[64,2048]{1,0:T(8,128)(2,1)S(1)}, bf16[64,2048]{1,0:T(8,128)(2,1)S(1)}, u32[]{:S(2)}, u32[]{:S(2)}) %collective-permute-start.39) | collective-permute-done | bytes 262176 | tf_op jit(solution)/shard_map/ppermute | solution.py:115
  286.2 7.8 %collective-permute-done.40 = bf16[128,2048]{1,0:T(8,128)(2,1)S(1)} collective-permute-done((bf16[128,2048]{1,0:T(8,128)(2,1)S(1)}, bf16[128,2048]{1,0:T(8,128)(2,1)S(1)}, u32[]{:S(2)}, u32[]{:S(2)}) %collective-permute-start.40) | collective-permute-done | bytes 524320 | tf_op jit(solution)/shard_map/ppermute | solution.py:115
  304.7 8.8 %shard_map.171 = (f32[1792,2048]{1,0:T(8,128)}, f32[128,896]{1,0:T(8,128)S(1)}) custom-call(bf16[128,896]{1,0:T(8,128)(2,1)S(1)} %get-tuple-element.82.refs_0_, bf16[128,896]{1,0:T(8,128)(2,1)S(1)} %get-tuple-element.81.refs_1_, bf16[128,896]{1,0:T(8,128)(2,1)S(1)} %collective-permute-done.12.refs_2_, ...), custom_call_target="tpu_custom_call", output_to_operand_aliasing={{1}: (17, {})} | custom-call | flops 3758096384 | bytes 18612224 | tf_op jit(solution)/shard_map/pallas_call | solution.py:59
  346.4 9.5 %shard_map.172 = (f32[2048,2048]{1,0:T(8,128)}, f32[128]{0:T(128)S(1)}) custom-call(bf16[64,2048]{1,0:T(8,128)(2,1)S(1)} %get-tuple-element.61.refs_0_, bf16[64,2048]{1,0:T(8,128)(2,1)S(1)} %get-tuple-element.65.refs_1_, bf16[64,2048]{1,0:T(8,128)(2,1)S(1)} %get-tuple-element.62.refs_2_, ...), custom_call_target="tpu_custom_call", output_to_operand_aliasing={{1}: (17, {})} | custom-call | flops 4294967296 | bytes 20971520 | tf_op jit(solution)/shard_map/pallas_call | solution.py:59
  356.3 6.0 %collective-permute-done.48.refs_9_ = bf16[128,1792]{1,0:T(8,128)(2,1)S(1)} collective-permute-done((bf16[128,1792]{1,0:T(8,128)(2,1)S(1)}, bf16[128,1792]{1,0:T(8,128)(2,1)S(1)}, u32[]{:S(2)}, u32[]{:S(2)}) %collective-permute-start.48) | collective-permute-done | bytes 458784 | tf_op jit(solution)/shard_map/ppermute | solution.py:169
  367.5 10.1 %collective-permute-done.49.refs_10_ = bf16[128,1792]{1,0:T(8,128)(2,1)S(1)} collective-permute-done((bf16[128,1792]{1,0:T(8,128)(2,1)S(1)}, bf16[128,1792]{1,0:T(8,128)(2,1)S(1)}, u32[]{:S(2)}, u32[]{:S(2)}) %collective-permute-start.49) | collective-permute-done | bytes 458784 | tf_op jit(solution)/shard_map/ppermute | solution.py:169
  380.1 7.4 %collective-permute-done.52.refs_10_ = bf16[128,1792]{1,0:T(8,128)(2,1)S(1)} collective-permute-done((bf16[128,1792]{1,0:T(8,128)(2,1)S(1)}, bf16[128,1792]{1,0:T(8,128)(2,1)S(1)}, u32[]{:S(2)}, u32[]{:S(2)}) %collective-permute-start.52) | collective-permute-done | bytes 458784 | tf_op jit(solution)/shard_map/ppermute | solution.py:169
  390.3 7.0 %collective-permute-done.50.refs_11_ = bf16[128,1792]{1,0:T(8,128)(2,1)S(1)} collective-permute-done((bf16[128,1792]{1,0:T(8,128)(2,1)S(1)}, bf16[128,1792]{1,0:T(8,128)(2,1)S(1)}, u32[]{:S(2)}, u32[]{:S(2)}) %collective-permute-start.50) | collective-permute-done | bytes 458784 | tf_op jit(solution)/shard_map/ppermute | solution.py:169
  429.4 9.8 %shard_map.173 = (f32[2048,1792]{1,0:T(8,128)}, f32[128,2048]{1,0:T(8,128)S(1)}) custom-call(bf16[64,2048]{1,0:T(8,128)(2,1)S(1)} %get-tuple-element.69.refs_0_, bf16[64,2048]{1,0:T(8,128)(2,1)S(1)} %get-tuple-element.73.refs_1_, bf16[64,2048]{1,0:T(8,128)(2,1)S(1)} %get-tuple-element.72.refs_2_, ...), custom_call_target="tpu_custom_call", output_to_operand_aliasing={{1}: (13, {})} | custom-call | flops 3758096384 | bytes 18612224 | tf_op jit(solution)/shard_map/pallas_call | solution.py:59
  442.1 9.8 %shard_map.174 = (f32[2048,1792]{1,0:T(8,128)}, f32[64,2048]{1,0:T(8,128)S(1)}) custom-call(bf16[64,2048]{1,0:T(8,128)(2,1)S(1)} %get-tuple-element.69.refs_0_, bf16[64,2048]{1,0:T(8,128)(2,1)S(1)} %get-tuple-element.73.refs_1_, bf16[64,2048]{1,0:T(8,128)(2,1)S(1)} %get-tuple-element.72.refs_2_, ...), custom_call_target="tpu_custom_call", output_to_operand_aliasing={{1}: (13, {})} | custom-call | flops 3758096384 | bytes 18612224 | tf_op jit(solution)/shard_map/pallas_call | solution.py:59
  (314 shorter events, 224.2 us)
Async XLA Ops:
  29.1 15.5 %collective-permute-start.3 = (bf16[128,1792]{1,0:T(8,128)(2,1)S(1)}, bf16[128,1792]{1,0:T(8,128)(2,1)S(1)}, u32[]{:S(2)}, u32[]{:S(2)}) collective-permute-start(bf16[128,1792]{1,0:T(8,128)(2,1)S(1)} %convolution_convert_fusion.1), channel_id=1, source_target_pairs={{0,8},{8,16},{16,24},{24,0},{1,9},{9,17},{17,25},{25,1},{2,10},{10... | collective-permute-start | bytes 1376264 | tf_op jit(solution)/shard_map/ppermute | solution.py:169
  33.2 24.5 %collective-permute-start.9 = (bf16[128,1792]{1,0:T(8,128)(2,1)}, bf16[128,1792]{1,0:T(8,128)(2,1)}, u32[]{:S(2)}, u32[]{:S(2)}) collective-permute-start(bf16[128,1792]{1,0:T(8,128)(2,1)} %convolution_convert_fusion), channel_id=1, source_target_pairs={{0,8},{8,16},{16,24},{24,0},{1,9},{9,17},{17,25},{25,1},{2,10},{10... | collective-permute-start | bytes 1376264 | tf_op jit(solution)/shard_map/ppermute | solution.py:169
  46.5 16.4 %collective-permute-start.8 = (f32[512]{0:T(512)S(1)}, f32[512]{0:T(512)S(1)}, u32[]{:S(2)}, u32[]{:S(2)}) collective-permute-start(f32[512]{0:T(512)S(1)} %maximum_select_fusion.1), channel_id=1, source_target_pairs={{0,24},{8,16},{16,8},{24,0},{1,25},{9,17},{17,9},{25,1},{2,26},{10... | collective-permute-start | bytes 6152 | tf_op jit(solution)/shard_map/ppermute | solution.py:205
  48.5 14.4 %collective-permute-start.7 = (f32[512]{0:T(512)S(1)}, f32[512]{0:T(512)}, u32[]{:S(2)}, u32[]{:S(2)}) collective-permute-start(f32[512]{0:T(512)S(1)} %maximum_select_fusion.1), channel_id=1, source_target_pairs={{0,16},{8,24},{16,0},{24,8},{1,17},{9,25},{17,1},{25,9},{2,18},{10... | collective-permute-start | bytes 6152 | tf_op jit(solution)/shard_map/ppermute | solution.py:205
  48.5 15.0 %collective-permute-start.6 = (f32[512]{0:T(512)S(1)}, f32[512]{0:T(512)}, u32[]{:S(2)}, u32[]{:S(2)}) collective-permute-start(f32[512]{0:T(512)S(1)} %maximum_select_fusion.1), channel_id=1, source_target_pairs={{0,8},{8,0},{16,24},{24,16},{1,9},{9,1},{17,25},{25,17},{2,10},{10... | collective-permute-start | bytes 6152 | tf_op jit(solution)/shard_map/ppermute | solution.py:205
  52.9 13.3 %collective-permute-start.4 = (bf16[128,1792]{1,0:T(8,128)(2,1)}, bf16[128,1792]{1,0:T(8,128)(2,1)}, u32[]{:S(2)}, u32[]{:S(2)}) collective-permute-start(bf16[128,1792]{1,0:T(8,128)(2,1)} %fusion.7), channel_id=1, source_target_pairs={{0,8},{8,16},{16,24},{24,0},{1,9},{9,17},{17,25},{25,1},{2,10},{10... | collective-permute-start | bytes 1376264 | tf_op jit(solution)/shard_map/ppermute | solution.py:169
  53.8 18.1 %all-to-all-start = ((bf16[16,8,2048]{2,0,1:T(8,128)(2,1)}), bf16[16,8,2048]{2,0,1:T(8,128)(2,1)S(1)}, u32[]{:S(2)}, u32[]{:S(2)}) async-start(bf16[16,8,2048]{2,0,1:T(8,128)(2,1)} %bitcast.57), calls=%async_computation | async-start | bytes 1048576 | tf_op jit(solution)/shard_map/all_to_all | solution.py:243
  61.9 15.2 %collective-permute-start.10 = (bf16[128,1792]{1,0:T(8,128)(2,1)S(1)}, bf16[128,1792]{1,0:T(8,128)(2,1)S(1)}, u32[]{:S(2)}, u32[]{:S(2)}) collective-permute-start(bf16[128,1792]{1,0:T(8,128)(2,1)S(1)} %fusion.9), channel_id=1, source_target_pairs={{0,8},{8,16},{16,24},{24,0},{1,9},{9,17},{17,25},{25,1},{2,10},{10... | collective-permute-start | bytes 1376264 | tf_op jit(solution)/shard_map/ppermute | solution.py:169
  71.2 15.9 %collective-permute-start.5 = (bf16[128,1792]{1,0:T(8,128)(2,1)}, bf16[128,1792]{1,0:T(8,128)(2,1)}, u32[]{:S(2)}, u32[]{:S(2)}) collective-permute-start(bf16[128,1792]{1,0:T(8,128)(2,1)} %fusion.6), channel_id=1, source_target_pairs={{0,8},{8,16},{16,24},{24,0},{1,9},{9,17},{17,25},{25,1},{2,10},{10... | collective-permute-start | bytes 1376264 | tf_op jit(solution)/shard_map/ppermute | solution.py:169
  81.5 15.1 %collective-permute-start.11 = (bf16[128,1792]{1,0:T(8,128)(2,1)S(1)}, bf16[128,1792]{1,0:T(8,128)(2,1)S(1)}, u32[]{:S(2)}, u32[]{:S(2)}) collective-permute-start(bf16[128,1792]{1,0:T(8,128)(2,1)S(1)} %fusion.8), channel_id=1, source_target_pairs={{0,8},{8,16},{16,24},{24,0},{1,9},{9,17},{17,25},{25,1},{2,10},{10... | collective-permute-start | bytes 1376264 | tf_op jit(solution)/shard_map/ppermute | solution.py:169
  98.1 14.9 %collective-permute-start.12 = (bf16[128,896]{1,0:T(8,128)(2,1)S(1)}, bf16[128,896]{1,0:T(8,128)(2,1)S(1)}, u32[]{:S(2)}, u32[]{:S(2)}) collective-permute-start(bf16[128,896]{1,0:T(8,128)(2,1)S(1)} %get-tuple-element.82.refs_0_), channel_id=1, source_target_pairs={{0,8},{8,16},{16,24},{24,0},{1,9},{9,17},{17,25},{25,1},{2,10},{10... | collective-permute-start | bytes 688136 | tf_op jit(solution)/shard_map/ppermute | solution.py:169
  98.1 14.1 %collective-permute-start.13 = (bf16[128,896]{1,0:T(8,128)(2,1)S(1)}, bf16[128,896]{1,0:T(8,128)(2,1)S(1)}, u32[]{:S(2)}, u32[]{:S(2)}) collective-permute-start(bf16[128,896]{1,0:T(8,128)(2,1)S(1)} %get-tuple-element.81.refs_1_), channel_id=1, source_target_pairs={{0,8},{8,16},{16,24},{24,0},{1,9},{9,17},{17,25},{25,1},{2,10},{10... | collective-permute-start | bytes 688136 | tf_op jit(solution)/shard_map/ppermute | solution.py:169
  113.0 14.5 %collective-permute-start.14 = (bf16[128,896]{1,0:T(8,128)(2,1)S(1)}, bf16[128,896]{1,0:T(8,128)(2,1)S(1)}, u32[]{:S(2)}, u32[]{:S(2)}) collective-permute-start(bf16[128,896]{1,0:T(8,128)(2,1)S(1)} %collective-permute-done.12.refs_2_), channel_id=1, source_target_pairs={{0,8},{8,16},{16,24},{24,0},{1,9},{9,17},{17,25},{25,1},{2,10},{10... | collective-permute-start | bytes 688136 | tf_op jit(solution)/shard_map/ppermute | solution.py:169
  174.9 11.0 %collective-permute-start.24 = (bf16[128,1024]{1,0:T(8,128)(2,1)S(1)}, bf16[128,1024]{1,0:T(8,128)(2,1)S(1)}, u32[]{:S(2)}, u32[]{:S(2)}) collective-permute-start(bf16[128,1024]{1,0:T(8,128)(2,1)S(1)} %convolution_convert_fusion.3), channel_id=1, source_target_pairs={{0,8},{8,16},{16,24},{24,0},{1,9},{9,17},{17,25},{25,1},{2,10},{10... | collective-permute-start | bytes 786440 | tf_op jit(solution)/shard_map/ppermute | solution.py:169
  175.7 15.8 %collective-permute-start.27 = (bf16[128,1024]{1,0:T(8,128)(2,1)S(1)}, bf16[128,1024]{1,0:T(8,128)(2,1)S(1)}, u32[]{:S(2)}, u32[]{:S(2)}) collective-permute-start(bf16[128,1024]{1,0:T(8,128)(2,1)S(1)} %convolution_convert_fusion.2), channel_id=1, source_target_pairs={{0,8},{8,16},{16,24},{24,0},{1,9},{9,17},{17,25},{25,1},{2,10},{10... | collective-permute-start | bytes 786440 | tf_op jit(solution)/shard_map/ppermute | solution.py:169
  186.6 10.8 %collective-permute-start.25 = (bf16[128,1024]{1,0:T(8,128)(2,1)S(1)}, bf16[128,1024]{1,0:T(8,128)(2,1)S(1)}, u32[]{:S(2)}, u32[]{:S(2)}) collective-permute-start(bf16[128,1024]{1,0:T(8,128)(2,1)S(1)} %fusion.29), channel_id=1, source_target_pairs={{0,8},{8,16},{16,24},{24,0},{1,9},{9,17},{17,25},{25,1},{2,10},{10... | collective-permute-start | bytes 786440 | tf_op jit(solution)/shard_map/ppermute | solution.py:169
  192.2 11.1 %collective-permute-start.28 = (bf16[128,1024]{1,0:T(8,128)(2,1)S(1)}, bf16[128,1024]{1,0:T(8,128)(2,1)S(1)}, u32[]{:S(2)}, u32[]{:S(2)}) collective-permute-start(bf16[128,1024]{1,0:T(8,128)(2,1)S(1)} %fusion.31), channel_id=1, source_target_pairs={{0,8},{8,16},{16,24},{24,0},{1,9},{9,17},{17,25},{25,1},{2,10},{10... | collective-permute-start | bytes 786440 | tf_op jit(solution)/shard_map/ppermute | solution.py:169
  216.3 17.1 %collective-permute-start.30 = (bf16[128,1024]{1,0:T(8,128)(2,1)S(1)}, bf16[128,1024]{1,0:T(8,128)(2,1)S(1)}, u32[]{:S(2)}, u32[]{:S(2)}) collective-permute-start(bf16[128,1024]{1,0:T(8,128)(2,1)S(1)} %get-tuple-element.77.refs_8_), channel_id=1, source_target_pairs={{0,8},{8,16},{16,24},{24,0},{1,9},{9,17},{17,25},{25,1},{2,10},{10... | collective-permute-start | bytes 786440 | tf_op jit(solution)/shard_map/ppermute | solution.py:169
  216.3 13.3 %collective-permute-start.31 = (bf16[128,1024]{1,0:T(8,128)(2,1)S(1)}, bf16[128,1024]{1,0:T(8,128)(2,1)S(1)}, u32[]{:S(2)}, u32[]{:S(2)}) collective-permute-start(bf16[128,1024]{1,0:T(8,128)(2,1)S(1)} %get-tuple-element.78.refs_9_), channel_id=1, source_target_pairs={{0,8},{8,16},{16,24},{24,0},{1,9},{9,17},{17,25},{25,1},{2,10},{10... | collective-permute-start | bytes 786440 | tf_op jit(solution)/shard_map/ppermute | solution.py:169
  229.7 10.9 %collective-permute-start.33 = (bf16[128,1024]{1,0:T(8,128)(2,1)S(1)}, bf16[128,1024]{1,0:T(8,128)(2,1)S(1)}, u32[]{:S(2)}, u32[]{:S(2)}) collective-permute-start(bf16[128,1024]{1,0:T(8,128)(2,1)S(1)} %collective-permute-done.31.refs_11_), channel_id=1, source_target_pairs={{0,8},{8,16},{16,24},{24,0},{1,9},{9,17},{17,25},{25,1},{2,10},{10... | collective-permute-start | bytes 786440 | tf_op jit(solution)/shard_map/ppermute | solution.py:169
  233.4 12.8 %collective-permute-start.32 = (bf16[128,1024]{1,0:T(8,128)(2,1)S(1)}, bf16[128,1024]{1,0:T(8,128)(2,1)S(1)}, u32[]{:S(2)}, u32[]{:S(2)}) collective-permute-start(bf16[128,1024]{1,0:T(8,128)(2,1)S(1)} %collective-permute-done.30.refs_10_), channel_id=1, source_target_pairs={{0,8},{8,16},{16,24},{24,0},{1,9},{9,17},{17,25},{25,1},{2,10},{10... | collective-permute-start | bytes 786440 | tf_op jit(solution)/shard_map/ppermute | solution.py:169
  240.5 10.9 %collective-permute-start.35 = (bf16[128,1024]{1,0:T(8,128)(2,1)S(1)}, bf16[128,1024]{1,0:T(8,128)(2,1)S(1)}, u32[]{:S(2)}, u32[]{:S(2)}) collective-permute-start(bf16[128,1024]{1,0:T(8,128)(2,1)S(1)} %collective-permute-done.33.refs_13_), channel_id=1, source_target_pairs={{0,8},{8,16},{16,24},{24,0},{1,9},{9,17},{17,25},{25,1},{2,10},{10... | collective-permute-start | bytes 786440 | tf_op jit(solution)/shard_map/ppermute | solution.py:169
  299.6 13.9 %collective-permute-start.45 = (bf16[128,896]{1,0:T(8,128)(2,1)S(1)}, bf16[128,896]{1,0:T(8,128)(2,1)S(1)}, u32[]{:S(2)}, u32[]{:S(2)}) collective-permute-start(bf16[128,896]{1,0:T(8,128)(2,1)S(1)} %convolution_convert_fusion.4.refs_16_), channel_id=1, source_target_pairs={{0,8},{8,16},{16,24},{24,0},{1,9},{9,17},{17,25},{25,1},{2,10},{10... | collective-permute-start | bytes 688136 | tf_op jit(solution)/shard_map/ppermute | solution.py:169
  299.7 15.8 %collective-permute-start.42 = (bf16[128,896]{1,0:T(8,128)(2,1)S(1)}, bf16[128,896]{1,0:T(8,128)(2,1)S(1)}, u32[]{:S(2)}, u32[]{:S(2)}) collective-permute-start(bf16[128,896]{1,0:T(8,128)(2,1)S(1)} %convolution_convert_fusion.5), channel_id=1, source_target_pairs={{0,8},{8,16},{16,24},{24,0},{1,9},{9,17},{17,25},{25,1},{2,10},{10... | collective-permute-start | bytes 688136 | tf_op jit(solution)/shard_map/ppermute | solution.py:169
  340.9 23.9 %collective-permute-start.51 = (bf16[128,1792]{1,0:T(8,128)(2,1)S(1)}, bf16[128,1792]{1,0:T(8,128)(2,1)S(1)}, u32[]{:S(2)}, u32[]{:S(2)}) collective-permute-start(bf16[128,1792]{1,0:T(8,128)(2,1)S(1)} %get-tuple-element.51.refs_8_), channel_id=1, source_target_pairs={{0,8},{8,16},{16,24},{24,0},{1,9},{9,17},{17,25},{25,1},{2,10},{10... | collective-permute-start | bytes 1376264 | tf_op jit(solution)/shard_map/ppermute | solution.py:169
  343.5 18.8 %collective-permute-start.48 = (bf16[128,1792]{1,0:T(8,128)(2,1)S(1)}, bf16[128,1792]{1,0:T(8,128)(2,1)S(1)}, u32[]{:S(2)}, u32[]{:S(2)}) collective-permute-start(bf16[128,1792]{1,0:T(8,128)(2,1)S(1)} %get-tuple-element.52.refs_16_.refs_8_), channel_id=1, source_target_pairs={{0,8},{8,16},{16,24},{24,0},{1,9},{9,17},{17,25},{25,1},{2,10},{10... | collective-permute-start | bytes 1376264 | tf_op jit(solution)/shard_map/ppermute | solution.py:169
  362.3 15.3 %collective-permute-start.49 = (bf16[128,1792]{1,0:T(8,128)(2,1)S(1)}, bf16[128,1792]{1,0:T(8,128)(2,1)S(1)}, u32[]{:S(2)}, u32[]{:S(2)}) collective-permute-start(bf16[128,1792]{1,0:T(8,128)(2,1)S(1)} %broadcast_select_fusion.1), channel_id=1, source_target_pairs={{0,8},{8,16},{16,24},{24,0},{1,9},{9,17},{17,25},{25,1},{2,10},{10... | collective-permute-start | bytes 1376264 | tf_op jit(solution)/shard_map/ppermute | solution.py:169
  364.8 22.6 %collective-permute-start.52 = (bf16[128,1792]{1,0:T(8,128)(2,1)S(1)}, bf16[128,1792]{1,0:T(8,128)(2,1)S(1)}, u32[]{:S(2)}, u32[]{:S(2)}) collective-permute-start(bf16[128,1792]{1,0:T(8,128)(2,1)S(1)} %collective-permute-done.51.refs_9_), channel_id=1, source_target_pairs={{0,8},{8,16},{16,24},{24,0},{1,9},{9,17},{17,25},{25,1},{2,10},{10... | collective-permute-start | bytes 1376264 | tf_op jit(solution)/shard_map/ppermute | solution.py:169
  377.6 19.7 %collective-permute-start.50 = (bf16[128,1792]{1,0:T(8,128)(2,1)S(1)}, bf16[128,1792]{1,0:T(8,128)(2,1)S(1)}, u32[]{:S(2)}, u32[]{:S(2)}) collective-permute-start(bf16[128,1792]{1,0:T(8,128)(2,1)S(1)} %collective-permute-done.49.refs_10_), channel_id=1, source_target_pairs={{0,8},{8,16},{16,24},{24,0},{1,9},{9,17},{17,25},{25,1},{2,10},{10... | collective-permute-start | bytes 1376264 | tf_op jit(solution)/shard_map/ppermute | solution.py:169
  387.4 14.9 %collective-permute-start.53 = (bf16[128,1792]{1,0:T(8,128)(2,1)S(1)}, bf16[128,1792]{1,0:T(8,128)(2,1)S(1)}, u32[]{:S(2)}, u32[]{:S(2)}) collective-permute-start(bf16[128,1792]{1,0:T(8,128)(2,1)S(1)} %collective-permute-done.52.refs_10_), channel_id=1, source_target_pairs={{0,8},{8,16},{16,24},{24,0},{1,9},{9,17},{17,25},{25,1},{2,10},{10... | collective-permute-start | bytes 1376264 | tf_op jit(solution)/shard_map/ppermute | solution.py:169
  414.2 25.1 %collective-permute-start.55 = (bf16[128,2048]{1,0:T(8,128)(2,1)}, bf16[128,2048]{1,0:T(8,128)(2,1)}, u32[]{:S(2)}, u32[]{:S(2)}) collective-permute-start(bf16[128,2048]{1,0:T(8,128)(2,1)} %slice.403.refs_12_), channel_id=1, source_target_pairs={{0,4},{1,3},{2,6},{3,1},{4,0},{5,7},{6,2},{7,5},{8,12},{9,11},{10,... | collective-permute-start | bytes 1572872 | tf_op jit(solution)/shard_map/ppermute | solution.py:129
  440.6 11.4 %collective-permute-start.56 = (bf16[64,2048]{1,0:T(8,128)(2,1)S(1)}, bf16[64,2048]{1,0:T(8,128)(2,1)S(1)}, u32[]{:S(2)}, u32[]{:S(2)}) collective-permute-start(bf16[64,2048]{1,0:T(8,128)(2,1)S(1)} %slice.406.refs_12_), channel_id=1, source_target_pairs={{0,2},{1,5},{2,0},{3,7},{4,6},{5,1},{6,4},{7,3},{8,10},{9,13},{10,... | collective-permute-start | bytes 786440 | tf_op jit(solution)/shard_map/ppermute | solution.py:129
  (72 other events, 690.0 us)

commit v2 on v1

--- a/solution.py
+++ b/solution.py
@@ -20,9 +20,9 @@
     return lax.dot_general(left, right, (((1,), (1,)), ((), ())), preferred_element_type=F32)
 
 
-def grad_kernel(places, tile, *refs):
-    pieces = refs[: len(places)]
-    out_ref, _, left, right, sems = refs[-5:]
+def grad_kernel(places, n_inputs, tile, *refs):
+    pieces, out_ref = refs[: len(places)], refs[n_inputs]
+    left, right, sems = refs[-3:]
 
     @pl.when(pl.program_id(0) == 0)
     def load():
@@ -55,17 +55,17 @@
         shapes.append((row, column))
     (depth, m), (_, n) = shapes
     tile = 256 if m % 256 == 0 else 128
-    operands = pieces + list(earlier) + [through]
-    return pl.pallas_call(
-        functools.partial(grad_kernel, places, tile),
+    operands = pieces + list(earlier) + list(through)
+    first = len(operands) - len(through)
+    made, *through = pl.pallas_call(
+        functools.partial(grad_kernel, places, len(operands), tile),
         grid=(m // tile,),
         in_specs=[pl.BlockSpec(memory_space=pl.ANY)] * len(operands),
-        out_specs=[pl.BlockSpec((tile, n), lambda i: (i, 0)), pl.BlockSpec(memory_space=pl.ANY)],
-        out_shape=[
-            jax.ShapeDtypeStruct((m, n), F32),
-            jax.ShapeDtypeStruct(through.shape, through.dtype),
-        ],
-        input_output_aliases={len(operands) - 1: 1},
+        out_specs=[pl.BlockSpec((tile, n), lambda i: (i, 0))]
+        + [pl.BlockSpec(memory_space=pl.ANY)] * len(through),
+        out_shape=[jax.ShapeDtypeStruct((m, n), F32)]
+        + [jax.ShapeDtypeStruct(a.shape, a.dtype) for a in through],
+        input_output_aliases={first + i: 1 + i for i in range(len(through))},
         scratch_shapes=[
             pltpu.VMEM((depth, m), BF16),
             pltpu.VMEM((depth, n), BF16),
@@ -78,6 +78,7 @@
             transcendentals=0,
         ),
     )(*operands)
+    return made, through
 
 
 def reverse_bits(value, width):
@@ -128,14 +129,17 @@
             kept, sent = acc[:half], acc[half:].astype(full.dtype)
             got = lax.ppermute(sent, PLANE, perm)
             if i < len(beside):
-                kept = beside[i](kept, sent)
+                (kept,) = beside[i]([kept], sent)
             acc = kept + got.astype(F32)
         return acc
 
-    def total(self, value):
-        for perm in self.perms + [self.swap]:
-            value = value + lax.ppermute(value, PLANE, perm)
-        return value
+    def sum_direct(self, value):
+        value = value + lax.ppermute(value, PLANE, self.swap)
+        total = value
+        for chip in range(2, self.size, 2):
+            perm = [(c, c ^ chip) for c in range(self.size)]
+            total = total + lax.ppermute(value, PLANE, perm)
+        return total
 
 
 class Rows:
@@ -174,7 +178,7 @@
             rows = jnp.concatenate(parts[back % self.size], axis=0)
             sums = [product(rows) for product in products]
             if back == 2 and beside is not None:
-                sums[-1] = beside(sums[-1], sent[-1])
+                (sums[-1],) = beside([sums[-1]], sent[-1])
             if got is not None:
                 sums = [s + g.astype(F32) for s, g in zip(sums, got)]
             if back < self.size:
@@ -183,13 +187,10 @@
                 first = got[0] if first is None else first
         return sums, first
 
-    def gather(self, blocks, product, beside=None):
+    def gather(self, blocks, product):
         steps = [blocks]
         for back in range(1, self.size):
-            sent = steps[-1]
-            if back == 2 and beside is not None:
-                sent = sent[:-1] + [after(sent[-1], beside)]
-            steps.append([self.shift(b) for b in sent])
+            steps.append([self.shift(b) for b in steps[-1]])
         made = [product(step) for step in steps]
         return steps, made, self.placed(made)
 
@@ -206,13 +207,6 @@
                 value, "row", [(r, r ^ step) for r in range(self.size)]
             )
         return total
-
-    def total(self, value):
-        step = 1
-        while step < self.size:
-            value = value + lax.ppermute(value, "row", [(r, r ^ step) for r in range(self.size)])
-            step *= 2
-        return value
 
     def own_order(self, value):
         half = value.shape[0] // 2
@@ -269,14 +263,17 @@
             [m.astype(BF16) for m in masked],
             lambda bs: sum(mm_t(b, proj_w[:, lo:hi]) for b, (lo, hi) in zip(bs, ecuts)).astype(BF16),
         )
-        resid_grad = plane.scatter(back).astype(BF16)
-        resid_grads = rows.parts(*plane.gather(resid_grad))
-
         found = {}
 
         def grad(name, lefts, rights, through, *earlier):
             found[name], through = weight_grad(lefts, rights, through, *earlier)
             return through
+
+        resid_grad = plane.scatter(
+            back,
+            [lambda kept, sent: grad("proj", lines(residuals), pred_grads, kept, sent)],
+        ).astype(BF16)
+        resid_grads = rows.parts(*plane.gather(resid_grad))
 
         hid_grad, _ = rows.reduce(
             resid_grads,
@@ -288,30 +285,28 @@
         up_grad = hid_grad * activated
         blocks = [(gate_grad * inv).astype(BF16), (up_grad * inv).astype(BF16)]
 
-        last = grad("proj", lines(residuals), pred_grads, keep, blocks[1])
         grads, made, back = rows.gather(
             blocks,
             lambda b: (mm_t(b[0], gate_w) + mm_t(b[1], up_w)).astype(BF16),
-            last,
         )
         gates, ups = [g[:1] for g in grads], [g[1:] for g in grads]
-        normed_grad = plane.scatter(
-            back,
-            (
-                lambda kept, sent: grad("gate", lines(scaled), gates, kept, sent),
-                lambda kept, sent: grad("up", lines(scaled), ups, kept, sent),
-            ),
-        )
-        inner = jnp.sum(normed_grad * gain[None, :] * x.astype(F32), axis=1)
         loss_sum = 0.5 * sum(jnp.sum(m * e) for m, e in zip(masked, error))
-        loss_parts = jnp.stack([loss_sum, jnp.sum(last)])
         gain_sum = sum(
             jnp.sum(m.astype(F32) * jnp.concatenate(p, axis=0).astype(F32), axis=0)
             for m, p in zip(made, scaled)
         )
-        sums = plane.total(jnp.concatenate([gain_sum / gain, loss_parts]))
+        normed_grad = plane.scatter(
+            back,
+            [
+                lambda kept, sent: grad("gate", lines(scaled), gates, kept, sent),
+                lambda kept, sent: grad("up", lines(scaled), ups, kept, sent),
+            ],
+        )
+        sums = jnp.concatenate([gain_sum / gain, jnp.stack([loss_sum, jnp.sum(keep)])])
+        sums = plane.sum_direct(sums)
         grad_gain = sums[:-2]
-        sums = rows.total(jnp.concatenate([inner, sums[-2:]]))
+        inner = jnp.sum(normed_grad * gain[None, :] * x.astype(F32), axis=1)
+        sums = rows.sum_direct(jnp.concatenate([inner, sums[-2:]]))
         inner = sums[:-2]
         loss_value = sums[-2] / (sums[-1] / n_plane)
 

time: 474 us -> 453 us (0.956)
  matrix products: 104 us -> 80.3 us
  local copies, waits for them, and re-layouts: 15.7 us -> 9.46 us
  starting transfers between devices: 45 us -> 50.1 us
  waiting for transfers between devices: 237 us -> 242 us
    ppermute x36, waiting for transfers between devices: 148 us -> 175 us  [shift(): return lax.ppermute(value, 'row', self.ring)]
    dot_general x24, matrix products: 66 us -> 42.2 us  [mm_t(): lax.dot_general(left, right, (((1,), (1,)), ((), ())), preferred_element_...]
    ppermute x5 -> x4, waiting for transfers between devices: 14 us -> 1.11 us  [the longest x1 0.83 us: sum_direct(): value = value + lax.ppermute(value, PLANE, self.swap)]
    ppermute x6, waiting for transfers between devices: 25.8 us -> 17.8 us  [scatter(): got = lax.ppermute(sent, PLANE, perm)]
  transfers between devices with their start and end apart: 63 -> 65, of which waited for: 49 -> 49; matrix products, arithmetic and copies ran while one was open for 20% -> 17% of each run, Pallas kernels for 8% -> 9%
where the time goes in v2:
time: 453 us; the launch traced here: 444 us
  waiting for transfers between devices  242 us (53%)
  matrix products  80.3 us (18%)
  starting transfers between devices  50.1 us (11%)
  Pallas kernels  37.9 us (8%)
  between operations  14.5 us (3%)
  other arithmetic  10.1 us (2%)
  local copies, waits for them, and re-layouts  9.46 us (2%)
    ppermute x36, waiting for transfers between devices, shift(): return lax.ppermute(value, 'row', self.ring)  175 us
    dot_general x24, matrix products, mm_t(): lax.dot_general(left, right, (((1,), (1,)), ((), ())), preferred_element_...  42.2 us
    dot_general x24, matrix products, mm(): return jnp.dot(left, right, preferred_element_type=F32)  38.1 us
    pallas_call x4, Pallas kernels, weight_grad(): pl.pallas_call(functools.partial(grad_kernel, places, len(operands), tile...  37.9 us
    ppermute x6, waiting for transfers between devices, gather(): own = jnp.concatenate([own, lax.ppermute(own, PLANE, perm)], axis=0)  37.8 us
    ppermute x6, waiting for transfers between devices, scatter(): got = lax.ppermute(sent, PLANE, perm)  17.8 us
    ppermute x36, starting transfers between devices, shift(): return lax.ppermute(value, 'row', self.ring)  15.2 us
    ppermute x6, starting transfers between devices, gather(): own = jnp.concatenate([own, lax.ppermute(own, PLANE, perm)], axis=0)  10.2 us
  transfers between devices with their start and end apart: 65, of which 49 were waited for; matrix products, arithmetic and copies ran while one was open for 17% of the time, Pallas kernels for 9%

profile of v2, /device:TPU:0, one launch (start us, length us, event | category | flops | bytes accessed | tf_op | source)
XLA Modules:
  0.0 444.3 jit_solution(15620172098330356549)
XLA Ops:
  4.7 4.4 collective-permute-done
  11.2 7.2 %collective-permute-done.1 = bf16[128,2048]{1,0:T(8,128)(2,1)S(1)} collective-permute-done((bf16[128,2048]{1,0:T(8,128)(2,1)S(1)}, bf16[128,2048]{1,0:T(8,128)(2,1)S(1)}, u32[]{:S(2)}, u32[]{:S(2)}) %collective-permute-start.1) | collective-permute-done | bytes 524320 | tf_op jit(solution)/shard_map/ppermute | solution.py:116
  24.7 4.4 convolution_convert_fusion.1
  35.4 9.2 %collective-permute-done.3 = bf16[128,1792]{1,0:T(8,128)(2,1)S(1)} collective-permute-done((bf16[128,1792]{1,0:T(8,128)(2,1)S(1)}, bf16[128,1792]{1,0:T(8,128)(2,1)S(1)}, u32[]{:S(2)}, u32[]{:S(2)}) %collective-permute-start.3) | collective-permute-done | bytes 458784 | tf_op jit(solution)/shard_map/ppermute | solution.py:173
  66.2 5.0 %fusion.6 = bf16[128,1792]{1,0:T(8,128)(2,1)} fusion(bf16[2048,1792]{1,0:T(8,128)(2,1)} %param.14, bf16[128,1792]{1,0:T(8,128)(2,1)} %collective-permute-done.4, bf16[64,2048]{1,0:T(8,128)(2,1)S(1)} %get-tuple-element.76.refs_7_, bf16[64,2048]{1,0:T(8,128)(2,1)S(1)} %get-tuple-element.72.refs_6_), kind=kOutput, calls=%fused_computation.24 | convolution fusion | flops 941260800 | bytes 8781824 | tf_op jit(solution)/shard_map/dot_general | solution.py:16
  77.2 4.4 fusion.8
  81.7 5.4 %collective-permute-done.5 = bf16[128,1792]{1,0:T(8,128)(2,1)} collective-permute-done((bf16[128,1792]{1,0:T(8,128)(2,1)}, bf16[128,1792]{1,0:T(8,128)(2,1)}, u32[]{:S(2)}, u32[]{:S(2)}) %collective-permute-start.5) | collective-permute-done | bytes 458784 | tf_op jit(solution)/shard_map/ppermute | solution.py:173
  89.5 7.1 %collective-permute-done.11 = bf16[128,1792]{1,0:T(8,128)(2,1)S(1)} collective-permute-done((bf16[128,1792]{1,0:T(8,128)(2,1)S(1)}, bf16[128,1792]{1,0:T(8,128)(2,1)S(1)}, u32[]{:S(2)}, u32[]{:S(2)}) %collective-permute-start.11) | collective-permute-done | bytes 458784 | tf_op jit(solution)/shard_map/ppermute | solution.py:173
  100.9 11.4 %collective-permute-done.13.refs_3_ = bf16[128,896]{1,0:T(8,128)(2,1)S(1)} collective-permute-done((bf16[128,896]{1,0:T(8,128)(2,1)S(1)}, bf16[128,896]{1,0:T(8,128)(2,1)S(1)}, u32[]{:S(2)}, u32[]{:S(2)}) %collective-permute-start.13) | collective-permute-done | bytes 229408 | tf_op jit(solution)/shard_map/ppermute | solution.py:173
  113.8 8.8 %collective-permute-done.15.refs_5_ = bf16[128,896]{1,0:T(8,128)(2,1)S(1)} collective-permute-done((bf16[128,896]{1,0:T(8,128)(2,1)S(1)}, bf16[128,896]{1,0:T(8,128)(2,1)S(1)}, u32[]{:S(2)}, u32[]{:S(2)}) %collective-permute-start.15) | collective-permute-done | bytes 229408 | tf_op jit(solution)/shard_map/ppermute | solution.py:173
  128.2 4.6 %collective-permute-done.17.refs_7_ = bf16[128,896]{1,0:T(8,128)(2,1)S(1)} collective-permute-done((bf16[128,896]{1,0:T(8,128)(2,1)S(1)}, bf16[128,896]{1,0:T(8,128)(2,1)S(1)}, u32[]{:S(2)}, u32[]{:S(2)}) %collective-permute-start.17) | collective-permute-done | bytes 229408 | tf_op jit(solution)/shard_map/ppermute | solution.py:173
  140.9 7.8 %collective-permute-done.19 = bf16[128,2048]{1,0:T(8,128)(2,1)S(1)} collective-permute-done((bf16[128,2048]{1,0:T(8,128)(2,1)S(1)}, bf16[128,2048]{1,0:T(8,128)(2,1)S(1)}, u32[]{:S(2)}, u32[]{:S(2)}) %collective-permute-start.19) | collective-permute-done | bytes 524320 | tf_op jit(solution)/shard_map/ppermute | solution.py:130
  150.3 5.0 %collective-permute-done.20 = bf16[64,2048]{1,0:T(8,128)(2,1)S(1)} collective-permute-done((bf16[64,2048]{1,0:T(8,128)(2,1)S(1)}, bf16[64,2048]{1,0:T(8,128)(2,1)S(1)}, u32[]{:S(2)}, u32[]{:S(2)}) %collective-permute-start.20) | collective-permute-done | bytes 262176 | tf_op jit(solution)/shard_map/ppermute | solution.py:130
  156.9 5.0 %collective-permute-done.21 = bf16[64,2048]{1,0:T(8,128)(2,1)S(1)} collective-permute-done((bf16[64,2048]{1,0:T(8,128)(2,1)S(1)}, bf16[64,2048]{1,0:T(8,128)(2,1)S(1)}, u32[]{:S(2)}, u32[]{:S(2)}) %collective-permute-start.21) | collective-permute-done | bytes 262176 | tf_op jit(solution)/shard_map/ppermute | solution.py:116
  163.4 7.8 %collective-permute-done.22 = bf16[128,2048]{1,0:T(8,128)(2,1)S(1)} collective-permute-done((bf16[128,2048]{1,0:T(8,128)(2,1)S(1)}, bf16[128,2048]{1,0:T(8,128)(2,1)S(1)}, u32[]{:S(2)}, u32[]{:S(2)}) %collective-permute-start.22) | collective-permute-done | bytes 524320 | tf_op jit(solution)/shard_map/ppermute | solution.py:116
  175.8 10.1 %collective-permute-done.24 = bf16[128,1024]{1,0:T(8,128)(2,1)S(1)} collective-permute-done((bf16[128,1024]{1,0:T(8,128)(2,1)S(1)}, bf16[128,1024]{1,0:T(8,128)(2,1)S(1)}, u32[]{:S(2)}, u32[]{:S(2)}) %collective-permute-start.24) | collective-permute-done | bytes 262176 | tf_op jit(solution)/shard_map/ppermute | solution.py:173
  186.7 4.8 %collective-permute-done.27 = bf16[128,1024]{1,0:T(8,128)(2,1)S(1)} collective-permute-done((bf16[128,1024]{1,0:T(8,128)(2,1)S(1)}, bf16[128,1024]{1,0:T(8,128)(2,1)S(1)}, u32[]{:S(2)}, u32[]{:S(2)}) %collective-permute-start.27) | collective-permute-done | bytes 262176 | tf_op jit(solution)/shard_map/ppermute | solution.py:173
  192.3 5.1 %collective-permute-done.25 = bf16[128,1024]{1,0:T(8,128)(2,1)S(1)} collective-permute-done((bf16[128,1024]{1,0:T(8,128)(2,1)S(1)}, bf16[128,1024]{1,0:T(8,128)(2,1)S(1)}, u32[]{:S(2)}, u32[]{:S(2)}) %collective-permute-start.25) | collective-permute-done | bytes 262176 | tf_op jit(solution)/shard_map/ppermute | solution.py:173
  198.2 5.1 %collective-permute-done.28 = bf16[128,1024]{1,0:T(8,128)(2,1)S(1)} collective-permute-done((bf16[128,1024]{1,0:T(8,128)(2,1)S(1)}, bf16[128,1024]{1,0:T(8,128)(2,1)S(1)}, u32[]{:S(2)}, u32[]{:S(2)}) %collective-permute-start.28) | collective-permute-done | bytes 262176 | tf_op jit(solution)/shard_map/ppermute | solution.py:173
  218.2 10.0 %collective-permute-done.31.refs_11_ = bf16[128,1024]{1,0:T(8,128)(2,1)S(1)} collective-permute-done((bf16[128,1024]{1,0:T(8,128)(2,1)S(1)}, bf16[128,1024]{1,0:T(8,128)(2,1)S(1)}, u32[]{:S(2)}, u32[]{:S(2)}) %collective-permute-start.31) | collective-permute-done | bytes 262176 | tf_op jit(solution)/shard_map/ppermute | solution.py:173
  231.3 7.8 %collective-permute-done.33.refs_13_ = bf16[128,1024]{1,0:T(8,128)(2,1)S(1)} collective-permute-done((bf16[128,1024]{1,0:T(8,128)(2,1)S(1)}, bf16[128,1024]{1,0:T(8,128)(2,1)S(1)}, u32[]{:S(2)}, u32[]{:S(2)}) %collective-permute-start.33) | collective-permute-done | bytes 262176 | tf_op jit(solution)/shard_map/ppermute | solution.py:173
  259.7 9.5 %shard_map.171 = (f32[2048,2048]{1,0:T(8,128)}, f32[128,2048]{1,0:T(8,128)S(1)}) custom-call(bf16[64,2048]{1,0:T(8,128)(2,1)S(1)} %get-tuple-element.70.refs_0_, bf16[64,2048]{1,0:T(8,128)(2,1)S(1)} %get-tuple-element.66.refs_1_, bf16[64,2048]{1,0:T(8,128)(2,1)S(1)} %get-tuple-element.69.refs_2_, ...), custom_call_target="tpu_custom_call", output_to_operand_aliasing={{1}: (17, {})} | custom-call | flops 4294967296 | bytes 20971520 | tf_op jit(solution)/shard_map/pallas_call | solution.py:60
  270.9 4.9 %collective-permute-done.38 = bf16[64,2048]{1,0:T(8,128)(2,1)S(1)} collective-permute-done((bf16[64,2048]{1,0:T(8,128)(2,1)S(1)}, bf16[64,2048]{1,0:T(8,128)(2,1)S(1)}, u32[]{:S(2)}, u32[]{:S(2)}) %collective-permute-start.38) | collective-permute-done | bytes 262176 | tf_op jit(solution)/shard_map/ppermute | solution.py:130
  277.4 4.9 %collective-permute-done.39 = bf16[64,2048]{1,0:T(8,128)(2,1)S(1)} collective-permute-done((bf16[64,2048]{1,0:T(8,128)(2,1)S(1)}, bf16[64,2048]{1,0:T(8,128)(2,1)S(1)}, u32[]{:S(2)}, u32[]{:S(2)}) %collective-permute-start.39) | collective-permute-done | bytes 262176 | tf_op jit(solution)/shard_map/ppermute | solution.py:116
  283.1 8.5 %collective-permute-done.40 = bf16[128,2048]{1,0:T(8,128)(2,1)S(1)} collective-permute-done((bf16[128,2048]{1,0:T(8,128)(2,1)S(1)}, bf16[128,2048]{1,0:T(8,128)(2,1)S(1)}, u32[]{:S(2)}, u32[]{:S(2)}) %collective-permute-start.40) | collective-permute-done | bytes 524320 | tf_op jit(solution)/shard_map/ppermute | solution.py:116
  298.5 8.8 %shard_map.172 = (f32[1792,2048]{1,0:T(8,128)}, f32[128,896]{1,0:T(8,128)S(1)}) custom-call(bf16[128,896]{1,0:T(8,128)(2,1)S(1)} %get-tuple-element.84.refs_0_, bf16[128,896]{1,0:T(8,128)(2,1)S(1)} %get-tuple-element.83.refs_1_, bf16[128,896]{1,0:T(8,128)(2,1)S(1)} %collective-permute-done.12.refs_2_, ...), custom_call_target="tpu_custom_call", output_to_operand_aliasing={{1}: (17, {})} | custom-call | flops 3758096384 | bytes 18612224 | tf_op jit(solution)/shard_map/pallas_call | solution.py:60
  341.4 14.9 %collective-permute-done.48.refs_9_ = bf16[128,1792]{1,0:T(8,128)(2,1)S(1)} collective-permute-done((bf16[128,1792]{1,0:T(8,128)(2,1)S(1)}, bf16[128,1792]{1,0:T(8,128)(2,1)S(1)}, u32[]{:S(2)}, u32[]{:S(2)}) %collective-permute-start.48) | collective-permute-done | bytes 458784 | tf_op jit(solution)/shard_map/ppermute | solution.py:173
  361.8 9.7 %collective-permute-done.49.refs_10_ = bf16[128,1792]{1,0:T(8,128)(2,1)S(1)} collective-permute-done((bf16[128,1792]{1,0:T(8,128)(2,1)S(1)}, bf16[128,1792]{1,0:T(8,128)(2,1)S(1)}, u32[]{:S(2)}, u32[]{:S(2)}) %collective-permute-start.49) | collective-permute-done | bytes 458784 | tf_op jit(solution)/shard_map/ppermute | solution.py:173
  374.0 7.4 %collective-permute-done.52.refs_10_ = bf16[128,1792]{1,0:T(8,128)(2,1)S(1)} collective-permute-done((bf16[128,1792]{1,0:T(8,128)(2,1)S(1)}, bf16[128,1792]{1,0:T(8,128)(2,1)S(1)}, u32[]{:S(2)}, u32[]{:S(2)}) %collective-permute-start.52) | collective-permute-done | bytes 458784 | tf_op jit(solution)/shard_map/ppermute | solution.py:173
  384.2 7.0 %collective-permute-done.50.refs_11_ = bf16[128,1792]{1,0:T(8,128)(2,1)S(1)} collective-permute-done((bf16[128,1792]{1,0:T(8,128)(2,1)S(1)}, bf16[128,1792]{1,0:T(8,128)(2,1)S(1)}, u32[]{:S(2)}, u32[]{:S(2)}) %collective-permute-start.50) | collective-permute-done | bytes 458784 | tf_op jit(solution)/shard_map/ppermute | solution.py:173
  412.5 9.8 %shard_map.173 = (f32[2048,1792]{1,0:T(8,128)}, f32[128,2048]{1,0:T(8,128)S(1)}) custom-call(bf16[64,2048]{1,0:T(8,128)(2,1)S(1)} %get-tuple-element.71.refs_0_, bf16[64,2048]{1,0:T(8,128)(2,1)S(1)} %get-tuple-element.75.refs_1_, bf16[64,2048]{1,0:T(8,128)(2,1)S(1)} %get-tuple-element.74.refs_2_, ...), custom_call_target="tpu_custom_call", output_to_operand_aliasing={{1}: (13, {})} | custom-call | flops 3758096384 | bytes 18612224 | tf_op jit(solution)/shard_map/pallas_call | solution.py:60
  423.8 9.8 %shard_map.174 = (f32[2048,1792]{1,0:T(8,128)}, f32[64,2048]{1,0:T(8,128)S(1)}) custom-call(bf16[64,2048]{1,0:T(8,128)(2,1)S(1)} %get-tuple-element.71.refs_0_, bf16[64,2048]{1,0:T(8,128)(2,1)S(1)} %get-tuple-element.75.refs_1_, bf16[64,2048]{1,0:T(8,128)(2,1)S(1)} %get-tuple-element.74.refs_2_, ...), custom_call_target="tpu_custom_call", output_to_operand_aliasing={{1}: (13, {})} | custom-call | flops 3758096384 | bytes 18612224 | tf_op jit(solution)/shard_map/pallas_call | solution.py:60
  (313 shorter events, 194.1 us)
Async XLA Ops:
  29.1 15.5 %collective-permute-start.3 = (bf16[128,1792]{1,0:T(8,128)(2,1)S(1)}, bf16[128,1792]{1,0:T(8,128)(2,1)S(1)}, u32[]{:S(2)}, u32[]{:S(2)}) collective-permute-start(bf16[128,1792]{1,0:T(8,128)(2,1)S(1)} %convolution_convert_fusion.1), channel_id=1, source_target_pairs={{0,8},{8,16},{16,24},{24,0},{1,9},{9,17},{17,25},{25,1},{2,10},{10... | collective-permute-start | bytes 1376264 | tf_op jit(solution)/shard_map/ppermute | solution.py:173
  33.2 24.5 %collective-permute-start.9 = (bf16[128,1792]{1,0:T(8,128)(2,1)}, bf16[128,1792]{1,0:T(8,128)(2,1)}, u32[]{:S(2)}, u32[]{:S(2)}) collective-permute-start(bf16[128,1792]{1,0:T(8,128)(2,1)} %convolution_convert_fusion), channel_id=1, source_target_pairs={{0,8},{8,16},{16,24},{24,0},{1,9},{9,17},{17,25},{25,1},{2,10},{10... | collective-permute-start | bytes 1376264 | tf_op jit(solution)/shard_map/ppermute | solution.py:173
  46.5 16.4 %collective-permute-start.8 = (f32[512]{0:T(512)S(1)}, f32[512]{0:T(512)S(1)}, u32[]{:S(2)}, u32[]{:S(2)}) collective-permute-start(f32[512]{0:T(512)S(1)} %maximum_select_fusion.1), channel_id=1, source_target_pairs={{0,24},{8,16},{16,8},{24,0},{1,25},{9,17},{17,9},{25,1},{2,26},{10... | collective-permute-start | bytes 6152 | tf_op jit(solution)/shard_map/ppermute | solution.py:206
  48.5 14.4 %collective-permute-start.7 = (f32[512]{0:T(512)S(1)}, f32[512]{0:T(512)}, u32[]{:S(2)}, u32[]{:S(2)}) collective-permute-start(f32[512]{0:T(512)S(1)} %maximum_select_fusion.1), channel_id=1, source_target_pairs={{0,16},{8,24},{16,0},{24,8},{1,17},{9,25},{17,1},{25,9},{2,18},{10... | collective-permute-start | bytes 6152 | tf_op jit(solution)/shard_map/ppermute | solution.py:206
  48.5 15.0 %collective-permute-start.6 = (f32[512]{0:T(512)S(1)}, f32[512]{0:T(512)}, u32[]{:S(2)}, u32[]{:S(2)}) collective-permute-start(f32[512]{0:T(512)S(1)} %maximum_select_fusion.1), channel_id=1, source_target_pairs={{0,8},{8,0},{16,24},{24,16},{1,9},{9,1},{17,25},{25,17},{2,10},{10... | collective-permute-start | bytes 6152 | tf_op jit(solution)/shard_map/ppermute | solution.py:206
  52.9 13.3 %collective-permute-start.4 = (bf16[128,1792]{1,0:T(8,128)(2,1)}, bf16[128,1792]{1,0:T(8,128)(2,1)}, u32[]{:S(2)}, u32[]{:S(2)}) collective-permute-start(bf16[128,1792]{1,0:T(8,128)(2,1)} %fusion.7), channel_id=1, source_target_pairs={{0,8},{8,16},{16,24},{24,0},{1,9},{9,17},{17,25},{25,1},{2,10},{10... | collective-permute-start | bytes 1376264 | tf_op jit(solution)/shard_map/ppermute | solution.py:173
  53.8 18.1 %all-to-all-start = ((bf16[16,8,2048]{2,0,1:T(8,128)(2,1)}), bf16[16,8,2048]{2,0,1:T(8,128)(2,1)S(1)}, u32[]{:S(2)}, u32[]{:S(2)}) async-start(bf16[16,8,2048]{2,0,1:T(8,128)(2,1)} %bitcast.56), calls=%async_computation | async-start | bytes 1048576 | tf_op jit(solution)/shard_map/all_to_all | solution.py:237
  61.9 15.2 %collective-permute-start.10 = (bf16[128,1792]{1,0:T(8,128)(2,1)S(1)}, bf16[128,1792]{1,0:T(8,128)(2,1)S(1)}, u32[]{:S(2)}, u32[]{:S(2)}) collective-permute-start(bf16[128,1792]{1,0:T(8,128)(2,1)S(1)} %fusion.9), channel_id=1, source_target_pairs={{0,8},{8,16},{16,24},{24,0},{1,9},{9,17},{17,25},{25,1},{2,10},{10... | collective-permute-start | bytes 1376264 | tf_op jit(solution)/shard_map/ppermute | solution.py:173
  71.2 15.9 %collective-permute-start.5 = (bf16[128,1792]{1,0:T(8,128)(2,1)}, bf16[128,1792]{1,0:T(8,128)(2,1)}, u32[]{:S(2)}, u32[]{:S(2)}) collective-permute-start(bf16[128,1792]{1,0:T(8,128)(2,1)} %fusion.6), channel_id=1, source_target_pairs={{0,8},{8,16},{16,24},{24,0},{1,9},{9,17},{17,25},{25,1},{2,10},{10... | collective-permute-start | bytes 1376264 | tf_op jit(solution)/shard_map/ppermute | solution.py:173
  81.5 15.1 %collective-permute-start.11 = (bf16[128,1792]{1,0:T(8,128)(2,1)S(1)}, bf16[128,1792]{1,0:T(8,128)(2,1)S(1)}, u32[]{:S(2)}, u32[]{:S(2)}) collective-permute-start(bf16[128,1792]{1,0:T(8,128)(2,1)S(1)} %fusion.8), channel_id=1, source_target_pairs={{0,8},{8,16},{16,24},{24,0},{1,9},{9,17},{17,25},{25,1},{2,10},{10... | collective-permute-start | bytes 1376264 | tf_op jit(solution)/shard_map/ppermute | solution.py:173
  98.1 14.9 %collective-permute-start.12 = (bf16[128,896]{1,0:T(8,128)(2,1)S(1)}, bf16[128,896]{1,0:T(8,128)(2,1)S(1)}, u32[]{:S(2)}, u32[]{:S(2)}) collective-permute-start(bf16[128,896]{1,0:T(8,128)(2,1)S(1)} %get-tuple-element.84.refs_0_), channel_id=1, source_target_pairs={{0,8},{8,16},{16,24},{24,0},{1,9},{9,17},{17,25},{25,1},{2,10},{10... | collective-permute-start | bytes 688136 | tf_op jit(solution)/shard_map/ppermute | solution.py:173
  98.1 14.1 %collective-permute-start.13 = (bf16[128,896]{1,0:T(8,128)(2,1)S(1)}, bf16[128,896]{1,0:T(8,128)(2,1)S(1)}, u32[]{:S(2)}, u32[]{:S(2)}) collective-permute-start(bf16[128,896]{1,0:T(8,128)(2,1)S(1)} %get-tuple-element.83.refs_1_), channel_id=1, source_target_pairs={{0,8},{8,16},{16,24},{24,0},{1,9},{9,17},{17,25},{25,1},{2,10},{10... | collective-permute-start | bytes 688136 | tf_op jit(solution)/shard_map/ppermute | solution.py:173
  113.0 14.5 %collective-permute-start.14 = (bf16[128,896]{1,0:T(8,128)(2,1)S(1)}, bf16[128,896]{1,0:T(8,128)(2,1)S(1)}, u32[]{:S(2)}, u32[]{:S(2)}) collective-permute-start(bf16[128,896]{1,0:T(8,128)(2,1)S(1)} %collective-permute-done.12.refs_2_), channel_id=1, source_target_pairs={{0,8},{8,16},{16,24},{24,0},{1,9},{9,17},{17,25},{25,1},{2,10},{10... | collective-permute-start | bytes 688136 | tf_op jit(solution)/shard_map/ppermute | solution.py:173
  174.9 11.0 %collective-permute-start.24 = (bf16[128,1024]{1,0:T(8,128)(2,1)S(1)}, bf16[128,1024]{1,0:T(8,128)(2,1)S(1)}, u32[]{:S(2)}, u32[]{:S(2)}) collective-permute-start(bf16[128,1024]{1,0:T(8,128)(2,1)S(1)} %convolution_convert_fusion.3), channel_id=1, source_target_pairs={{0,8},{8,16},{16,24},{24,0},{1,9},{9,17},{17,25},{25,1},{2,10},{10... | collective-permute-start | bytes 786440 | tf_op jit(solution)/shard_map/ppermute | solution.py:173
  175.7 15.8 %collective-permute-start.27 = (bf16[128,1024]{1,0:T(8,128)(2,1)S(1)}, bf16[128,1024]{1,0:T(8,128)(2,1)S(1)}, u32[]{:S(2)}, u32[]{:S(2)}) collective-permute-start(bf16[128,1024]{1,0:T(8,128)(2,1)S(1)} %convolution_convert_fusion.2), channel_id=1, source_target_pairs={{0,8},{8,16},{16,24},{24,0},{1,9},{9,17},{17,25},{25,1},{2,10},{10... | collective-permute-start | bytes 786440 | tf_op jit(solution)/shard_map/ppermute | solution.py:173
  186.6 10.8 %collective-permute-start.25 = (bf16[128,1024]{1,0:T(8,128)(2,1)S(1)}, bf16[128,1024]{1,0:T(8,128)(2,1)S(1)}, u32[]{:S(2)}, u32[]{:S(2)}) collective-permute-start(bf16[128,1024]{1,0:T(8,128)(2,1)S(1)} %fusion.29), channel_id=1, source_target_pairs={{0,8},{8,16},{16,24},{24,0},{1,9},{9,17},{17,25},{25,1},{2,10},{10... | collective-permute-start | bytes 786440 | tf_op jit(solution)/shard_map/ppermute | solution.py:173
  192.3 11.1 %collective-permute-start.28 = (bf16[128,1024]{1,0:T(8,128)(2,1)S(1)}, bf16[128,1024]{1,0:T(8,128)(2,1)S(1)}, u32[]{:S(2)}, u32[]{:S(2)}) collective-permute-start(bf16[128,1024]{1,0:T(8,128)(2,1)S(1)} %fusion.31), channel_id=1, source_target_pairs={{0,8},{8,16},{16,24},{24,0},{1,9},{9,17},{17,25},{25,1},{2,10},{10... | collective-permute-start | bytes 786440 | tf_op jit(solution)/shard_map/ppermute | solution.py:173
  198.1 10.7 %collective-permute-start.26 = (bf16[128,1024]{1,0:T(8,128)(2,1)S(1)}, bf16[128,1024]{1,0:T(8,128)(2,1)S(1)}, u32[]{:S(2)}, u32[]{:S(2)}) collective-permute-start(bf16[128,1024]{1,0:T(8,128)(2,1)S(1)} %fusion.28), channel_id=1, source_target_pairs={{0,8},{8,16},{16,24},{24,0},{1,9},{9,17},{17,25},{25,1},{2,10},{10... | collective-permute-start | bytes 786440 | tf_op jit(solution)/shard_map/ppermute | solution.py:173
  214.9 14.9 %collective-permute-start.30 = (bf16[128,1024]{1,0:T(8,128)(2,1)S(1)}, bf16[128,1024]{1,0:T(8,128)(2,1)S(1)}, u32[]{:S(2)}, u32[]{:S(2)}) collective-permute-start(bf16[128,1024]{1,0:T(8,128)(2,1)S(1)} %get-tuple-element.79.refs_8_), channel_id=1, source_target_pairs={{0,8},{8,16},{16,24},{24,0},{1,9},{9,17},{17,25},{25,1},{2,10},{10... | collective-permute-start | bytes 786440 | tf_op jit(solution)/shard_map/ppermute | solution.py:173
  216.4 11.8 %collective-permute-start.31 = (bf16[128,1024]{1,0:T(8,128)(2,1)S(1)}, bf16[128,1024]{1,0:T(8,128)(2,1)S(1)}, u32[]{:S(2)}, u32[]{:S(2)}) collective-permute-start(bf16[128,1024]{1,0:T(8,128)(2,1)S(1)} %get-tuple-element.80.refs_9_), channel_id=1, source_target_pairs={{0,8},{8,16},{16,24},{24,0},{1,9},{9,17},{17,25},{25,1},{2,10},{10... | collective-permute-start | bytes 786440 | tf_op jit(solution)/shard_map/ppermute | solution.py:173
  228.2 11.0 %collective-permute-start.33 = (bf16[128,1024]{1,0:T(8,128)(2,1)S(1)}, bf16[128,1024]{1,0:T(8,128)(2,1)S(1)}, u32[]{:S(2)}, u32[]{:S(2)}) collective-permute-start(bf16[128,1024]{1,0:T(8,128)(2,1)S(1)} %collective-permute-done.31.refs_11_), channel_id=1, source_target_pairs={{0,8},{8,16},{16,24},{24,0},{1,9},{9,17},{17,25},{25,1},{2,10},{10... | collective-permute-start | bytes 786440 | tf_op jit(solution)/shard_map/ppermute | solution.py:173
  229.7 15.0 %collective-permute-start.32 = (bf16[128,1024]{1,0:T(8,128)(2,1)S(1)}, bf16[128,1024]{1,0:T(8,128)(2,1)S(1)}, u32[]{:S(2)}, u32[]{:S(2)}) collective-permute-start(bf16[128,1024]{1,0:T(8,128)(2,1)S(1)} %collective-permute-done.30.refs_10_), channel_id=1, source_target_pairs={{0,8},{8,16},{16,24},{24,0},{1,9},{9,17},{17,25},{25,1},{2,10},{10... | collective-permute-start | bytes 786440 | tf_op jit(solution)/shard_map/ppermute | solution.py:173
  258.1 11.0 %collective-permute-start.37 = (bf16[128,2048]{1,0:T(8,128)(2,1)S(1)}, bf16[128,2048]{1,0:T(8,128)(2,1)S(1)}, u32[]{:S(2)}, u32[]{:S(2)}) collective-permute-start(bf16[128,2048]{1,0:T(8,128)(2,1)S(1)} %slice.399.refs_16_), channel_id=1, source_target_pairs={{0,4},{1,3},{2,6},{3,1},{4,0},{5,7},{6,2},{7,5},{8,12},{9,11},{10,... | collective-permute-start | bytes 1572872 | tf_op jit(solution)/shard_map/ppermute | solution.py:130
  297.2 14.3 %collective-permute-start.42 = (bf16[128,896]{1,0:T(8,128)(2,1)S(1)}, bf16[128,896]{1,0:T(8,128)(2,1)S(1)}, u32[]{:S(2)}, u32[]{:S(2)}) collective-permute-start(bf16[128,896]{1,0:T(8,128)(2,1)S(1)} %convolution_convert_fusion.5), channel_id=1, source_target_pairs={{0,8},{8,16},{16,24},{24,0},{1,9},{9,17},{17,25},{25,1},{2,10},{10... | collective-permute-start | bytes 688136 | tf_op jit(solution)/shard_map/ppermute | solution.py:173
  333.7 25.1 %collective-permute-start.51 = (bf16[128,1792]{1,0:T(8,128)(2,1)S(1)}, bf16[128,1792]{1,0:T(8,128)(2,1)S(1)}, u32[]{:S(2)}, u32[]{:S(2)}) collective-permute-start(bf16[128,1792]{1,0:T(8,128)(2,1)S(1)} %get-tuple-element.53.refs_8_), channel_id=1, source_target_pairs={{0,8},{8,16},{16,24},{24,0},{1,9},{9,17},{17,25},{25,1},{2,10},{10... | collective-permute-start | bytes 1376264 | tf_op jit(solution)/shard_map/ppermute | solution.py:173
  336.3 20.0 %collective-permute-start.48 = (bf16[128,1792]{1,0:T(8,128)(2,1)S(1)}, bf16[128,1792]{1,0:T(8,128)(2,1)S(1)}, u32[]{:S(2)}, u32[]{:S(2)}) collective-permute-start(bf16[128,1792]{1,0:T(8,128)(2,1)S(1)} %get-tuple-element.54.refs_8_), channel_id=1, source_target_pairs={{0,8},{8,16},{16,24},{24,0},{1,9},{9,17},{17,25},{25,1},{2,10},{10... | collective-permute-start | bytes 1376264 | tf_op jit(solution)/shard_map/ppermute | solution.py:173
  356.3 15.3 %collective-permute-start.49 = (bf16[128,1792]{1,0:T(8,128)(2,1)S(1)}, bf16[128,1792]{1,0:T(8,128)(2,1)S(1)}, u32[]{:S(2)}, u32[]{:S(2)}) collective-permute-start(bf16[128,1792]{1,0:T(8,128)(2,1)S(1)} %collective-permute-done.48.refs_9_), channel_id=1, source_target_pairs={{0,8},{8,16},{16,24},{24,0},{1,9},{9,17},{17,25},{25,1},{2,10},{10... | collective-permute-start | bytes 1376264 | tf_op jit(solution)/shard_map/ppermute | solution.py:173
  358.8 22.6 %collective-permute-start.52 = (bf16[128,1792]{1,0:T(8,128)(2,1)S(1)}, bf16[128,1792]{1,0:T(8,128)(2,1)S(1)}, u32[]{:S(2)}, u32[]{:S(2)}) collective-permute-start(bf16[128,1792]{1,0:T(8,128)(2,1)S(1)} %collective-permute-done.51.refs_9_), channel_id=1, source_target_pairs={{0,8},{8,16},{16,24},{24,0},{1,9},{9,17},{17,25},{25,1},{2,10},{10... | collective-permute-start | bytes 1376264 | tf_op jit(solution)/shard_map/ppermute | solution.py:173
  371.6 19.7 %collective-permute-start.50 = (bf16[128,1792]{1,0:T(8,128)(2,1)S(1)}, bf16[128,1792]{1,0:T(8,128)(2,1)S(1)}, u32[]{:S(2)}, u32[]{:S(2)}) collective-permute-start(bf16[128,1792]{1,0:T(8,128)(2,1)S(1)} %collective-permute-done.49.refs_10_), channel_id=1, source_target_pairs={{0,8},{8,16},{16,24},{24,0},{1,9},{9,17},{17,25},{25,1},{2,10},{10... | collective-permute-start | bytes 1376264 | tf_op jit(solution)/shard_map/ppermute | solution.py:173
  381.4 16.2 %collective-permute-start.53 = (bf16[128,1792]{1,0:T(8,128)(2,1)S(1)}, bf16[128,1792]{1,0:T(8,128)(2,1)S(1)}, u32[]{:S(2)}, u32[]{:S(2)}) collective-permute-start(bf16[128,1792]{1,0:T(8,128)(2,1)S(1)} %collective-permute-done.52.refs_10_), channel_id=1, source_target_pairs={{0,8},{8,16},{16,24},{24,0},{1,9},{9,17},{17,25},{25,1},{2,10},{10... | collective-permute-start | bytes 1376264 | tf_op jit(solution)/shard_map/ppermute | solution.py:173
  411.3 11.1 %collective-permute-start.55 = (bf16[128,2048]{1,0:T(8,128)(2,1)S(1)}, bf16[128,2048]{1,0:T(8,128)(2,1)S(1)}, u32[]{:S(2)}, u32[]{:S(2)}) collective-permute-start(bf16[128,2048]{1,0:T(8,128)(2,1)S(1)} %slice.398.refs_12_), channel_id=1, source_target_pairs={{0,4},{1,3},{2,6},{3,1},{4,0},{5,7},{6,2},{7,5},{8,12},{9,11},{10,... | collective-permute-start | bytes 1572872 | tf_op jit(solution)/shard_map/ppermute | solution.py:130
  422.7 10.9 %collective-permute-start.56 = (bf16[64,2048]{1,0:T(8,128)(2,1)S(1)}, bf16[64,2048]{1,0:T(8,128)(2,1)S(1)}, u32[]{:S(2)}, u32[]{:S(2)}) collective-permute-start(bf16[64,2048]{1,0:T(8,128)(2,1)S(1)} %slice.401.refs_12_), channel_id=1, source_target_pairs={{0,2},{1,5},{2,0},{3,7},{4,6},{5,1},{6,4},{7,3},{8,10},{9,13},{10,... | collective-permute-start | bytes 786440 | tf_op jit(solution)/shard_map/ppermute | solution.py:130
  (74 other events, 726.9 us)

commit v3 on v2

--- a/solution.py
+++ b/solution.py
@@ -110,13 +110,16 @@
             self.perms.append([(c, c ^ (odd if c & 1 else even)) for c in range(size)])
         self.swap = [(c, c ^ 1) for c in range(size)]
 
-    def gather(self, block):
+    def partner(self, block):
+        return lax.ppermute(block, PLANE, self.perms[0])
+
+    def gather(self, block, paired=False):
         own = block
-        for perm in self.perms:
+        for perm in self.perms[1:] if paired else self.perms:
             own = jnp.concatenate([own, lax.ppermute(own, PLANE, perm)], axis=0)
         return own, lax.ppermute(own, PLANE, self.swap)
 
-    def scatter(self, full, beside=()):
+    def scatter(self, full, beside=(), paired=False):
         b = full.shape[0] // self.size
         block = lambda i: full[i * b : (i + 1) * b]
         half = self.size // 2
@@ -125,6 +128,12 @@
         got = lax.ppermute(send, PLANE, self.swap)
         acc = mine.astype(F32) + got.astype(F32)
         for i, perm in enumerate(reversed(self.perms)):
+            if paired and i == len(self.perms) - 1:
+                sent = acc.astype(full.dtype)
+                got = lax.ppermute(sent, PLANE, perm)
+                middle = acc.shape[0] // 2
+                got = jnp.concatenate([got[middle:], got[:middle]], axis=0)
+                return sent.astype(F32) + got.astype(F32)
             half = acc.shape[0] // 2
             kept, sent = acc[:half], acc[half:].astype(full.dtype)
             got = lax.ppermute(sent, PLANE, perm)
@@ -239,7 +248,8 @@
         )
         target = rows.own_order(target).astype(F32)
         keep = rows.own_order(loss_mask.astype(F32))
-        inv = after(inv, target)
+        x_other = plane.partner(after(x, moved))
+        inv = after(after(inv, target), x_other)
         gate, up = gate * inv, up * inv
         sigma = jax.nn.sigmoid(gate)
         activated = gate * sigma
@@ -249,8 +259,9 @@
             [hidden[:, lo:hi] for lo, hi in cuts],
             lambda bs: sum(mm(b, down_w[lo:hi]) for b, (lo, hi) in zip(bs, cuts)).astype(BF16),
         )
-        residual = (x.astype(F32) + plane.scatter(ffn)).astype(BF16)
-        residuals = rows.parts(*plane.gather(residual))
+        x_pair = jnp.concatenate([x, x_other], axis=0)
+        residual = (x_pair.astype(F32) + plane.scatter(ffn, paired=True)).astype(BF16)
+        residuals = rows.parts(*plane.gather(residual, paired=True))
 
         ecuts = halves(proj_w.shape[1])
         predicted, _ = rows.reduce(
@@ -272,8 +283,9 @@
         resid_grad = plane.scatter(
             back,
             [lambda kept, sent: grad("proj", lines(residuals), pred_grads, kept, sent)],
+            paired=True,
         ).astype(BF16)
-        resid_grads = rows.parts(*plane.gather(resid_grad))
+        resid_grads = rows.parts(*plane.gather(resid_grad, paired=True))
 
         hid_grad, _ = rows.reduce(
             resid_grads,
@@ -312,7 +324,7 @@
 
         inv_own = inv_all[:block]
         grad_input = (
-            resid_grad.astype(F32)
+            resid_grad[:block].astype(F32)
             + gain[None, :] * normed_grad
             - x.astype(F32) * (inv_own * inv_own * inner / features)[:, None]
         )

time: 453 us -> 449 us (level)
  waiting for transfers between devices: 242 us -> 237 us
    ppermute x6 -> x4, waiting for transfers between devices: 37.8 us -> 27.8 us  [gather(): own = jnp.concatenate([own, lax.ppermute(own, PLANE, perm)], axis=0)]
    ppermute x6, waiting for transfers between devices: 17.8 us -> 24.5 us  [scatter(): got = lax.ppermute(sent, PLANE, perm)]
    ppermute x6 -> x4, starting transfers between devices: 10.2 us -> 7.27 us  [gather(): own = jnp.concatenate([own, lax.ppermute(own, PLANE, perm)], axis=0)]
  transfers between devices with their start and end apart: 65 -> 64, of which waited for: 49 -> 46; matrix products, arithmetic and copies ran while one was open for 17% -> 17% of each run, Pallas kernels for 9% -> 9%
where the time goes in v3:
time: 449 us; the launch traced here: 441 us
  waiting for transfers between devices  237 us (53%)
  matrix products  78.4 us (17%)
  starting transfers between devices  50.2 us (11%)
  Pallas kernels  37.9 us (8%)
  between operations  15.6 us (3%)
  other arithmetic  11.3 us (3%)
  local copies, waits for them, and re-layouts  10.4 us (2%)
    ppermute x36, waiting for transfers between devices, shift(): return lax.ppermute(value, 'row', self.ring)  171 us
    dot_general x24, matrix products, mm_t(): lax.dot_general(left, right, (((1,), (1,)), ((), ())), preferred_element_...  42.3 us
    pallas_call x4, Pallas kernels, weight_grad(): pl.pallas_call(functools.partial(grad_kernel, places, len(operands), tile...  37.9 us
    dot_general x24, matrix products, mm(): return jnp.dot(left, right, preferred_element_type=F32)  36.2 us
    ppermute x4, waiting for transfers between devices, gather(): own = jnp.concatenate([own, lax.ppermute(own, PLANE, perm)], axis=0)  27.8 us
    ppermute x6, waiting for transfers between devices, scatter(): got = lax.ppermute(sent, PLANE, perm)  24.5 us
    ppermute x36, starting transfers between devices, shift(): return lax.ppermute(value, 'row', self.ring)  16.8 us
  transfers between devices with their start and end apart: 64, of which 46 were waited for; matrix products, arithmetic and copies ran while one was open for 17% of the time, Pallas kernels for 9%

profile of v3, /device:TPU:0, one launch (start us, length us, event | category | flops | bytes accessed | tf_op | source)
XLA Modules:
  0.0 440.7 jit_solution(241698618271600945)
XLA Ops:
  4.6 4.4 collective-permute-done
  11.2 7.2 %collective-permute-done.1 = bf16[128,2048]{1,0:T(8,128)(2,1)S(1)} collective-permute-done((bf16[128,2048]{1,0:T(8,128)(2,1)S(1)}, bf16[128,2048]{1,0:T(8,128)(2,1)S(1)}, u32[]{:S(2)}, u32[]{:S(2)}) %collective-permute-start.1) | collective-permute-done | bytes 524320 | tf_op jit(solution)/shard_map/ppermute | solution.py:119
  26.2 4.4 convolution_convert_fusion.1
  37.0 9.2 %collective-permute-done.3 = bf16[128,1792]{1,0:T(8,128)(2,1)S(1)} collective-permute-done((bf16[128,1792]{1,0:T(8,128)(2,1)S(1)}, bf16[128,1792]{1,0:T(8,128)(2,1)S(1)}, u32[]{:S(2)}, u32[]{:S(2)}) %collective-permute-start.3) | collective-permute-done | bytes 458784 | tf_op jit(solution)/shard_map/ppermute | solution.py:182
  61.4 4.3 fusion.9
  80.8 4.4 fusion.8
  85.6 5.6 %collective-permute-done.6 = bf16[128,1792]{1,0:T(8,128)(2,1)} collective-permute-done((bf16[128,1792]{1,0:T(8,128)(2,1)}, bf16[128,1792]{1,0:T(8,128)(2,1)}, u32[]{:S(2)}, u32[]{:S(2)}) %collective-permute-start.6) | collective-permute-done | bytes 458784 | tf_op jit(solution)/shard_map/ppermute | solution.py:182
  93.6 6.9 %collective-permute-done.12 = bf16[128,1792]{1,0:T(8,128)(2,1)S(1)} collective-permute-done((bf16[128,1792]{1,0:T(8,128)(2,1)S(1)}, bf16[128,1792]{1,0:T(8,128)(2,1)S(1)}, u32[]{:S(2)}, u32[]{:S(2)}) %collective-permute-start.12) | collective-permute-done | bytes 458784 | tf_op jit(solution)/shard_map/ppermute | solution.py:182
  104.8 11.1 %collective-permute-done.14.refs_3_ = bf16[128,896]{1,0:T(8,128)(2,1)S(1)} collective-permute-done((bf16[128,896]{1,0:T(8,128)(2,1)S(1)}, bf16[128,896]{1,0:T(8,128)(2,1)S(1)}, u32[]{:S(2)}, u32[]{:S(2)}) %collective-permute-start.14) | collective-permute-done | bytes 229408 | tf_op jit(solution)/shard_map/ppermute | solution.py:182
  117.5 8.8 %collective-permute-done.16.refs_5_ = bf16[128,896]{1,0:T(8,128)(2,1)S(1)} collective-permute-done((bf16[128,896]{1,0:T(8,128)(2,1)S(1)}, bf16[128,896]{1,0:T(8,128)(2,1)S(1)}, u32[]{:S(2)}, u32[]{:S(2)}) %collective-permute-start.16) | collective-permute-done | bytes 229408 | tf_op jit(solution)/shard_map/ppermute | solution.py:182
  132.0 4.4 %collective-permute-done.18.refs_7_ = bf16[128,896]{1,0:T(8,128)(2,1)S(1)} collective-permute-done((bf16[128,896]{1,0:T(8,128)(2,1)S(1)}, bf16[128,896]{1,0:T(8,128)(2,1)S(1)}, u32[]{:S(2)}, u32[]{:S(2)}) %collective-permute-start.18) | collective-permute-done | bytes 229408 | tf_op jit(solution)/shard_map/ppermute | solution.py:182
  143.3 9.2 %collective-permute-done.20 = bf16[128,2048]{1,0:T(8,128)(2,1)S(1)} collective-permute-done((bf16[128,2048]{1,0:T(8,128)(2,1)S(1)}, bf16[128,2048]{1,0:T(8,128)(2,1)S(1)}, u32[]{:S(2)}, u32[]{:S(2)}) %collective-permute-start.20) | collective-permute-done | bytes 524320 | tf_op jit(solution)/shard_map/ppermute | solution.py:139
  154.1 7.7 %collective-permute-done.21 = bf16[128,2048]{1,0:T(8,128)(2,1)S(1)} collective-permute-done((bf16[128,2048]{1,0:T(8,128)(2,1)S(1)}, bf16[128,2048]{1,0:T(8,128)(2,1)S(1)}, u32[]{:S(2)}, u32[]{:S(2)}) %collective-permute-start.21) | collective-permute-done | bytes 524320 | tf_op jit(solution)/shard_map/ppermute | solution.py:133
  162.2 9.2 %collective-permute-done.22 = bf16[128,2048]{1,0:T(8,128)(2,1)S(1)} collective-permute-done((bf16[128,2048]{1,0:T(8,128)(2,1)S(1)}, bf16[128,2048]{1,0:T(8,128)(2,1)S(1)}, u32[]{:S(2)}, u32[]{:S(2)}) %collective-permute-start.22) | collective-permute-done | bytes 524320 | tf_op jit(solution)/shard_map/ppermute | solution.py:119
  175.9 10.1 %collective-permute-done.24 = bf16[128,1024]{1,0:T(8,128)(2,1)S(1)} collective-permute-done((bf16[128,1024]{1,0:T(8,128)(2,1)S(1)}, bf16[128,1024]{1,0:T(8,128)(2,1)S(1)}, u32[]{:S(2)}, u32[]{:S(2)}) %collective-permute-start.24) | collective-permute-done | bytes 262176 | tf_op jit(solution)/shard_map/ppermute | solution.py:182
  186.9 4.8 %collective-permute-done.27 = bf16[128,1024]{1,0:T(8,128)(2,1)S(1)} collective-permute-done((bf16[128,1024]{1,0:T(8,128)(2,1)S(1)}, bf16[128,1024]{1,0:T(8,128)(2,1)S(1)}, u32[]{:S(2)}, u32[]{:S(2)}) %collective-permute-start.27) | collective-permute-done | bytes 262176 | tf_op jit(solution)/shard_map/ppermute | solution.py:182
  192.5 5.1 %collective-permute-done.25 = bf16[128,1024]{1,0:T(8,128)(2,1)S(1)} collective-permute-done((bf16[128,1024]{1,0:T(8,128)(2,1)S(1)}, bf16[128,1024]{1,0:T(8,128)(2,1)S(1)}, u32[]{:S(2)}, u32[]{:S(2)}) %collective-permute-start.25) | collective-permute-done | bytes 262176 | tf_op jit(solution)/shard_map/ppermute | solution.py:182
  198.8 4.6 %collective-permute-done.28 = bf16[128,1024]{1,0:T(8,128)(2,1)S(1)} collective-permute-done((bf16[128,1024]{1,0:T(8,128)(2,1)S(1)}, bf16[128,1024]{1,0:T(8,128)(2,1)S(1)}, u32[]{:S(2)}, u32[]{:S(2)}) %collective-permute-start.28) | collective-permute-done | bytes 262176 | tf_op jit(solution)/shard_map/ppermute | solution.py:182
  204.2 5.2 %collective-permute-done.26 = bf16[128,1024]{1,0:T(8,128)(2,1)S(1)} collective-permute-done((bf16[128,1024]{1,0:T(8,128)(2,1)S(1)}, bf16[128,1024]{1,0:T(8,128)(2,1)S(1)}, u32[]{:S(2)}, u32[]{:S(2)}) %collective-permute-start.26) | collective-permute-done | bytes 262176 | tf_op jit(solution)/shard_map/ppermute | solution.py:182
  218.3 10.5 %collective-permute-done.31.refs_11_ = bf16[128,1024]{1,0:T(8,128)(2,1)S(1)} collective-permute-done((bf16[128,1024]{1,0:T(8,128)(2,1)S(1)}, bf16[128,1024]{1,0:T(8,128)(2,1)S(1)}, u32[]{:S(2)}, u32[]{:S(2)}) %collective-permute-start.31) | collective-permute-done | bytes 262176 | tf_op jit(solution)/shard_map/ppermute | solution.py:182
  232.0 7.9 %collective-permute-done.33.refs_13_ = bf16[128,1024]{1,0:T(8,128)(2,1)S(1)} collective-permute-done((bf16[128,1024]{1,0:T(8,128)(2,1)S(1)}, bf16[128,1024]{1,0:T(8,128)(2,1)S(1)}, u32[]{:S(2)}, u32[]{:S(2)}) %collective-permute-start.33) | collective-permute-done | bytes 262176 | tf_op jit(solution)/shard_map/ppermute | solution.py:182
  259.1 9.5 %shard_map.171 = (f32[2048,2048]{1,0:T(8,128)}, f32[128,2048]{1,0:T(8,128)S(1)}) custom-call(bf16[64,2048]{1,0:T(8,128)(2,1)S(1)} %get-tuple-element.68.refs_0_, bf16[64,2048]{1,0:T(8,128)(2,1)S(1)} %get-tuple-element.66.refs_1_, bf16[64,2048]{1,0:T(8,128)(2,1)S(1)} %get-tuple-element.69.refs_2_, ...), custom_call_target="tpu_custom_call", output_to_operand_aliasing={{1}: (17, {})} | custom-call | flops 4294967296 | bytes 20971520 | tf_op jit(solution)/shard_map/pallas_call | solution.py:60
  270.3 7.6 %collective-permute-done.38 = bf16[128,2048]{1,0:T(8,128)(2,1)S(1)} collective-permute-done((bf16[128,2048]{1,0:T(8,128)(2,1)S(1)}, bf16[128,2048]{1,0:T(8,128)(2,1)S(1)}, u32[]{:S(2)}, u32[]{:S(2)}) %collective-permute-start.38) | collective-permute-done | bytes 524320 | tf_op jit(solution)/shard_map/ppermute | solution.py:133
  280.2 7.2 %collective-permute-done.39 = bf16[128,2048]{1,0:T(8,128)(2,1)S(1)} collective-permute-done((bf16[128,2048]{1,0:T(8,128)(2,1)S(1)}, bf16[128,2048]{1,0:T(8,128)(2,1)S(1)}, u32[]{:S(2)}, u32[]{:S(2)}) %collective-permute-start.39) | collective-permute-done | bytes 524320 | tf_op jit(solution)/shard_map/ppermute | solution.py:119
  294.3 8.8 %shard_map.172 = (f32[1792,2048]{1,0:T(8,128)}, f32[128,896]{1,0:T(8,128)S(1)}) custom-call(bf16[128,896]{1,0:T(8,128)(2,1)S(1)} %get-tuple-element.88.refs_0_, bf16[128,896]{1,0:T(8,128)(2,1)S(1)} %get-tuple-element.87.refs_1_, bf16[128,896]{1,0:T(8,128)(2,1)S(1)} %collective-permute-done.13.refs_2_, ...), custom_call_target="tpu_custom_call", output_to_operand_aliasing={{1}: (17, {})} | custom-call | flops 3758096384 | bytes 18612224 | tf_op jit(solution)/shard_map/pallas_call | solution.py:60
  337.2 14.5 %collective-permute-done.47.refs_9_ = bf16[128,1792]{1,0:T(8,128)(2,1)S(1)} collective-permute-done((bf16[128,1792]{1,0:T(8,128)(2,1)S(1)}, bf16[128,1792]{1,0:T(8,128)(2,1)S(1)}, u32[]{:S(2)}, u32[]{:S(2)}) %collective-permute-start.47) | collective-permute-done | bytes 458784 | tf_op jit(solution)/shard_map/ppermute | solution.py:182
  357.9 9.1 %collective-permute-done.48.refs_10_ = bf16[128,1792]{1,0:T(8,128)(2,1)S(1)} collective-permute-done((bf16[128,1792]{1,0:T(8,128)(2,1)S(1)}, bf16[128,1792]{1,0:T(8,128)(2,1)S(1)}, u32[]{:S(2)}, u32[]{:S(2)}) %collective-permute-start.48) | collective-permute-done | bytes 458784 | tf_op jit(solution)/shard_map/ppermute | solution.py:182
  369.4 7.4 %collective-permute-done.51.refs_10_ = bf16[128,1792]{1,0:T(8,128)(2,1)S(1)} collective-permute-done((bf16[128,1792]{1,0:T(8,128)(2,1)S(1)}, bf16[128,1792]{1,0:T(8,128)(2,1)S(1)}, u32[]{:S(2)}, u32[]{:S(2)}) %collective-permute-start.51) | collective-permute-done | bytes 458784 | tf_op jit(solution)/shard_map/ppermute | solution.py:182
  379.6 7.0 %collective-permute-done.49.refs_11_ = bf16[128,1792]{1,0:T(8,128)(2,1)S(1)} collective-permute-done((bf16[128,1792]{1,0:T(8,128)(2,1)S(1)}, bf16[128,1792]{1,0:T(8,128)(2,1)S(1)}, u32[]{:S(2)}, u32[]{:S(2)}) %collective-permute-start.49) | collective-permute-done | bytes 458784 | tf_op jit(solution)/shard_map/ppermute | solution.py:182
  408.7 9.8 %shard_map.173 = (f32[2048,1792]{1,0:T(8,128)}, f32[128,2048]{1,0:T(8,128)S(1)}) custom-call(bf16[64,2048]{1,0:T(8,128)(2,1)S(1)} %get-tuple-element.71.refs_0_, bf16[64,2048]{1,0:T(8,128)(2,1)S(1)} %get-tuple-element.75.refs_1_, bf16[64,2048]{1,0:T(8,128)(2,1)S(1)} %get-tuple-element.74.refs_2_, ...), custom_call_target="tpu_custom_call", output_to_operand_aliasing={{1}: (13, {})} | custom-call | flops 3758096384 | bytes 18612224 | tf_op jit(solution)/shard_map/pallas_call | solution.py:60
  420.3 9.8 %shard_map.174 = (f32[2048,1792]{1,0:T(8,128)}, f32[64,2048]{1,0:T(8,128)S(1)}) custom-call(bf16[64,2048]{1,0:T(8,128)(2,1)S(1)} %get-tuple-element.71.refs_0_, bf16[64,2048]{1,0:T(8,128)(2,1)S(1)} %get-tuple-element.75.refs_1_, bf16[64,2048]{1,0:T(8,128)(2,1)S(1)} %get-tuple-element.74.refs_2_, ...), custom_call_target="tpu_custom_call", output_to_operand_aliasing={{1}: (13, {})} | custom-call | flops 3758096384 | bytes 18612224 | tf_op jit(solution)/shard_map/pallas_call | solution.py:60
  430.5 4.3 collective-permute-start.60
  (314 shorter events, 185.2 us)
Async XLA Ops:
  30.7 15.5 %collective-permute-start.3 = (bf16[128,1792]{1,0:T(8,128)(2,1)S(1)}, bf16[128,1792]{1,0:T(8,128)(2,1)S(1)}, u32[]{:S(2)}, u32[]{:S(2)}) collective-permute-start(bf16[128,1792]{1,0:T(8,128)(2,1)S(1)} %convolution_convert_fusion.1), channel_id=1, source_target_pairs={{0,8},{8,16},{16,24},{24,0},{1,9},{9,17},{17,25},{25,1},{2,10},{10... | collective-permute-start | bytes 1376264 | tf_op jit(solution)/shard_map/ppermute | solution.py:182
  34.8 24.5 %collective-permute-start.10 = (bf16[128,1792]{1,0:T(8,128)(2,1)}, bf16[128,1792]{1,0:T(8,128)(2,1)}, u32[]{:S(2)}, u32[]{:S(2)}) collective-permute-start(bf16[128,1792]{1,0:T(8,128)(2,1)} %convolution_convert_fusion), channel_id=1, source_target_pairs={{0,8},{8,16},{16,24},{24,0},{1,9},{9,17},{17,25},{25,1},{2,10},{10... | collective-permute-start | bytes 1376264 | tf_op jit(solution)/shard_map/ppermute | solution.py:182
  48.0 17.6 %collective-permute-start.9 = (f32[512]{0:T(512)S(1)}, f32[512]{0:T(512)S(1)}, u32[]{:S(2)}, u32[]{:S(2)}) collective-permute-start(f32[512]{0:T(512)S(1)} %maximum_select_fusion.1), channel_id=1, source_target_pairs={{0,24},{8,16},{16,8},{24,0},{1,25},{9,17},{17,9},{25,1},{2,26},{10... | collective-permute-start | bytes 6152 | tf_op jit(solution)/shard_map/ppermute | solution.py:215
  50.0 16.6 %collective-permute-start.8 = (f32[512]{0:T(512)S(1)}, f32[512]{0:T(512)S(1)}, u32[]{:S(2)}, u32[]{:S(2)}) collective-permute-start(f32[512]{0:T(512)S(1)} %maximum_select_fusion.1), channel_id=1, source_target_pairs={{0,16},{8,24},{16,0},{24,8},{1,17},{9,25},{17,1},{25,9},{2,18},{10... | collective-permute-start | bytes 6152 | tf_op jit(solution)/shard_map/ppermute | solution.py:215
  50.0 16.6 %collective-permute-start.7 = (f32[512]{0:T(512)S(1)}, f32[512]{0:T(512)S(1)}, u32[]{:S(2)}, u32[]{:S(2)}) collective-permute-start(f32[512]{0:T(512)S(1)} %maximum_select_fusion.1), channel_id=1, source_target_pairs={{0,8},{8,0},{16,24},{24,16},{1,9},{9,1},{17,25},{25,17},{2,10},{10... | collective-permute-start | bytes 6152 | tf_op jit(solution)/shard_map/ppermute | solution.py:215
  54.5 18.3 %collective-permute-start.5 = (bf16[128,1792]{1,0:T(8,128)(2,1)}, bf16[128,1792]{1,0:T(8,128)(2,1)}, u32[]{:S(2)}, u32[]{:S(2)}) collective-permute-start(bf16[128,1792]{1,0:T(8,128)(2,1)} %fusion.7), channel_id=1, source_target_pairs={{0,8},{8,16},{16,24},{24,0},{1,9},{9,17},{17,25},{25,1},{2,10},{10... | collective-permute-start | bytes 1376264 | tf_op jit(solution)/shard_map/ppermute | solution.py:182
  55.4 21.3 %all-to-all-start = ((bf16[16,8,2048]{2,0,1:T(8,128)(2,1)}), bf16[16,8,2048]{2,0,1:T(8,128)(2,1)S(1)}, u32[]{:S(2)}, u32[]{:S(2)}) async-start(bf16[16,8,2048]{2,0,1:T(8,128)(2,1)} %bitcast.57), calls=%async_computation | async-start | bytes 1048576 | tf_op jit(solution)/shard_map/all_to_all | solution.py:246
  59.3 11.6 %collective-permute-start.4 = (bf16[64,2048]{1,0:T(8,128)(2,1)S(1)}, bf16[64,2048]{1,0:T(8,128)(2,1)S(1)}, u32[]{:S(2)}, u32[]{:S(2)}) collective-permute-start(bf16[64,2048]{1,0:T(8,128)(2,1)S(1)} %broadcast_select_fusion.1), channel_id=1, source_target_pairs={{0,2},{1,5},{2,0},{3,7},{4,6},{5,1},{6,4},{7,3},{8,10},{9,13},{10,... | collective-permute-start | bytes 786440 | tf_op jit(solution)/shard_map/ppermute | solution.py:114
  65.7 15.1 %collective-permute-start.11 = (bf16[128,1792]{1,0:T(8,128)(2,1)S(1)}, bf16[128,1792]{1,0:T(8,128)(2,1)}, u32[]{:S(2)}, u32[]{:S(2)}) collective-permute-start(bf16[128,1792]{1,0:T(8,128)(2,1)S(1)} %fusion.9), channel_id=1, source_target_pairs={{0,8},{8,16},{16,24},{24,0},{1,9},{9,17},{17,25},{25,1},{2,10},{10... | collective-permute-start | bytes 1376264 | tf_op jit(solution)/shard_map/ppermute | solution.py:182
  75.8 15.4 %collective-permute-start.6 = (bf16[128,1792]{1,0:T(8,128)(2,1)}, bf16[128,1792]{1,0:T(8,128)(2,1)}, u32[]{:S(2)}, u32[]{:S(2)}) collective-permute-start(bf16[128,1792]{1,0:T(8,128)(2,1)} %fusion.6), channel_id=1, source_target_pairs={{0,8},{8,16},{16,24},{24,0},{1,9},{9,17},{17,25},{25,1},{2,10},{10... | collective-permute-start | bytes 1376264 | tf_op jit(solution)/shard_map/ppermute | solution.py:182
  85.2 15.3 %collective-permute-start.12 = (bf16[128,1792]{1,0:T(8,128)(2,1)S(1)}, bf16[128,1792]{1,0:T(8,128)(2,1)S(1)}, u32[]{:S(2)}, u32[]{:S(2)}) collective-permute-start(bf16[128,1792]{1,0:T(8,128)(2,1)S(1)} %fusion.8), channel_id=1, source_target_pairs={{0,8},{8,16},{16,24},{24,0},{1,9},{9,17},{17,25},{25,1},{2,10},{10... | collective-permute-start | bytes 1376264 | tf_op jit(solution)/shard_map/ppermute | solution.py:182
  102.0 14.7 %collective-permute-start.13 = (bf16[128,896]{1,0:T(8,128)(2,1)S(1)}, bf16[128,896]{1,0:T(8,128)(2,1)S(1)}, u32[]{:S(2)}, u32[]{:S(2)}) collective-permute-start(bf16[128,896]{1,0:T(8,128)(2,1)S(1)} %get-tuple-element.88.refs_0_), channel_id=1, source_target_pairs={{0,8},{8,16},{16,24},{24,0},{1,9},{9,17},{17,25},{25,1},{2,10},{10... | collective-permute-start | bytes 688136 | tf_op jit(solution)/shard_map/ppermute | solution.py:182
  102.0 13.9 %collective-permute-start.14 = (bf16[128,896]{1,0:T(8,128)(2,1)S(1)}, bf16[128,896]{1,0:T(8,128)(2,1)S(1)}, u32[]{:S(2)}, u32[]{:S(2)}) collective-permute-start(bf16[128,896]{1,0:T(8,128)(2,1)S(1)} %get-tuple-element.87.refs_1_), channel_id=1, source_target_pairs={{0,8},{8,16},{16,24},{24,0},{1,9},{9,17},{17,25},{25,1},{2,10},{10... | collective-permute-start | bytes 688136 | tf_op jit(solution)/shard_map/ppermute | solution.py:182
  116.7 14.5 %collective-permute-start.15 = (bf16[128,896]{1,0:T(8,128)(2,1)S(1)}, bf16[128,896]{1,0:T(8,128)(2,1)S(1)}, u32[]{:S(2)}, u32[]{:S(2)}) collective-permute-start(bf16[128,896]{1,0:T(8,128)(2,1)S(1)} %collective-permute-done.13.refs_2_), channel_id=1, source_target_pairs={{0,8},{8,16},{16,24},{24,0},{1,9},{9,17},{17,25},{25,1},{2,10},{10... | collective-permute-start | bytes 688136 | tf_op jit(solution)/shard_map/ppermute | solution.py:182
  175.1 11.0 %collective-permute-start.24 = (bf16[128,1024]{1,0:T(8,128)(2,1)S(1)}, bf16[128,1024]{1,0:T(8,128)(2,1)S(1)}, u32[]{:S(2)}, u32[]{:S(2)}) collective-permute-start(bf16[128,1024]{1,0:T(8,128)(2,1)S(1)} %convolution_convert_fusion.3), channel_id=1, source_target_pairs={{0,8},{8,16},{16,24},{24,0},{1,9},{9,17},{17,25},{25,1},{2,10},{10... | collective-permute-start | bytes 786440 | tf_op jit(solution)/shard_map/ppermute | solution.py:182
  175.9 15.8 %collective-permute-start.27 = (bf16[128,1024]{1,0:T(8,128)(2,1)S(1)}, bf16[128,1024]{1,0:T(8,128)(2,1)S(1)}, u32[]{:S(2)}, u32[]{:S(2)}) collective-permute-start(bf16[128,1024]{1,0:T(8,128)(2,1)S(1)} %convolution_convert_fusion.2), channel_id=1, source_target_pairs={{0,8},{8,16},{16,24},{24,0},{1,9},{9,17},{17,25},{25,1},{2,10},{10... | collective-permute-start | bytes 786440 | tf_op jit(solution)/shard_map/ppermute | solution.py:182
  186.8 10.8 %collective-permute-start.25 = (bf16[128,1024]{1,0:T(8,128)(2,1)S(1)}, bf16[128,1024]{1,0:T(8,128)(2,1)S(1)}, u32[]{:S(2)}, u32[]{:S(2)}) collective-permute-start(bf16[128,1024]{1,0:T(8,128)(2,1)S(1)} %fusion.29), channel_id=1, source_target_pairs={{0,8},{8,16},{16,24},{24,0},{1,9},{9,17},{17,25},{25,1},{2,10},{10... | collective-permute-start | bytes 786440 | tf_op jit(solution)/shard_map/ppermute | solution.py:182
  192.4 11.0 %collective-permute-start.28 = (bf16[128,1024]{1,0:T(8,128)(2,1)S(1)}, bf16[128,1024]{1,0:T(8,128)(2,1)S(1)}, u32[]{:S(2)}, u32[]{:S(2)}) collective-permute-start(bf16[128,1024]{1,0:T(8,128)(2,1)S(1)} %fusion.31), channel_id=1, source_target_pairs={{0,8},{8,16},{16,24},{24,0},{1,9},{9,17},{17,25},{25,1},{2,10},{10... | collective-permute-start | bytes 786440 | tf_op jit(solution)/shard_map/ppermute | solution.py:182
  198.3 11.1 %collective-permute-start.26 = (bf16[128,1024]{1,0:T(8,128)(2,1)S(1)}, bf16[128,1024]{1,0:T(8,128)(2,1)S(1)}, u32[]{:S(2)}, u32[]{:S(2)}) collective-permute-start(bf16[128,1024]{1,0:T(8,128)(2,1)S(1)} %fusion.28), channel_id=1, source_target_pairs={{0,8},{8,16},{16,24},{24,0},{1,9},{9,17},{17,25},{25,1},{2,10},{10... | collective-permute-start | bytes 786440 | tf_op jit(solution)/shard_map/ppermute | solution.py:182
  214.9 15.4 %collective-permute-start.30 = (bf16[128,1024]{1,0:T(8,128)(2,1)S(1)}, bf16[128,1024]{1,0:T(8,128)(2,1)S(1)}, u32[]{:S(2)}, u32[]{:S(2)}) collective-permute-start(bf16[128,1024]{1,0:T(8,128)(2,1)S(1)} %get-tuple-element.79.refs_8_), channel_id=1, source_target_pairs={{0,8},{8,16},{16,24},{24,0},{1,9},{9,17},{17,25},{25,1},{2,10},{10... | collective-permute-start | bytes 786440 | tf_op jit(solution)/shard_map/ppermute | solution.py:182
  216.5 12.4 %collective-permute-start.31 = (bf16[128,1024]{1,0:T(8,128)(2,1)S(1)}, bf16[128,1024]{1,0:T(8,128)(2,1)S(1)}, u32[]{:S(2)}, u32[]{:S(2)}) collective-permute-start(bf16[128,1024]{1,0:T(8,128)(2,1)S(1)} %get-tuple-element.80.refs_9_), channel_id=1, source_target_pairs={{0,8},{8,16},{16,24},{24,0},{1,9},{9,17},{17,25},{25,1},{2,10},{10... | collective-permute-start | bytes 786440 | tf_op jit(solution)/shard_map/ppermute | solution.py:182
  228.8 11.0 %collective-permute-start.33 = (bf16[128,1024]{1,0:T(8,128)(2,1)S(1)}, bf16[128,1024]{1,0:T(8,128)(2,1)S(1)}, u32[]{:S(2)}, u32[]{:S(2)}) collective-permute-start(bf16[128,1024]{1,0:T(8,128)(2,1)S(1)} %collective-permute-done.31.refs_11_), channel_id=1, source_target_pairs={{0,8},{8,16},{16,24},{24,0},{1,9},{9,17},{17,25},{25,1},{2,10},{10... | collective-permute-start | bytes 786440 | tf_op jit(solution)/shard_map/ppermute | solution.py:182
  230.4 15.1 %collective-permute-start.32 = (bf16[128,1024]{1,0:T(8,128)(2,1)S(1)}, bf16[128,1024]{1,0:T(8,128)(2,1)S(1)}, u32[]{:S(2)}, u32[]{:S(2)}) collective-permute-start(bf16[128,1024]{1,0:T(8,128)(2,1)S(1)} %collective-permute-done.30.refs_10_), channel_id=1, source_target_pairs={{0,8},{8,16},{16,24},{24,0},{1,9},{9,17},{17,25},{25,1},{2,10},{10... | collective-permute-start | bytes 786440 | tf_op jit(solution)/shard_map/ppermute | solution.py:182
  293.0 14.3 %collective-permute-start.41 = (bf16[128,896]{1,0:T(8,128)(2,1)S(1)}, bf16[128,896]{1,0:T(8,128)(2,1)S(1)}, u32[]{:S(2)}, u32[]{:S(2)}) collective-permute-start(bf16[128,896]{1,0:T(8,128)(2,1)S(1)} %convolution_convert_fusion.5), channel_id=1, source_target_pairs={{0,8},{8,16},{16,24},{24,0},{1,9},{9,17},{17,25},{25,1},{2,10},{10... | collective-permute-start | bytes 688136 | tf_op jit(solution)/shard_map/ppermute | solution.py:182
  329.3 24.8 %collective-permute-start.50 = (bf16[128,1792]{1,0:T(8,128)(2,1)S(1)}, bf16[128,1792]{1,0:T(8,128)(2,1)S(1)}, u32[]{:S(2)}, u32[]{:S(2)}) collective-permute-start(bf16[128,1792]{1,0:T(8,128)(2,1)S(1)} %get-tuple-element.53.refs_8_), channel_id=1, source_target_pairs={{0,8},{8,16},{16,24},{24,0},{1,9},{9,17},{17,25},{25,1},{2,10},{10... | collective-permute-start | bytes 1376264 | tf_op jit(solution)/shard_map/ppermute | solution.py:182
  331.9 19.8 %collective-permute-start.47 = (bf16[128,1792]{1,0:T(8,128)(2,1)S(1)}, bf16[128,1792]{1,0:T(8,128)(2,1)S(1)}, u32[]{:S(2)}, u32[]{:S(2)}) collective-permute-start(bf16[128,1792]{1,0:T(8,128)(2,1)S(1)} %get-tuple-element.54.refs_8_), channel_id=1, source_target_pairs={{0,8},{8,16},{16,24},{24,0},{1,9},{9,17},{17,25},{25,1},{2,10},{10... | collective-permute-start | bytes 1376264 | tf_op jit(solution)/shard_map/ppermute | solution.py:182
  351.7 15.3 %collective-permute-start.48 = (bf16[128,1792]{1,0:T(8,128)(2,1)S(1)}, bf16[128,1792]{1,0:T(8,128)(2,1)S(1)}, u32[]{:S(2)}, u32[]{:S(2)}) collective-permute-start(bf16[128,1792]{1,0:T(8,128)(2,1)S(1)} %collective-permute-done.47.refs_9_), channel_id=1, source_target_pairs={{0,8},{8,16},{16,24},{24,0},{1,9},{9,17},{17,25},{25,1},{2,10},{10... | collective-permute-start | bytes 1376264 | tf_op jit(solution)/shard_map/ppermute | solution.py:182
  354.2 22.6 %collective-permute-start.51 = (bf16[128,1792]{1,0:T(8,128)(2,1)S(1)}, bf16[128,1792]{1,0:T(8,128)(2,1)S(1)}, u32[]{:S(2)}, u32[]{:S(2)}) collective-permute-start(bf16[128,1792]{1,0:T(8,128)(2,1)S(1)} %collective-permute-done.50.refs_9_), channel_id=1, source_target_pairs={{0,8},{8,16},{16,24},{24,0},{1,9},{9,17},{17,25},{25,1},{2,10},{10... | collective-permute-start | bytes 1376264 | tf_op jit(solution)/shard_map/ppermute | solution.py:182
  367.0 19.7 %collective-permute-start.49 = (bf16[128,1792]{1,0:T(8,128)(2,1)S(1)}, bf16[128,1792]{1,0:T(8,128)(2,1)S(1)}, u32[]{:S(2)}, u32[]{:S(2)}) collective-permute-start(bf16[128,1792]{1,0:T(8,128)(2,1)S(1)} %collective-permute-done.48.refs_10_), channel_id=1, source_target_pairs={{0,8},{8,16},{16,24},{24,0},{1,9},{9,17},{17,25},{25,1},{2,10},{10... | collective-permute-start | bytes 1376264 | tf_op jit(solution)/shard_map/ppermute | solution.py:182
  376.8 16.0 %collective-permute-start.52 = (bf16[128,1792]{1,0:T(8,128)(2,1)S(1)}, bf16[128,1792]{1,0:T(8,128)(2,1)S(1)}, u32[]{:S(2)}, u32[]{:S(2)}) collective-permute-start(bf16[128,1792]{1,0:T(8,128)(2,1)S(1)} %collective-permute-done.51.refs_10_), channel_id=1, source_target_pairs={{0,8},{8,16},{16,24},{24,0},{1,9},{9,17},{17,25},{25,1},{2,10},{10... | collective-permute-start | bytes 1376264 | tf_op jit(solution)/shard_map/ppermute | solution.py:182
  406.4 12.1 %collective-permute-start.54 = (bf16[128,2048]{1,0:T(8,128)(2,1)S(1)}, bf16[128,2048]{1,0:T(8,128)(2,1)S(1)}, u32[]{:S(2)}, u32[]{:S(2)}) collective-permute-start(bf16[128,2048]{1,0:T(8,128)(2,1)S(1)} %slice.402.refs_12_), channel_id=1, source_target_pairs={{0,4},{1,3},{2,6},{3,1},{4,0},{5,7},{6,2},{7,5},{8,12},{9,11},{10,... | collective-permute-start | bytes 1572872 | tf_op jit(solution)/shard_map/ppermute | solution.py:139
  418.8 11.3 %collective-permute-start.55 = (bf16[64,2048]{1,0:T(8,128)(2,1)S(1)}, bf16[64,2048]{1,0:T(8,128)(2,1)S(1)}, u32[]{:S(2)}, u32[]{:S(2)}) collective-permute-start(bf16[64,2048]{1,0:T(8,128)(2,1)S(1)} %slice.405.refs_12_), channel_id=1, source_target_pairs={{0,2},{1,5},{2,0},{3,7},{4,6},{5,1},{6,4},{7,3},{8,10},{9,13},{10,... | collective-permute-start | bytes 786440 | tf_op jit(solution)/shard_map/ppermute | solution.py:139
  (74 other events, 721.4 us)

commit v4 on v3

--- a/solution.py
+++ b/solution.py
@@ -54,7 +54,7 @@
             row += line[0].shape[0]
         shapes.append((row, column))
     (depth, m), (_, n) = shapes
-    tile = 256 if m % 256 == 0 else 128
+    tile = next(t for t in (512, 256, 128) if m % t == 0)
     operands = pieces + list(earlier) + list(through)
     first = len(operands) - len(through)
     made, *through = pl.pallas_call(
@@ -71,7 +71,7 @@
             pltpu.VMEM((depth, n), BF16),
             pltpu.SemaphoreType.DMA((len(pieces),)),
         ],
-        compiler_params=pltpu.CompilerParams(vmem_limit_bytes=14 << 20),
+        compiler_params=pltpu.CompilerParams(vmem_limit_bytes=16 << 20),
         cost_estimate=pl.CostEstimate(
             flops=2 * depth * m * n,
             bytes_accessed=2 * depth * (m + n) + 4 * m * n,
@@ -182,7 +182,7 @@
         return lax.ppermute(value, "row", self.ring)
 
     def reduce(self, parts, products, beside=None):
-        got, first = None, None
+        got, arrived = None, []
         for back in range(1, self.size + 1):
             rows = jnp.concatenate(parts[back % self.size], axis=0)
             sums = [product(rows) for product in products]
@@ -193,8 +193,8 @@
             if back < self.size:
                 sent = [s.astype(BF16) for s in sums]
                 got = [self.shift(s) for s in sent]
-                first = got[0] if first is None else first
-        return sums, first
+                arrived.append(got[-1])
+        return sums, arrived
 
     def gather(self, blocks, product):
         steps = [blocks]
@@ -239,16 +239,16 @@
         scaled = rows.parts(own, other)
         (gate, up), moved = rows.reduce(scaled, [lambda a: mm(a, gate_w), lambda a: mm(a, up_w)])
         squares = [jnp.sum(jnp.square(p.astype(F32) / gain[None, :]), axis=1) for p in (own, other)]
-        squares = rows.sum_direct(after(jnp.concatenate(squares), moved))
+        squares = rows.sum_direct(after(jnp.concatenate(squares), moved[0]))
         inv_all = lax.rsqrt(squares / features + 1e-05)
         inv = jnp.concatenate(rows.parts(*jnp.split(inv_all, 2))[0])[:, None]
 
         target = lax.all_to_all(
-            after(teacher, moved), PLANE, split_axis=1, concat_axis=0, tiled=True
+            after(teacher, moved[1]), PLANE, split_axis=1, concat_axis=0, tiled=True
         )
         target = rows.own_order(target).astype(F32)
         keep = rows.own_order(loss_mask.astype(F32))
-        x_other = plane.partner(after(x, moved))
+        x_other = plane.partner(after(x, moved[0]))
         inv = after(after(inv, target), x_other)
         gate, up = gate * inv, up * inv
         sigma = jax.nn.sigmoid(gate)

time: 449 us -> 461 us (1.027)
  waiting for transfers between devices: 237 us -> 255 us
    ppermute x36, waiting for transfers between devices: 171 us -> 186 us  [shift(): return lax.ppermute(value, 'row', self.ring)]
    all_to_all x1, waiting for transfers between devices: 0.01 us -> 4.76 us  [body(): lax.all_to_all(after(teacher, moved[1]), PLANE, split_axis=1, concat_axis...]
  transfers between devices with their start and end apart: 64 -> 64, of which waited for: 46 -> 48; matrix products, arithmetic and copies ran while one was open for 17% -> 16% of each run, Pallas kernels for 9% -> 8%
where the time goes in v4:
time: 461 us; the launch traced here: 452 us
  waiting for transfers between devices  255 us (55%)
  matrix products  76.4 us (17%)
  starting transfers between devices  47.8 us (10%)
  Pallas kernels  34.5 us (7%)
  between operations  17.1 us (4%)
  other arithmetic  11.3 us (2%)
  local copies, waits for them, and re-layouts  10.2 us (2%)
    ppermute x36, waiting for transfers between devices, shift(): return lax.ppermute(value, 'row', self.ring)  186 us
    dot_general x24, matrix products, mm_t(): lax.dot_general(left, right, (((1,), (1,)), ((), ())), preferred_element_...  42.2 us
    pallas_call x4, Pallas kernels, weight_grad(): pl.pallas_call(functools.partial(grad_kernel, places, len(operands), tile...  34.5 us
    dot_general x24, matrix products, mm(): return jnp.dot(left, right, preferred_element_type=F32)  34.1 us
    ppermute x4, waiting for transfers between devices, gather(): own = jnp.concatenate([own, lax.ppermute(own, PLANE, perm)], axis=0)  27.9 us
    ppermute x6, waiting for transfers between devices, scatter(): got = lax.ppermute(sent, PLANE, perm)  23.5 us
    ppermute x36, starting transfers between devices, shift(): return lax.ppermute(value, 'row', self.ring)  14.7 us
  transfers between devices with their start and end apart: 64, of which 48 were waited for; matrix products, arithmetic and copies ran while one was open for 16% of the time, Pallas kernels for 8%

profile of v4, /device:TPU:0, one launch (start us, length us, event | category | flops | bytes accessed | tf_op | source)
XLA Modules:
  0.0 452.0 jit_solution(5381383049656559034)
XLA Ops:
  4.7 4.4 collective-permute-done
  11.2 7.2 %collective-permute-done.1 = bf16[128,2048]{1,0:T(8,128)(2,1)S(1)} collective-permute-done((bf16[128,2048]{1,0:T(8,128)(2,1)S(1)}, bf16[128,2048]{1,0:T(8,128)(2,1)S(1)}, u32[]{:S(2)}, u32[]{:S(2)}) %collective-permute-start.1) | collective-permute-done | bytes 524320 | tf_op jit(solution)/shard_map/ppermute | solution.py:119
  25.5 4.4 convolution_convert_fusion
  35.5 19.5 %collective-permute-done.3 = bf16[128,1792]{1,0:T(8,128)(2,1)S(1)} collective-permute-done((bf16[128,1792]{1,0:T(8,128)(2,1)S(1)}, bf16[128,1792]{1,0:T(8,128)(2,1)S(1)}, u32[]{:S(2)}, u32[]{:S(2)}) %collective-permute-start.3) | collective-permute-done | bytes 458784 | tf_op jit(solution)/shard_map/ppermute | solution.py:182
  71.0 7.0 %collective-permute-done.6 = bf16[128,1792]{1,0:T(8,128)(2,1)S(1)} collective-permute-done((bf16[128,1792]{1,0:T(8,128)(2,1)S(1)}, bf16[128,1792]{1,0:T(8,128)(2,1)S(1)}, u32[]{:S(2)}, u32[]{:S(2)}) %collective-permute-start.6) | collective-permute-done | bytes 458784 | tf_op jit(solution)/shard_map/ppermute | solution.py:182
  79.9 7.8 %collective-permute-done.8 = bf16[128,1792]{1,0:T(8,128)(2,1)S(1)} collective-permute-done((bf16[128,1792]{1,0:T(8,128)(2,1)S(1)}, bf16[128,1792]{1,0:T(8,128)(2,1)S(1)}, u32[]{:S(2)}, u32[]{:S(2)}) %collective-permute-start.8) | collective-permute-done | bytes 458784 | tf_op jit(solution)/shard_map/ppermute | solution.py:182
  94.2 5.0 %fusion.9 = bf16[128,1792]{1,0:T(8,128)(2,1)} fusion(bf16[2048,1792]{1,0:T(8,128)(2,1)} %param.15, bf16[128,1792]{1,0:T(8,128)(2,1)S(1)} %collective-permute-done.8, bf16[64,2048]{1,0:T(8,128)(2,1)S(1)} %get-tuple-element.76.refs_7_, bf16[64,2048]{1,0:T(8,128)(2,1)S(1)} %get-tuple-element.72.refs_6_), kind=kOutput, calls=%fused_computation.27 | convolution fusion | flops 941260800 | bytes 8781824 | tf_op jit(solution)/shard_map/dot_general | solution.py:16
  99.2 4.8 %all-to-all-done = bf16[16,8,2048]{2,0,1:T(8,128)(2,1)S(1)} async-done(((bf16[16,8,2048]{2,0,1:T(8,128)(2,1)}), bf16[16,8,2048]{2,0,1:T(8,128)(2,1)S(1)}, u32[]{:S(2)}, u32[]{:S(2)}) %all-to-all-start) | async-done | bytes 524320 | tf_op jit(solution)/shard_map/all_to_all | solution.py:246
  106.4 4.4 fusion.1
  118.7 11.9 %collective-permute-done.14.refs_3_ = bf16[128,896]{1,0:T(8,128)(2,1)S(1)} collective-permute-done((bf16[128,896]{1,0:T(8,128)(2,1)S(1)}, bf16[128,896]{1,0:T(8,128)(2,1)S(1)}, u32[]{:S(2)}, u32[]{:S(2)}) %collective-permute-start.14) | collective-permute-done | bytes 229408 | tf_op jit(solution)/shard_map/ppermute | solution.py:182
  132.2 8.8 %collective-permute-done.16.refs_5_ = bf16[128,896]{1,0:T(8,128)(2,1)S(1)} collective-permute-done((bf16[128,896]{1,0:T(8,128)(2,1)S(1)}, bf16[128,896]{1,0:T(8,128)(2,1)S(1)}, u32[]{:S(2)}, u32[]{:S(2)}) %collective-permute-start.16) | collective-permute-done | bytes 229408 | tf_op jit(solution)/shard_map/ppermute | solution.py:182
  146.6 4.4 collective-permute-done.18.refs_7_
  159.2 7.9 %collective-permute-done.20 = bf16[128,2048]{1,0:T(8,128)(2,1)S(1)} collective-permute-done((bf16[128,2048]{1,0:T(8,128)(2,1)S(1)}, bf16[128,2048]{1,0:T(8,128)(2,1)S(1)}, u32[]{:S(2)}, u32[]{:S(2)}) %collective-permute-start.20) | collective-permute-done | bytes 524320 | tf_op jit(solution)/shard_map/ppermute | solution.py:139
  168.6 7.9 %collective-permute-done.21 = bf16[128,2048]{1,0:T(8,128)(2,1)S(1)} collective-permute-done((bf16[128,2048]{1,0:T(8,128)(2,1)S(1)}, bf16[128,2048]{1,0:T(8,128)(2,1)S(1)}, u32[]{:S(2)}, u32[]{:S(2)}) %collective-permute-start.21) | collective-permute-done | bytes 524320 | tf_op jit(solution)/shard_map/ppermute | solution.py:133
  178.1 7.9 %collective-permute-done.22 = bf16[128,2048]{1,0:T(8,128)(2,1)S(1)} collective-permute-done((bf16[128,2048]{1,0:T(8,128)(2,1)S(1)}, bf16[128,2048]{1,0:T(8,128)(2,1)S(1)}, u32[]{:S(2)}, u32[]{:S(2)}) %collective-permute-start.22) | collective-permute-done | bytes 524320 | tf_op jit(solution)/shard_map/ppermute | solution.py:119
  190.6 10.1 %collective-permute-done.24 = bf16[128,1024]{1,0:T(8,128)(2,1)S(1)} collective-permute-done((bf16[128,1024]{1,0:T(8,128)(2,1)S(1)}, bf16[128,1024]{1,0:T(8,128)(2,1)S(1)}, u32[]{:S(2)}, u32[]{:S(2)}) %collective-permute-start.24) | collective-permute-done | bytes 262176 | tf_op jit(solution)/shard_map/ppermute | solution.py:182
  201.5 4.8 %collective-permute-done.27 = bf16[128,1024]{1,0:T(8,128)(2,1)S(1)} collective-permute-done((bf16[128,1024]{1,0:T(8,128)(2,1)S(1)}, bf16[128,1024]{1,0:T(8,128)(2,1)S(1)}, u32[]{:S(2)}, u32[]{:S(2)}) %collective-permute-start.27) | collective-permute-done | bytes 262176 | tf_op jit(solution)/shard_map/ppermute | solution.py:182
  207.2 5.1 %collective-permute-done.25 = bf16[128,1024]{1,0:T(8,128)(2,1)S(1)} collective-permute-done((bf16[128,1024]{1,0:T(8,128)(2,1)S(1)}, bf16[128,1024]{1,0:T(8,128)(2,1)S(1)}, u32[]{:S(2)}, u32[]{:S(2)}) %collective-permute-start.25) | collective-permute-done | bytes 262176 | tf_op jit(solution)/shard_map/ppermute | solution.py:182
  213.4 4.6 %collective-permute-done.28 = bf16[128,1024]{1,0:T(8,128)(2,1)S(1)} collective-permute-done((bf16[128,1024]{1,0:T(8,128)(2,1)S(1)}, bf16[128,1024]{1,0:T(8,128)(2,1)S(1)}, u32[]{:S(2)}, u32[]{:S(2)}) %collective-permute-start.28) | collective-permute-done | bytes 262176 | tf_op jit(solution)/shard_map/ppermute | solution.py:182
  218.8 5.2 %collective-permute-done.26 = bf16[128,1024]{1,0:T(8,128)(2,1)S(1)} collective-permute-done((bf16[128,1024]{1,0:T(8,128)(2,1)S(1)}, bf16[128,1024]{1,0:T(8,128)(2,1)S(1)}, u32[]{:S(2)}, u32[]{:S(2)}) %collective-permute-start.26) | collective-permute-done | bytes 262176 | tf_op jit(solution)/shard_map/ppermute | solution.py:182
  233.0 10.5 %collective-permute-done.31.refs_11_ = bf16[128,1024]{1,0:T(8,128)(2,1)S(1)} collective-permute-done((bf16[128,1024]{1,0:T(8,128)(2,1)S(1)}, bf16[128,1024]{1,0:T(8,128)(2,1)S(1)}, u32[]{:S(2)}, u32[]{:S(2)}) %collective-permute-start.31) | collective-permute-done | bytes 262176 | tf_op jit(solution)/shard_map/ppermute | solution.py:182
  246.7 7.9 %collective-permute-done.33.refs_13_ = bf16[128,1024]{1,0:T(8,128)(2,1)S(1)} collective-permute-done((bf16[128,1024]{1,0:T(8,128)(2,1)S(1)}, bf16[128,1024]{1,0:T(8,128)(2,1)S(1)}, u32[]{:S(2)}, u32[]{:S(2)}) %collective-permute-start.33) | collective-permute-done | bytes 262176 | tf_op jit(solution)/shard_map/ppermute | solution.py:182
  275.0 8.5 %shard_map.171 = (f32[2048,2048]{1,0:T(8,128)}, f32[128,2048]{1,0:T(8,128)S(1)}) custom-call(bf16[64,2048]{1,0:T(8,128)(2,1)S(1)} %get-tuple-element.68.refs_0_, bf16[64,2048]{1,0:T(8,128)(2,1)S(1)} %get-tuple-element.66.refs_1_, bf16[64,2048]{1,0:T(8,128)(2,1)S(1)} %get-tuple-element.69.refs_2_, ...), custom_call_target="tpu_custom_call", output_to_operand_aliasing={{1}: (17, {})} | custom-call | flops 4294967296 | bytes 20971520 | tf_op jit(solution)/shard_map/pallas_call | solution.py:60
  285.1 7.7 %collective-permute-done.38 = bf16[128,2048]{1,0:T(8,128)(2,1)S(1)} collective-permute-done((bf16[128,2048]{1,0:T(8,128)(2,1)S(1)}, bf16[128,2048]{1,0:T(8,128)(2,1)S(1)}, u32[]{:S(2)}, u32[]{:S(2)}) %collective-permute-start.38) | collective-permute-done | bytes 524320 | tf_op jit(solution)/shard_map/ppermute | solution.py:133
  293.9 8.4 %collective-permute-done.39 = bf16[128,2048]{1,0:T(8,128)(2,1)S(1)} collective-permute-done((bf16[128,2048]{1,0:T(8,128)(2,1)S(1)}, bf16[128,2048]{1,0:T(8,128)(2,1)S(1)}, u32[]{:S(2)}, u32[]{:S(2)}) %collective-permute-start.39) | collective-permute-done | bytes 524320 | tf_op jit(solution)/shard_map/ppermute | solution.py:119
  309.2 8.8 %shard_map.172 = (f32[1792,2048]{1,0:T(8,128)}, f32[128,896]{1,0:T(8,128)S(1)}) custom-call(bf16[128,896]{1,0:T(8,128)(2,1)S(1)} %get-tuple-element.88.refs_0_, bf16[128,896]{1,0:T(8,128)(2,1)S(1)} %get-tuple-element.87.refs_1_, bf16[128,896]{1,0:T(8,128)(2,1)S(1)} %collective-permute-done.13.refs_2_, ...), custom_call_target="tpu_custom_call", output_to_operand_aliasing={{1}: (17, {})} | custom-call | flops 3758096384 | bytes 18612224 | tf_op jit(solution)/shard_map/pallas_call | solution.py:60
  352.1 14.5 %collective-permute-done.47.refs_9_ = bf16[128,1792]{1,0:T(8,128)(2,1)S(1)} collective-permute-done((bf16[128,1792]{1,0:T(8,128)(2,1)S(1)}, bf16[128,1792]{1,0:T(8,128)(2,1)S(1)}, u32[]{:S(2)}, u32[]{:S(2)}) %collective-permute-start.47) | collective-permute-done | bytes 458784 | tf_op jit(solution)/shard_map/ppermute | solution.py:182
  372.8 9.0 %collective-permute-done.48.refs_10_ = bf16[128,1792]{1,0:T(8,128)(2,1)S(1)} collective-permute-done((bf16[128,1792]{1,0:T(8,128)(2,1)S(1)}, bf16[128,1792]{1,0:T(8,128)(2,1)S(1)}, u32[]{:S(2)}, u32[]{:S(2)}) %collective-permute-start.48) | collective-permute-done | bytes 458784 | tf_op jit(solution)/shard_map/ppermute | solution.py:182
  384.3 7.4 %collective-permute-done.51.refs_10_ = bf16[128,1792]{1,0:T(8,128)(2,1)S(1)} collective-permute-done((bf16[128,1792]{1,0:T(8,128)(2,1)S(1)}, bf16[128,1792]{1,0:T(8,128)(2,1)S(1)}, u32[]{:S(2)}, u32[]{:S(2)}) %collective-permute-start.51) | collective-permute-done | bytes 458784 | tf_op jit(solution)/shard_map/ppermute | solution.py:182
  394.5 7.0 %collective-permute-done.49.refs_11_ = bf16[128,1792]{1,0:T(8,128)(2,1)S(1)} collective-permute-done((bf16[128,1792]{1,0:T(8,128)(2,1)S(1)}, bf16[128,1792]{1,0:T(8,128)(2,1)S(1)}, u32[]{:S(2)}, u32[]{:S(2)}) %collective-permute-start.49) | collective-permute-done | bytes 458784 | tf_op jit(solution)/shard_map/ppermute | solution.py:182
  422.7 8.6 %shard_map.173 = (f32[2048,1792]{1,0:T(8,128)}, f32[128,2048]{1,0:T(8,128)S(1)}) custom-call(bf16[64,2048]{1,0:T(8,128)(2,1)S(1)} %get-tuple-element.71.refs_0_, bf16[64,2048]{1,0:T(8,128)(2,1)S(1)} %get-tuple-element.75.refs_1_, bf16[64,2048]{1,0:T(8,128)(2,1)S(1)} %get-tuple-element.74.refs_2_, ...), custom_call_target="tpu_custom_call", output_to_operand_aliasing={{1}: (13, {})} | custom-call | flops 3758096384 | bytes 18612224 | tf_op jit(solution)/shard_map/pallas_call | solution.py:60
  432.6 8.6 %shard_map.174 = (f32[2048,1792]{1,0:T(8,128)}, f32[64,2048]{1,0:T(8,128)S(1)}) custom-call(bf16[64,2048]{1,0:T(8,128)(2,1)S(1)} %get-tuple-element.71.refs_0_, bf16[64,2048]{1,0:T(8,128)(2,1)S(1)} %get-tuple-element.75.refs_1_, bf16[64,2048]{1,0:T(8,128)(2,1)S(1)} %get-tuple-element.74.refs_2_, ...), custom_call_target="tpu_custom_call", output_to_operand_aliasing={{1}: (13, {})} | custom-call | flops 3758096384 | bytes 18612224 | tf_op jit(solution)/shard_map/pallas_call | solution.py:60
  (314 shorter events, 184.8 us)
Async XLA Ops:
  29.9 31.4 %collective-permute-start.5 = (bf16[128,1792]{1,0:T(8,128)(2,1)S(1)}, bf16[128,1792]{1,0:T(8,128)(2,1)S(1)}, u32[]{:S(2)}, u32[]{:S(2)}) collective-permute-start(bf16[128,1792]{1,0:T(8,128)(2,1)S(1)} %convolution_convert_fusion), channel_id=1, source_target_pairs={{0,8},{8,16},{16,24},{24,0},{1,9},{9,17},{17,25},{25,1},{2,10},{10... | collective-permute-start | bytes 1376264 | tf_op jit(solution)/shard_map/ppermute | solution.py:182
  33.3 21.8 %collective-permute-start.3 = (bf16[128,1792]{1,0:T(8,128)(2,1)S(1)}, bf16[128,1792]{1,0:T(8,128)(2,1)S(1)}, u32[]{:S(2)}, u32[]{:S(2)}) collective-permute-start(bf16[128,1792]{1,0:T(8,128)(2,1)S(1)} %convolution_convert_fusion.1), channel_id=1, source_target_pairs={{0,8},{8,16},{16,24},{24,0},{1,9},{9,17},{17,25},{25,1},{2,10},{10... | collective-permute-start | bytes 1376264 | tf_op jit(solution)/shard_map/ppermute | solution.py:182
  62.6 15.3 %collective-permute-start.6 = (bf16[128,1792]{1,0:T(8,128)(2,1)S(1)}, bf16[128,1792]{1,0:T(8,128)(2,1)S(1)}, u32[]{:S(2)}, u32[]{:S(2)}) collective-permute-start(bf16[128,1792]{1,0:T(8,128)(2,1)S(1)} %fusion.7), channel_id=1, source_target_pairs={{0,8},{8,16},{16,24},{24,0},{1,9},{9,17},{17,25},{25,1},{2,10},{10... | collective-permute-start | bytes 1376264 | tf_op jit(solution)/shard_map/ppermute | solution.py:182
  65.5 22.3 %collective-permute-start.8 = (bf16[128,1792]{1,0:T(8,128)(2,1)S(1)}, bf16[128,1792]{1,0:T(8,128)(2,1)S(1)}, u32[]{:S(2)}, u32[]{:S(2)}) collective-permute-start(bf16[128,1792]{1,0:T(8,128)(2,1)S(1)} %fusion.8), channel_id=1, source_target_pairs={{0,8},{8,16},{16,24},{24,0},{1,9},{9,17},{17,25},{25,1},{2,10},{10... | collective-permute-start | bytes 1376264 | tf_op jit(solution)/shard_map/ppermute | solution.py:182
  79.9 26.5 %collective-permute-start.7 = (bf16[128,1792]{1,0:T(8,128)(2,1)}, bf16[128,1792]{1,0:T(8,128)(2,1)}, u32[]{:S(2)}, u32[]{:S(2)}) collective-permute-start(bf16[128,1792]{1,0:T(8,128)(2,1)} %fusion.6), channel_id=1, source_target_pairs={{0,8},{8,16},{16,24},{24,0},{1,9},{9,17},{17,25},{25,1},{2,10},{10... | collective-permute-start | bytes 1376264 | tf_op jit(solution)/shard_map/ppermute | solution.py:182
  90.5 13.5 %all-to-all-start = ((bf16[16,8,2048]{2,0,1:T(8,128)(2,1)}), bf16[16,8,2048]{2,0,1:T(8,128)(2,1)S(1)}, u32[]{:S(2)}, u32[]{:S(2)}) async-start(bf16[16,8,2048]{2,0,1:T(8,128)(2,1)} %bitcast.58), calls=%async_computation | async-start | bytes 1048576 | tf_op jit(solution)/shard_map/all_to_all | solution.py:246
  99.2 15.0 %collective-permute-start.12 = (bf16[128,1792]{1,0:T(8,128)(2,1)}, bf16[128,1792]{1,0:T(8,128)(2,1)}, u32[]{:S(2)}, u32[]{:S(2)}) collective-permute-start(bf16[128,1792]{1,0:T(8,128)(2,1)} %fusion.9), channel_id=1, source_target_pairs={{0,8},{8,16},{16,24},{24,0},{1,9},{9,17},{17,25},{25,1},{2,10},{10... | collective-permute-start | bytes 1376264 | tf_op jit(solution)/shard_map/ppermute | solution.py:182
  116.6 14.7 %collective-permute-start.13 = (bf16[128,896]{1,0:T(8,128)(2,1)S(1)}, bf16[128,896]{1,0:T(8,128)(2,1)S(1)}, u32[]{:S(2)}, u32[]{:S(2)}) collective-permute-start(bf16[128,896]{1,0:T(8,128)(2,1)S(1)} %get-tuple-element.88.refs_0_), channel_id=1, source_target_pairs={{0,8},{8,16},{16,24},{24,0},{1,9},{9,17},{17,25},{25,1},{2,10},{10... | collective-permute-start | bytes 688136 | tf_op jit(solution)/shard_map/ppermute | solution.py:182
  116.7 13.9 %collective-permute-start.14 = (bf16[128,896]{1,0:T(8,128)(2,1)S(1)}, bf16[128,896]{1,0:T(8,128)(2,1)S(1)}, u32[]{:S(2)}, u32[]{:S(2)}) collective-permute-start(bf16[128,896]{1,0:T(8,128)(2,1)S(1)} %get-tuple-element.87.refs_1_), channel_id=1, source_target_pairs={{0,8},{8,16},{16,24},{24,0},{1,9},{9,17},{17,25},{25,1},{2,10},{10... | collective-permute-start | bytes 688136 | tf_op jit(solution)/shard_map/ppermute | solution.py:182
  130.6 10.3 %collective-permute-start.16 = (bf16[128,896]{1,0:T(8,128)(2,1)S(1)}, bf16[128,896]{1,0:T(8,128)(2,1)S(1)}, u32[]{:S(2)}, u32[]{:S(2)}) collective-permute-start(bf16[128,896]{1,0:T(8,128)(2,1)S(1)} %collective-permute-done.14.refs_3_), channel_id=1, source_target_pairs={{0,8},{8,16},{16,24},{24,0},{1,9},{9,17},{17,25},{25,1},{2,10},{10... | collective-permute-start | bytes 688136 | tf_op jit(solution)/shard_map/ppermute | solution.py:182
  131.4 14.5 %collective-permute-start.15 = (bf16[128,896]{1,0:T(8,128)(2,1)S(1)}, bf16[128,896]{1,0:T(8,128)(2,1)S(1)}, u32[]{:S(2)}, u32[]{:S(2)}) collective-permute-start(bf16[128,896]{1,0:T(8,128)(2,1)S(1)} %collective-permute-done.13.refs_2_), channel_id=1, source_target_pairs={{0,8},{8,16},{16,24},{24,0},{1,9},{9,17},{17,25},{25,1},{2,10},{10... | collective-permute-start | bytes 688136 | tf_op jit(solution)/shard_map/ppermute | solution.py:182
  141.0 10.1 %collective-permute-start.18 = (bf16[128,896]{1,0:T(8,128)(2,1)S(1)}, bf16[128,896]{1,0:T(8,128)(2,1)S(1)}, u32[]{:S(2)}, u32[]{:S(2)}) collective-permute-start(bf16[128,896]{1,0:T(8,128)(2,1)S(1)} %collective-permute-done.16.refs_5_), channel_id=1, source_target_pairs={{0,8},{8,16},{16,24},{24,0},{1,9},{9,17},{17,25},{25,1},{2,10},{10... | collective-permute-start | bytes 688136 | tf_op jit(solution)/shard_map/ppermute | solution.py:182
  189.7 11.0 %collective-permute-start.24 = (bf16[128,1024]{1,0:T(8,128)(2,1)S(1)}, bf16[128,1024]{1,0:T(8,128)(2,1)S(1)}, u32[]{:S(2)}, u32[]{:S(2)}) collective-permute-start(bf16[128,1024]{1,0:T(8,128)(2,1)S(1)} %convolution_convert_fusion.3), channel_id=1, source_target_pairs={{0,8},{8,16},{16,24},{24,0},{1,9},{9,17},{17,25},{25,1},{2,10},{10... | collective-permute-start | bytes 786440 | tf_op jit(solution)/shard_map/ppermute | solution.py:182
  190.5 15.8 %collective-permute-start.27 = (bf16[128,1024]{1,0:T(8,128)(2,1)S(1)}, bf16[128,1024]{1,0:T(8,128)(2,1)S(1)}, u32[]{:S(2)}, u32[]{:S(2)}) collective-permute-start(bf16[128,1024]{1,0:T(8,128)(2,1)S(1)} %convolution_convert_fusion.2), channel_id=1, source_target_pairs={{0,8},{8,16},{16,24},{24,0},{1,9},{9,17},{17,25},{25,1},{2,10},{10... | collective-permute-start | bytes 786440 | tf_op jit(solution)/shard_map/ppermute | solution.py:182
  201.5 10.8 %collective-permute-start.25 = (bf16[128,1024]{1,0:T(8,128)(2,1)S(1)}, bf16[128,1024]{1,0:T(8,128)(2,1)S(1)}, u32[]{:S(2)}, u32[]{:S(2)}) collective-permute-start(bf16[128,1024]{1,0:T(8,128)(2,1)S(1)} %fusion.29), channel_id=1, source_target_pairs={{0,8},{8,16},{16,24},{24,0},{1,9},{9,17},{17,25},{25,1},{2,10},{10... | collective-permute-start | bytes 786440 | tf_op jit(solution)/shard_map/ppermute | solution.py:182
  207.1 11.0 %collective-permute-start.28 = (bf16[128,1024]{1,0:T(8,128)(2,1)S(1)}, bf16[128,1024]{1,0:T(8,128)(2,1)S(1)}, u32[]{:S(2)}, u32[]{:S(2)}) collective-permute-start(bf16[128,1024]{1,0:T(8,128)(2,1)S(1)} %fusion.31), channel_id=1, source_target_pairs={{0,8},{8,16},{16,24},{24,0},{1,9},{9,17},{17,25},{25,1},{2,10},{10... | collective-permute-start | bytes 786440 | tf_op jit(solution)/shard_map/ppermute | solution.py:182
  213.0 11.1 %collective-permute-start.26 = (bf16[128,1024]{1,0:T(8,128)(2,1)S(1)}, bf16[128,1024]{1,0:T(8,128)(2,1)S(1)}, u32[]{:S(2)}, u32[]{:S(2)}) collective-permute-start(bf16[128,1024]{1,0:T(8,128)(2,1)S(1)} %fusion.28), channel_id=1, source_target_pairs={{0,8},{8,16},{16,24},{24,0},{1,9},{9,17},{17,25},{25,1},{2,10},{10... | collective-permute-start | bytes 786440 | tf_op jit(solution)/shard_map/ppermute | solution.py:182
  229.6 15.4 %collective-permute-start.30 = (bf16[128,1024]{1,0:T(8,128)(2,1)S(1)}, bf16[128,1024]{1,0:T(8,128)(2,1)S(1)}, u32[]{:S(2)}, u32[]{:S(2)}) collective-permute-start(bf16[128,1024]{1,0:T(8,128)(2,1)S(1)} %get-tuple-element.79.refs_8_), channel_id=1, source_target_pairs={{0,8},{8,16},{16,24},{24,0},{1,9},{9,17},{17,25},{25,1},{2,10},{10... | collective-permute-start | bytes 786440 | tf_op jit(solution)/shard_map/ppermute | solution.py:182
  231.2 12.4 %collective-permute-start.31 = (bf16[128,1024]{1,0:T(8,128)(2,1)S(1)}, bf16[128,1024]{1,0:T(8,128)(2,1)S(1)}, u32[]{:S(2)}, u32[]{:S(2)}) collective-permute-start(bf16[128,1024]{1,0:T(8,128)(2,1)S(1)} %get-tuple-element.80.refs_9_), channel_id=1, source_target_pairs={{0,8},{8,16},{16,24},{24,0},{1,9},{9,17},{17,25},{25,1},{2,10},{10... | collective-permute-start | bytes 786440 | tf_op jit(solution)/shard_map/ppermute | solution.py:182
  243.5 11.0 %collective-permute-start.33 = (bf16[128,1024]{1,0:T(8,128)(2,1)S(1)}, bf16[128,1024]{1,0:T(8,128)(2,1)S(1)}, u32[]{:S(2)}, u32[]{:S(2)}) collective-permute-start(bf16[128,1024]{1,0:T(8,128)(2,1)S(1)} %collective-permute-done.31.refs_11_), channel_id=1, source_target_pairs={{0,8},{8,16},{16,24},{24,0},{1,9},{9,17},{17,25},{25,1},{2,10},{10... | collective-permute-start | bytes 786440 | tf_op jit(solution)/shard_map/ppermute | solution.py:182
  245.1 15.1 %collective-permute-start.32 = (bf16[128,1024]{1,0:T(8,128)(2,1)S(1)}, bf16[128,1024]{1,0:T(8,128)(2,1)S(1)}, u32[]{:S(2)}, u32[]{:S(2)}) collective-permute-start(bf16[128,1024]{1,0:T(8,128)(2,1)S(1)} %collective-permute-done.30.refs_10_), channel_id=1, source_target_pairs={{0,8},{8,16},{16,24},{24,0},{1,9},{9,17},{17,25},{25,1},{2,10},{10... | collective-permute-start | bytes 786440 | tf_op jit(solution)/shard_map/ppermute | solution.py:182
  254.6 10.4 %collective-permute-start.35 = (bf16[128,1024]{1,0:T(8,128)(2,1)S(1)}, bf16[128,1024]{1,0:T(8,128)(2,1)S(1)}, u32[]{:S(2)}, u32[]{:S(2)}) collective-permute-start(bf16[128,1024]{1,0:T(8,128)(2,1)S(1)} %collective-permute-done.33.refs_13_), channel_id=1, source_target_pairs={{0,8},{8,16},{16,24},{24,0},{1,9},{9,17},{17,25},{25,1},{2,10},{10... | collective-permute-start | bytes 786440 | tf_op jit(solution)/shard_map/ppermute | solution.py:182
  273.6 9.9 %collective-permute-start.37 = (bf16[128,2048]{1,0:T(8,128)(2,1)S(1)}, bf16[128,2048]{1,0:T(8,128)(2,1)S(1)}, u32[]{:S(2)}, u32[]{:S(2)}) collective-permute-start(bf16[128,2048]{1,0:T(8,128)(2,1)S(1)} %slice.407.refs_16_), channel_id=1, source_target_pairs={{0,4},{1,3},{2,6},{3,1},{4,0},{5,7},{6,2},{7,5},{8,12},{9,11},{10,... | collective-permute-start | bytes 1572872 | tf_op jit(solution)/shard_map/ppermute | solution.py:139
  307.8 10.3 %collective-permute-start.44 = (bf16[128,896]{1,0:T(8,128)(2,1)S(1)}, bf16[128,896]{1,0:T(8,128)(2,1)S(1)}, u32[]{:S(2)}, u32[]{:S(2)}) collective-permute-start(bf16[128,896]{1,0:T(8,128)(2,1)S(1)} %convolution_convert_fusion.4.refs_16_), channel_id=1, source_target_pairs={{0,8},{8,16},{16,24},{24,0},{1,9},{9,17},{17,25},{25,1},{2,10},{10... | collective-permute-start | bytes 688136 | tf_op jit(solution)/shard_map/ppermute | solution.py:182
  307.9 14.3 %collective-permute-start.41 = (bf16[128,896]{1,0:T(8,128)(2,1)S(1)}, bf16[128,896]{1,0:T(8,128)(2,1)S(1)}, u32[]{:S(2)}, u32[]{:S(2)}) collective-permute-start(bf16[128,896]{1,0:T(8,128)(2,1)S(1)} %convolution_convert_fusion.5), channel_id=1, source_target_pairs={{0,8},{8,16},{16,24},{24,0},{1,9},{9,17},{17,25},{25,1},{2,10},{10... | collective-permute-start | bytes 688136 | tf_op jit(solution)/shard_map/ppermute | solution.py:182
  344.2 24.9 %collective-permute-start.50 = (bf16[128,1792]{1,0:T(8,128)(2,1)S(1)}, bf16[128,1792]{1,0:T(8,128)(2,1)S(1)}, u32[]{:S(2)}, u32[]{:S(2)}) collective-permute-start(bf16[128,1792]{1,0:T(8,128)(2,1)S(1)} %get-tuple-element.53.refs_8_), channel_id=1, source_target_pairs={{0,8},{8,16},{16,24},{24,0},{1,9},{9,17},{17,25},{25,1},{2,10},{10... | collective-permute-start | bytes 1376264 | tf_op jit(solution)/shard_map/ppermute | solution.py:182
  346.8 19.8 %collective-permute-start.47 = (bf16[128,1792]{1,0:T(8,128)(2,1)S(1)}, bf16[128,1792]{1,0:T(8,128)(2,1)S(1)}, u32[]{:S(2)}, u32[]{:S(2)}) collective-permute-start(bf16[128,1792]{1,0:T(8,128)(2,1)S(1)} %get-tuple-element.54.refs_8_), channel_id=1, source_target_pairs={{0,8},{8,16},{16,24},{24,0},{1,9},{9,17},{17,25},{25,1},{2,10},{10... | collective-permute-start | bytes 1376264 | tf_op jit(solution)/shard_map/ppermute | solution.py:182
  366.6 15.3 %collective-permute-start.48 = (bf16[128,1792]{1,0:T(8,128)(2,1)S(1)}, bf16[128,1792]{1,0:T(8,128)(2,1)S(1)}, u32[]{:S(2)}, u32[]{:S(2)}) collective-permute-start(bf16[128,1792]{1,0:T(8,128)(2,1)S(1)} %collective-permute-done.47.refs_9_), channel_id=1, source_target_pairs={{0,8},{8,16},{16,24},{24,0},{1,9},{9,17},{17,25},{25,1},{2,10},{10... | collective-permute-start | bytes 1376264 | tf_op jit(solution)/shard_map/ppermute | solution.py:182
  369.1 22.6 %collective-permute-start.51 = (bf16[128,1792]{1,0:T(8,128)(2,1)S(1)}, bf16[128,1792]{1,0:T(8,128)(2,1)S(1)}, u32[]{:S(2)}, u32[]{:S(2)}) collective-permute-start(bf16[128,1792]{1,0:T(8,128)(2,1)S(1)} %collective-permute-done.50.refs_9_), channel_id=1, source_target_pairs={{0,8},{8,16},{16,24},{24,0},{1,9},{9,17},{17,25},{25,1},{2,10},{10... | collective-permute-start | bytes 1376264 | tf_op jit(solution)/shard_map/ppermute | solution.py:182
  381.9 19.7 %collective-permute-start.49 = (bf16[128,1792]{1,0:T(8,128)(2,1)S(1)}, bf16[128,1792]{1,0:T(8,128)(2,1)S(1)}, u32[]{:S(2)}, u32[]{:S(2)}) collective-permute-start(bf16[128,1792]{1,0:T(8,128)(2,1)S(1)} %collective-permute-done.48.refs_10_), channel_id=1, source_target_pairs={{0,8},{8,16},{16,24},{24,0},{1,9},{9,17},{17,25},{25,1},{2,10},{10... | collective-permute-start | bytes 1376264 | tf_op jit(solution)/shard_map/ppermute | solution.py:182
  391.7 16.0 %collective-permute-start.52 = (bf16[128,1792]{1,0:T(8,128)(2,1)S(1)}, bf16[128,1792]{1,0:T(8,128)(2,1)S(1)}, u32[]{:S(2)}, u32[]{:S(2)}) collective-permute-start(bf16[128,1792]{1,0:T(8,128)(2,1)S(1)} %collective-permute-done.51.refs_10_), channel_id=1, source_target_pairs={{0,8},{8,16},{16,24},{24,0},{1,9},{9,17},{17,25},{25,1},{2,10},{10... | collective-permute-start | bytes 1376264 | tf_op jit(solution)/shard_map/ppermute | solution.py:182
  421.4 10.0 %collective-permute-start.54 = (bf16[128,2048]{1,0:T(8,128)(2,1)S(1)}, bf16[128,2048]{1,0:T(8,128)(2,1)S(1)}, u32[]{:S(2)}, u32[]{:S(2)}) collective-permute-start(bf16[128,2048]{1,0:T(8,128)(2,1)S(1)} %slice.406.refs_12_), channel_id=1, source_target_pairs={{0,4},{1,3},{2,6},{3,1},{4,0},{5,7},{6,2},{7,5},{8,12},{9,11},{10,... | collective-permute-start | bytes 1572872 | tf_op jit(solution)/shard_map/ppermute | solution.py:139
  (74 other events, 736.3 us)

commit v5 on v4

--- a/solution.py
+++ b/solution.py
@@ -110,9 +110,6 @@
             self.perms.append([(c, c ^ (odd if c & 1 else even)) for c in range(size)])
         self.swap = [(c, c ^ 1) for c in range(size)]
 
-    def partner(self, block):
-        return lax.ppermute(block, PLANE, self.perms[0])
-
     def gather(self, block, paired=False):
         own = block
         for perm in self.perms[1:] if paired else self.perms:
@@ -193,7 +190,7 @@
             if back < self.size:
                 sent = [s.astype(BF16) for s in sums]
                 got = [self.shift(s) for s in sent]
-                arrived.append(got[-1])
+                arrived.append(got)
         return sums, arrived
 
     def gather(self, blocks, product):
@@ -239,17 +236,16 @@
         scaled = rows.parts(own, other)
         (gate, up), moved = rows.reduce(scaled, [lambda a: mm(a, gate_w), lambda a: mm(a, up_w)])
         squares = [jnp.sum(jnp.square(p.astype(F32) / gain[None, :]), axis=1) for p in (own, other)]
-        squares = rows.sum_direct(after(jnp.concatenate(squares), moved[0]))
+        squares = rows.sum_direct(after(jnp.concatenate(squares), moved[1][0]))
         inv_all = lax.rsqrt(squares / features + 1e-05)
         inv = jnp.concatenate(rows.parts(*jnp.split(inv_all, 2))[0])[:, None]
 
         target = lax.all_to_all(
-            after(teacher, moved[1]), PLANE, split_axis=1, concat_axis=0, tiled=True
+            after(teacher, moved[0][0]), PLANE, split_axis=1, concat_axis=0, tiled=True
         )
         target = rows.own_order(target).astype(F32)
         keep = rows.own_order(loss_mask.astype(F32))
-        x_other = plane.partner(after(x, moved[0]))
-        inv = after(after(inv, target), x_other)
+        inv = after(inv, target)
         gate, up = gate * inv, up * inv
         sigma = jax.nn.sigmoid(gate)
         activated = gate * sigma
@@ -259,8 +255,9 @@
             [hidden[:, lo:hi] for lo, hi in cuts],
             lambda bs: sum(mm(b, down_w[lo:hi]) for b, (lo, hi) in zip(bs, cuts)).astype(BF16),
         )
-        x_pair = jnp.concatenate([x, x_other], axis=0)
-        residual = (x_pair.astype(F32) + plane.scatter(ffn, paired=True)).astype(BF16)
+        x_other = own[block : 2 * block].astype(F32) / gain[None, :]
+        x_pair = jnp.concatenate([x.astype(F32), x_other], axis=0)
+        residual = (x_pair + plane.scatter(ffn, paired=True)).astype(BF16)
         residuals = rows.parts(*plane.gather(residual, paired=True))
 
         ecuts = halves(proj_w.shape[1])

time: 461 us -> 442 us (0.959)
  waiting for transfers between devices: 255 us -> 234 us
    ppermute x36, waiting for transfers between devices: 186 us -> 173 us  [shift(): return lax.ppermute(value, 'row', self.ring)]
    all_to_all x1, waiting for transfers between devices: 4.76 us -> 0.01 us  [body(): lax.all_to_all(after(teacher, moved[0][0]), PLANE, split_axis=1, concat_a...]
  transfers between devices with their start and end apart: 64 -> 63, of which waited for: 48 -> 47; matrix products, arithmetic and copies ran while one was open for 16% -> 18% of each run, Pallas kernels for 8% -> 8%
where the time goes in v5:
time: 442 us; the launch traced here: 433 us
  waiting for transfers between devices  234 us (53%)
  matrix products  80.4 us (18%)
  starting transfers between devices  46.2 us (10%)
  Pallas kernels  34.5 us (8%)
  between operations  15.6 us (4%)
  other arithmetic  11.3 us (3%)
  local copies, waits for them, and re-layouts  10.5 us (2%)
    ppermute x36, waiting for transfers between devices, shift(): return lax.ppermute(value, 'row', self.ring)  173 us
    dot_general x24, matrix products, mm_t(): lax.dot_general(left, right, (((1,), (1,)), ((), ())), preferred_element_...  42.3 us
    dot_general x24, matrix products, mm(): return jnp.dot(left, right, preferred_element_type=F32)  38.1 us
    pallas_call x4, Pallas kernels, weight_grad(): pl.pallas_call(functools.partial(grad_kernel, places, len(operands), tile...  34.5 us
    ppermute x4, waiting for transfers between devices, gather(): own = jnp.concatenate([own, lax.ppermute(own, PLANE, perm)], axis=0)  27.8 us
    ppermute x6, waiting for transfers between devices, scatter(): got = lax.ppermute(sent, PLANE, perm)  23.9 us
    ppermute x36, starting transfers between devices, shift(): return lax.ppermute(value, 'row', self.ring)  15 us
  transfers between devices with their start and end apart: 63, of which 47 were waited for; matrix products, arithmetic and copies ran while one was open for 18% of the time, Pallas kernels for 8%

profile of v5, /device:TPU:0, one launch (start us, length us, event | category | flops | bytes accessed | tf_op | source)
XLA Modules:
  0.0 432.9 jit_solution(8809482063432156199)
XLA Ops:
  4.7 4.4 %collective-permute-done = bf16[64,2048]{1,0:T(8,128)(2,1)S(1)} collective-permute-done((bf16[64,2048]{1,0:T(8,128)(2,1)S(1)}, bf16[64,2048]{1,0:T(8,128)(2,1)S(1)}, u32[]{:S(2)}, u32[]{:S(2)}) %collective-permute-start) | collective-permute-done | bytes 262176 | tf_op jit(solution)/shard_map/ppermute | solution.py:116
  11.2 7.2 %collective-permute-done.1 = bf16[128,2048]{1,0:T(8,128)(2,1)S(1)} collective-permute-done((bf16[128,2048]{1,0:T(8,128)(2,1)S(1)}, bf16[128,2048]{1,0:T(8,128)(2,1)S(1)}, u32[]{:S(2)}, u32[]{:S(2)}) %collective-permute-start.1) | collective-permute-done | bytes 524320 | tf_op jit(solution)/shard_map/ppermute | solution.py:116
  26.3 4.4 %convolution_convert_fusion.1 = bf16[128,1792]{1,0:T(8,128)(2,1)S(1)} fusion(bf16[2048,1792]{1,0:T(8,128)(2,1)} %param.14, bf16[64,2048]{1,0:T(8,128)(2,1)S(1)} %get-tuple-element.78.refs_3_, bf16[64,2048]{1,0:T(8,128)(2,1)S(1)} %get-tuple-element.74.refs_2_), kind=kOutput, calls=%fused_computation.45 | convolution fusion | flops 940802048 | bytes 8323072 | tf_op jit(solution)/shard_map/dot_general | solution.py:16
  37.0 9.2 %collective-permute-done.3 = bf16[128,1792]{1,0:T(8,128)(2,1)S(1)} collective-permute-done((bf16[128,1792]{1,0:T(8,128)(2,1)S(1)}, bf16[128,1792]{1,0:T(8,128)(2,1)S(1)}, u32[]{:S(2)}, u32[]{:S(2)}) %collective-permute-start.3) | collective-permute-done | bytes 458784 | tf_op jit(solution)/shard_map/ppermute | solution.py:179
  56.1 5.0 %fusion.9 = bf16[128,1792]{1,0:T(8,128)(2,1)} fusion(bf16[2048,1792]{1,0:T(8,128)(2,1)} %param.15, bf16[128,1792]{1,0:T(8,128)(2,1)} %collective-permute-done.9, bf16[64,2048]{1,0:T(8,128)(2,1)S(1)} %get-tuple-element.77.refs_5_, bf16[64,2048]{1,0:T(8,128)(2,1)S(1)} %get-tuple-element.73.refs_4_), kind=kOutput, calls=%fused_computation.27 | convolution fusion | flops 941260800 | bytes 8781824 | tf_op jit(solution)/shard_map/dot_general | solution.py:16
  61.2 4.7 %collective-permute-done.4 = bf16[128,1792]{1,0:T(8,128)(2,1)S(1)} collective-permute-done((bf16[128,1792]{1,0:T(8,128)(2,1)}, bf16[128,1792]{1,0:T(8,128)(2,1)S(1)}, u32[]{:S(2)}, u32[]{:S(2)}) %collective-permute-start.4) | collective-permute-done | bytes 458784 | tf_op jit(solution)/shard_map/ppermute | solution.py:179
  76.6 4.4 %fusion.8 = bf16[128,1792]{1,0:T(8,128)(2,1)S(1)} fusion(bf16[2048,1792]{1,0:T(8,128)(2,1)} %param.15, bf16[128,1792]{1,0:T(8,128)(2,1)} %collective-permute-done.10, bf16[64,2048]{1,0:T(8,128)(2,1)S(1)} %get-tuple-element.76.refs_7_, bf16[64,2048]{1,0:T(8,128)(2,1)S(1)} %get-tuple-element.72.refs_6_), kind=kOutput, calls=%fused_computation.26 | convolution fusion | flops 941260800 | bytes 8781824 | tf_op jit(solution)/shard_map/dot_general | solution.py:16
  84.6 7.2 %collective-permute-done.5 = bf16[128,1792]{1,0:T(8,128)(2,1)} collective-permute-done((bf16[128,1792]{1,0:T(8,128)(2,1)S(1)}, bf16[128,1792]{1,0:T(8,128)(2,1)}, u32[]{:S(2)}, u32[]{:S(2)}) %collective-permute-start.5) | collective-permute-done | bytes 458784 | tf_op jit(solution)/shard_map/ppermute | solution.py:179
  94.2 5.1 %collective-permute-done.11 = bf16[128,1792]{1,0:T(8,128)(2,1)S(1)} collective-permute-done((bf16[128,1792]{1,0:T(8,128)(2,1)S(1)}, bf16[128,1792]{1,0:T(8,128)(2,1)S(1)}, u32[]{:S(2)}, u32[]{:S(2)}) %collective-permute-start.11) | collective-permute-done | bytes 458784 | tf_op jit(solution)/shard_map/ppermute | solution.py:179
  102.9 10.1 %collective-permute-done.13.refs_3_ = bf16[128,896]{1,0:T(8,128)(2,1)S(1)} collective-permute-done((bf16[128,896]{1,0:T(8,128)(2,1)S(1)}, bf16[128,896]{1,0:T(8,128)(2,1)S(1)}, u32[]{:S(2)}, u32[]{:S(2)}) %collective-permute-start.13) | collective-permute-done | bytes 229408 | tf_op jit(solution)/shard_map/ppermute | solution.py:179
  114.5 7.8 %collective-permute-done.15.refs_5_ = bf16[128,896]{1,0:T(8,128)(2,1)S(1)} collective-permute-done((bf16[128,896]{1,0:T(8,128)(2,1)S(1)}, bf16[128,896]{1,0:T(8,128)(2,1)S(1)}, u32[]{:S(2)}, u32[]{:S(2)}) %collective-permute-start.15) | collective-permute-done | bytes 229408 | tf_op jit(solution)/shard_map/ppermute | solution.py:179
  140.3 8.1 %collective-permute-done.19 = bf16[128,2048]{1,0:T(8,128)(2,1)S(1)} collective-permute-done((bf16[128,2048]{1,0:T(8,128)(2,1)S(1)}, bf16[128,2048]{1,0:T(8,128)(2,1)S(1)}, u32[]{:S(2)}, u32[]{:S(2)}) %collective-permute-start.19) | collective-permute-done | bytes 524320 | tf_op jit(solution)/shard_map/ppermute | solution.py:136
  149.8 8.0 %collective-permute-done.20 = bf16[128,2048]{1,0:T(8,128)(2,1)S(1)} collective-permute-done((bf16[128,2048]{1,0:T(8,128)(2,1)S(1)}, bf16[128,2048]{1,0:T(8,128)(2,1)S(1)}, u32[]{:S(2)}, u32[]{:S(2)}) %collective-permute-start.20) | collective-permute-done | bytes 524320 | tf_op jit(solution)/shard_map/ppermute | solution.py:130
  159.2 8.1 %collective-permute-done.21 = bf16[128,2048]{1,0:T(8,128)(2,1)S(1)} collective-permute-done((bf16[128,2048]{1,0:T(8,128)(2,1)S(1)}, bf16[128,2048]{1,0:T(8,128)(2,1)S(1)}, u32[]{:S(2)}, u32[]{:S(2)}) %collective-permute-start.21) | collective-permute-done | bytes 524320 | tf_op jit(solution)/shard_map/ppermute | solution.py:116
  171.8 10.1 %collective-permute-done.23 = bf16[128,1024]{1,0:T(8,128)(2,1)S(1)} collective-permute-done((bf16[128,1024]{1,0:T(8,128)(2,1)S(1)}, bf16[128,1024]{1,0:T(8,128)(2,1)S(1)}, u32[]{:S(2)}, u32[]{:S(2)}) %collective-permute-start.23) | collective-permute-done | bytes 262176 | tf_op jit(solution)/shard_map/ppermute | solution.py:179
  182.8 4.8 %collective-permute-done.26 = bf16[128,1024]{1,0:T(8,128)(2,1)S(1)} collective-permute-done((bf16[128,1024]{1,0:T(8,128)(2,1)S(1)}, bf16[128,1024]{1,0:T(8,128)(2,1)S(1)}, u32[]{:S(2)}, u32[]{:S(2)}) %collective-permute-start.26) | collective-permute-done | bytes 262176 | tf_op jit(solution)/shard_map/ppermute | solution.py:179
  188.4 5.1 %collective-permute-done.24 = bf16[128,1024]{1,0:T(8,128)(2,1)S(1)} collective-permute-done((bf16[128,1024]{1,0:T(8,128)(2,1)S(1)}, bf16[128,1024]{1,0:T(8,128)(2,1)S(1)}, u32[]{:S(2)}, u32[]{:S(2)}) %collective-permute-start.24) | collective-permute-done | bytes 262176 | tf_op jit(solution)/shard_map/ppermute | solution.py:179
  194.7 4.6 %collective-permute-done.27 = bf16[128,1024]{1,0:T(8,128)(2,1)S(1)} collective-permute-done((bf16[128,1024]{1,0:T(8,128)(2,1)S(1)}, bf16[128,1024]{1,0:T(8,128)(2,1)S(1)}, u32[]{:S(2)}, u32[]{:S(2)}) %collective-permute-start.27) | collective-permute-done | bytes 262176 | tf_op jit(solution)/shard_map/ppermute | solution.py:179
  200.1 5.2 %collective-permute-done.25 = bf16[128,1024]{1,0:T(8,128)(2,1)S(1)} collective-permute-done((bf16[128,1024]{1,0:T(8,128)(2,1)S(1)}, bf16[128,1024]{1,0:T(8,128)(2,1)S(1)}, u32[]{:S(2)}, u32[]{:S(2)}) %collective-permute-start.25) | collective-permute-done | bytes 262176 | tf_op jit(solution)/shard_map/ppermute | solution.py:179
  214.2 10.5 %collective-permute-done.30.refs_11_ = bf16[128,1024]{1,0:T(8,128)(2,1)S(1)} collective-permute-done((bf16[128,1024]{1,0:T(8,128)(2,1)S(1)}, bf16[128,1024]{1,0:T(8,128)(2,1)S(1)}, u32[]{:S(2)}, u32[]{:S(2)}) %collective-permute-start.30) | collective-permute-done | bytes 262176 | tf_op jit(solution)/shard_map/ppermute | solution.py:179
  227.9 7.9 %collective-permute-done.32.refs_13_ = bf16[128,1024]{1,0:T(8,128)(2,1)S(1)} collective-permute-done((bf16[128,1024]{1,0:T(8,128)(2,1)S(1)}, bf16[128,1024]{1,0:T(8,128)(2,1)S(1)}, u32[]{:S(2)}, u32[]{:S(2)}) %collective-permute-start.32) | collective-permute-done | bytes 262176 | tf_op jit(solution)/shard_map/ppermute | solution.py:179
  256.0 8.5 %shard_map.171 = (f32[2048,2048]{1,0:T(8,128)}, f32[128,2048]{1,0:T(8,128)S(1)}) custom-call(bf16[64,2048]{1,0:T(8,128)(2,1)S(1)} %get-tuple-element.68.refs_0_, bf16[64,2048]{1,0:T(8,128)(2,1)S(1)} %get-tuple-element.66.refs_1_, bf16[64,2048]{1,0:T(8,128)(2,1)S(1)} %get-tuple-element.69.refs_2_, ...), custom_call_target="tpu_custom_call", output_to_operand_aliasing={{1}: (17, {})} | custom-call | flops 4294967296 | bytes 20971520 | tf_op jit(solution)/shard_map/pallas_call | solution.py:60
  266.1 7.7 %collective-permute-done.37 = bf16[128,2048]{1,0:T(8,128)(2,1)S(1)} collective-permute-done((bf16[128,2048]{1,0:T(8,128)(2,1)S(1)}, bf16[128,2048]{1,0:T(8,128)(2,1)S(1)}, u32[]{:S(2)}, u32[]{:S(2)}) %collective-permute-start.37) | collective-permute-done | bytes 524320 | tf_op jit(solution)/shard_map/ppermute | solution.py:130
  275.1 8.2 %collective-permute-done.38 = bf16[128,2048]{1,0:T(8,128)(2,1)S(1)} collective-permute-done((bf16[128,2048]{1,0:T(8,128)(2,1)S(1)}, bf16[128,2048]{1,0:T(8,128)(2,1)S(1)}, u32[]{:S(2)}, u32[]{:S(2)}) %collective-permute-start.38) | collective-permute-done | bytes 524320 | tf_op jit(solution)/shard_map/ppermute | solution.py:116
  290.3 8.8 %shard_map.172 = (f32[1792,2048]{1,0:T(8,128)}, f32[128,896]{1,0:T(8,128)S(1)}) custom-call(bf16[128,896]{1,0:T(8,128)(2,1)S(1)} %get-tuple-element.88.refs_0_, bf16[128,896]{1,0:T(8,128)(2,1)S(1)} %get-tuple-element.87.refs_1_, bf16[128,896]{1,0:T(8,128)(2,1)S(1)} %collective-permute-done.12.refs_2_, ...), custom_call_target="tpu_custom_call", output_to_operand_aliasing={{1}: (17, {})} | custom-call | flops 3758096384 | bytes 18612224 | tf_op jit(solution)/shard_map/pallas_call | solution.py:60
  333.1 14.5 %collective-permute-done.46.refs_9_ = bf16[128,1792]{1,0:T(8,128)(2,1)S(1)} collective-permute-done((bf16[128,1792]{1,0:T(8,128)(2,1)S(1)}, bf16[128,1792]{1,0:T(8,128)(2,1)S(1)}, u32[]{:S(2)}, u32[]{:S(2)}) %collective-permute-start.46) | collective-permute-done | bytes 458784 | tf_op jit(solution)/shard_map/ppermute | solution.py:179
  353.8 9.0 %collective-permute-done.47.refs_10_ = bf16[128,1792]{1,0:T(8,128)(2,1)S(1)} collective-permute-done((bf16[128,1792]{1,0:T(8,128)(2,1)S(1)}, bf16[128,1792]{1,0:T(8,128)(2,1)S(1)}, u32[]{:S(2)}, u32[]{:S(2)}) %collective-permute-start.47) | collective-permute-done | bytes 458784 | tf_op jit(solution)/shard_map/ppermute | solution.py:179
  365.4 7.4 %collective-permute-done.50.refs_10_ = bf16[128,1792]{1,0:T(8,128)(2,1)S(1)} collective-permute-done((bf16[128,1792]{1,0:T(8,128)(2,1)S(1)}, bf16[128,1792]{1,0:T(8,128)(2,1)S(1)}, u32[]{:S(2)}, u32[]{:S(2)}) %collective-permute-start.50) | collective-permute-done | bytes 458784 | tf_op jit(solution)/shard_map/ppermute | solution.py:179
  375.5 7.0 %collective-permute-done.48.refs_11_ = bf16[128,1792]{1,0:T(8,128)(2,1)S(1)} collective-permute-done((bf16[128,1792]{1,0:T(8,128)(2,1)S(1)}, bf16[128,1792]{1,0:T(8,128)(2,1)S(1)}, u32[]{:S(2)}, u32[]{:S(2)}) %collective-permute-start.48) | collective-permute-done | bytes 458784 | tf_op jit(solution)/shard_map/ppermute | solution.py:179
  403.6 8.7 %shard_map.173 = (f32[2048,1792]{1,0:T(8,128)}, f32[128,2048]{1,0:T(8,128)S(1)}) custom-call(bf16[64,2048]{1,0:T(8,128)(2,1)S(1)} %get-tuple-element.71.refs_0_, bf16[64,2048]{1,0:T(8,128)(2,1)S(1)} %get-tuple-element.75.refs_1_, bf16[64,2048]{1,0:T(8,128)(2,1)S(1)} %get-tuple-element.74.refs_2_, ...), custom_call_target="tpu_custom_call", output_to_operand_aliasing={{1}: (13, {})} | custom-call | flops 3758096384 | bytes 18612224 | tf_op jit(solution)/shard_map/pallas_call | solution.py:60
  413.6 8.6 %shard_map.174 = (f32[2048,1792]{1,0:T(8,128)}, f32[64,2048]{1,0:T(8,128)S(1)}) custom-call(bf16[64,2048]{1,0:T(8,128)(2,1)S(1)} %get-tuple-element.71.refs_0_, bf16[64,2048]{1,0:T(8,128)(2,1)S(1)} %get-tuple-element.75.refs_1_, bf16[64,2048]{1,0:T(8,128)(2,1)S(1)} %get-tuple-element.74.refs_2_, ...), custom_call_target="tpu_custom_call", output_to_operand_aliasing={{1}: (13, {})} | custom-call | flops 3758096384 | bytes 18612224 | tf_op jit(solution)/shard_map/pallas_call | solution.py:60
  422.6 4.3 collective-permute-start.59
  (306 shorter events, 182.7 us)
Async XLA Ops:
  30.7 15.5 %collective-permute-start.3 = (bf16[128,1792]{1,0:T(8,128)(2,1)S(1)}, bf16[128,1792]{1,0:T(8,128)(2,1)S(1)}, u32[]{:S(2)}, u32[]{:S(2)}) collective-permute-start(bf16[128,1792]{1,0:T(8,128)(2,1)S(1)} %convolution_convert_fusion.1), channel_id=1, source_target_pairs={{0,8},{8,16},{16,24},{24,0},{1,9},{9,17},{17,25},{25,1},{2,10},{10... | collective-permute-start | bytes 1376264 | tf_op jit(solution)/shard_map/ppermute | solution.py:179
  34.8 21.4 %collective-permute-start.9 = (bf16[128,1792]{1,0:T(8,128)(2,1)}, bf16[128,1792]{1,0:T(8,128)(2,1)}, u32[]{:S(2)}, u32[]{:S(2)}) collective-permute-start(bf16[128,1792]{1,0:T(8,128)(2,1)} %convolution_convert_fusion), channel_id=1, source_target_pairs={{0,8},{8,16},{16,24},{24,0},{1,9},{9,17},{17,25},{25,1},{2,10},{10... | collective-permute-start | bytes 1376264 | tf_op jit(solution)/shard_map/ppermute | solution.py:179
  48.2 17.7 %collective-permute-start.4 = (bf16[128,1792]{1,0:T(8,128)(2,1)}, bf16[128,1792]{1,0:T(8,128)(2,1)S(1)}, u32[]{:S(2)}, u32[]{:S(2)}) collective-permute-start(bf16[128,1792]{1,0:T(8,128)(2,1)} %fusion.7), channel_id=1, source_target_pairs={{0,8},{8,16},{16,24},{24,0},{1,9},{9,17},{17,25},{25,1},{2,10},{10... | collective-permute-start | bytes 1376264 | tf_op jit(solution)/shard_map/ppermute | solution.py:179
  50.9 25.6 %all-to-all-start = ((bf16[16,8,2048]{2,0,1:T(8,128)(2,1)}), bf16[16,8,2048]{2,0,1:T(8,128)(2,1)S(1)}, u32[]{:S(2)}, u32[]{:S(2)}) async-start(bf16[16,8,2048]{2,0,1:T(8,128)(2,1)} %bitcast.57), calls=%async_computation | async-start | bytes 1048576 | tf_op jit(solution)/shard_map/all_to_all | solution.py:243
  61.1 15.4 %collective-permute-start.10 = (bf16[128,1792]{1,0:T(8,128)(2,1)}, bf16[128,1792]{1,0:T(8,128)(2,1)}, u32[]{:S(2)}, u32[]{:S(2)}) collective-permute-start(bf16[128,1792]{1,0:T(8,128)(2,1)} %fusion.9), channel_id=1, source_target_pairs={{0,8},{8,16},{16,24},{24,0},{1,9},{9,17},{17,25},{25,1},{2,10},{10... | collective-permute-start | bytes 1376264 | tf_op jit(solution)/shard_map/ppermute | solution.py:179
  67.7 16.6 %collective-permute-start.8 = (f32[512]{0:T(512)S(1)}, f32[512]{0:T(512)S(1)}, u32[]{:S(2)}, u32[]{:S(2)}) collective-permute-start(f32[512]{0:T(512)S(1)} %maximum_select_fusion.1), channel_id=1, source_target_pairs={{0,24},{8,16},{16,8},{24,0},{1,25},{9,17},{17,9},{25,1},{2,26},{10... | collective-permute-start | bytes 6152 | tf_op jit(solution)/shard_map/ppermute | solution.py:212
  69.7 14.6 %collective-permute-start.7 = (f32[512]{0:T(512)S(1)}, f32[512]{0:T(512)S(1)}, u32[]{:S(2)}, u32[]{:S(2)}) collective-permute-start(f32[512]{0:T(512)S(1)} %maximum_select_fusion.1), channel_id=1, source_target_pairs={{0,16},{8,24},{16,0},{24,8},{1,17},{9,25},{17,1},{25,9},{2,18},{10... | collective-permute-start | bytes 6152 | tf_op jit(solution)/shard_map/ppermute | solution.py:212
  69.7 14.6 %collective-permute-start.6 = (f32[512]{0:T(512)S(1)}, f32[512]{0:T(512)S(1)}, u32[]{:S(2)}, u32[]{:S(2)}) collective-permute-start(f32[512]{0:T(512)S(1)} %maximum_select_fusion.1), channel_id=1, source_target_pairs={{0,8},{8,0},{16,24},{24,16},{1,9},{9,1},{17,25},{25,17},{2,10},{10... | collective-permute-start | bytes 6152 | tf_op jit(solution)/shard_map/ppermute | solution.py:212
  76.4 15.4 %collective-permute-start.5 = (bf16[128,1792]{1,0:T(8,128)(2,1)S(1)}, bf16[128,1792]{1,0:T(8,128)(2,1)}, u32[]{:S(2)}, u32[]{:S(2)}) collective-permute-start(bf16[128,1792]{1,0:T(8,128)(2,1)S(1)} %fusion.6), channel_id=1, source_target_pairs={{0,8},{8,16},{16,24},{24,0},{1,9},{9,17},{17,25},{25,1},{2,10},{10... | collective-permute-start | bytes 1376264 | tf_op jit(solution)/shard_map/ppermute | solution.py:179
  83.2 16.1 %collective-permute-start.11 = (bf16[128,1792]{1,0:T(8,128)(2,1)S(1)}, bf16[128,1792]{1,0:T(8,128)(2,1)S(1)}, u32[]{:S(2)}, u32[]{:S(2)}) collective-permute-start(bf16[128,1792]{1,0:T(8,128)(2,1)S(1)} %fusion.8), channel_id=1, source_target_pairs={{0,8},{8,16},{16,24},{24,0},{1,9},{9,17},{17,25},{25,1},{2,10},{10... | collective-permute-start | bytes 1376264 | tf_op jit(solution)/shard_map/ppermute | solution.py:179
  100.8 12.9 %collective-permute-start.12 = (bf16[128,896]{1,0:T(8,128)(2,1)S(1)}, bf16[128,896]{1,0:T(8,128)(2,1)S(1)}, u32[]{:S(2)}, u32[]{:S(2)}) collective-permute-start(bf16[128,896]{1,0:T(8,128)(2,1)S(1)} %get-tuple-element.88.refs_0_), channel_id=1, source_target_pairs={{0,8},{8,16},{16,24},{24,0},{1,9},{9,17},{17,25},{25,1},{2,10},{10... | collective-permute-start | bytes 688136 | tf_op jit(solution)/shard_map/ppermute | solution.py:179
  100.8 12.1 %collective-permute-start.13 = (bf16[128,896]{1,0:T(8,128)(2,1)S(1)}, bf16[128,896]{1,0:T(8,128)(2,1)S(1)}, u32[]{:S(2)}, u32[]{:S(2)}) collective-permute-start(bf16[128,896]{1,0:T(8,128)(2,1)S(1)} %get-tuple-element.87.refs_1_), channel_id=1, source_target_pairs={{0,8},{8,16},{16,24},{24,0},{1,9},{9,17},{17,25},{25,1},{2,10},{10... | collective-permute-start | bytes 688136 | tf_op jit(solution)/shard_map/ppermute | solution.py:179
  113.6 13.5 %collective-permute-start.14 = (bf16[128,896]{1,0:T(8,128)(2,1)S(1)}, bf16[128,896]{1,0:T(8,128)(2,1)S(1)}, u32[]{:S(2)}, u32[]{:S(2)}) collective-permute-start(bf16[128,896]{1,0:T(8,128)(2,1)S(1)} %collective-permute-done.12.refs_2_), channel_id=1, source_target_pairs={{0,8},{8,16},{16,24},{24,0},{1,9},{9,17},{17,25},{25,1},{2,10},{10... | collective-permute-start | bytes 688136 | tf_op jit(solution)/shard_map/ppermute | solution.py:179
  171.0 11.0 %collective-permute-start.23 = (bf16[128,1024]{1,0:T(8,128)(2,1)S(1)}, bf16[128,1024]{1,0:T(8,128)(2,1)S(1)}, u32[]{:S(2)}, u32[]{:S(2)}) collective-permute-start(bf16[128,1024]{1,0:T(8,128)(2,1)S(1)} %convolution_convert_fusion.3), channel_id=1, source_target_pairs={{0,8},{8,16},{16,24},{24,0},{1,9},{9,17},{17,25},{25,1},{2,10},{10... | collective-permute-start | bytes 786440 | tf_op jit(solution)/shard_map/ppermute | solution.py:179
  171.8 15.8 %collective-permute-start.26 = (bf16[128,1024]{1,0:T(8,128)(2,1)S(1)}, bf16[128,1024]{1,0:T(8,128)(2,1)S(1)}, u32[]{:S(2)}, u32[]{:S(2)}) collective-permute-start(bf16[128,1024]{1,0:T(8,128)(2,1)S(1)} %convolution_convert_fusion.2), channel_id=1, source_target_pairs={{0,8},{8,16},{16,24},{24,0},{1,9},{9,17},{17,25},{25,1},{2,10},{10... | collective-permute-start | bytes 786440 | tf_op jit(solution)/shard_map/ppermute | solution.py:179
  182.7 10.8 %collective-permute-start.24 = (bf16[128,1024]{1,0:T(8,128)(2,1)S(1)}, bf16[128,1024]{1,0:T(8,128)(2,1)S(1)}, u32[]{:S(2)}, u32[]{:S(2)}) collective-permute-start(bf16[128,1024]{1,0:T(8,128)(2,1)S(1)} %fusion.29), channel_id=1, source_target_pairs={{0,8},{8,16},{16,24},{24,0},{1,9},{9,17},{17,25},{25,1},{2,10},{10... | collective-permute-start | bytes 786440 | tf_op jit(solution)/shard_map/ppermute | solution.py:179
  188.3 11.0 %collective-permute-start.27 = (bf16[128,1024]{1,0:T(8,128)(2,1)S(1)}, bf16[128,1024]{1,0:T(8,128)(2,1)S(1)}, u32[]{:S(2)}, u32[]{:S(2)}) collective-permute-start(bf16[128,1024]{1,0:T(8,128)(2,1)S(1)} %fusion.31), channel_id=1, source_target_pairs={{0,8},{8,16},{16,24},{24,0},{1,9},{9,17},{17,25},{25,1},{2,10},{10... | collective-permute-start | bytes 786440 | tf_op jit(solution)/shard_map/ppermute | solution.py:179
  194.2 11.1 %collective-permute-start.25 = (bf16[128,1024]{1,0:T(8,128)(2,1)S(1)}, bf16[128,1024]{1,0:T(8,128)(2,1)S(1)}, u32[]{:S(2)}, u32[]{:S(2)}) collective-permute-start(bf16[128,1024]{1,0:T(8,128)(2,1)S(1)} %fusion.28), channel_id=1, source_target_pairs={{0,8},{8,16},{16,24},{24,0},{1,9},{9,17},{17,25},{25,1},{2,10},{10... | collective-permute-start | bytes 786440 | tf_op jit(solution)/shard_map/ppermute | solution.py:179
  210.8 15.4 %collective-permute-start.29 = (bf16[128,1024]{1,0:T(8,128)(2,1)S(1)}, bf16[128,1024]{1,0:T(8,128)(2,1)S(1)}, u32[]{:S(2)}, u32[]{:S(2)}) collective-permute-start(bf16[128,1024]{1,0:T(8,128)(2,1)S(1)} %get-tuple-element.79.refs_8_), channel_id=1, source_target_pairs={{0,8},{8,16},{16,24},{24,0},{1,9},{9,17},{17,25},{25,1},{2,10},{10... | collective-permute-start | bytes 786440 | tf_op jit(solution)/shard_map/ppermute | solution.py:179
  212.4 12.4 %collective-permute-start.30 = (bf16[128,1024]{1,0:T(8,128)(2,1)S(1)}, bf16[128,1024]{1,0:T(8,128)(2,1)S(1)}, u32[]{:S(2)}, u32[]{:S(2)}) collective-permute-start(bf16[128,1024]{1,0:T(8,128)(2,1)S(1)} %get-tuple-element.80.refs_9_), channel_id=1, source_target_pairs={{0,8},{8,16},{16,24},{24,0},{1,9},{9,17},{17,25},{25,1},{2,10},{10... | collective-permute-start | bytes 786440 | tf_op jit(solution)/shard_map/ppermute | solution.py:179
  224.7 11.0 %collective-permute-start.32 = (bf16[128,1024]{1,0:T(8,128)(2,1)S(1)}, bf16[128,1024]{1,0:T(8,128)(2,1)S(1)}, u32[]{:S(2)}, u32[]{:S(2)}) collective-permute-start(bf16[128,1024]{1,0:T(8,128)(2,1)S(1)} %collective-permute-done.30.refs_11_), channel_id=1, source_target_pairs={{0,8},{8,16},{16,24},{24,0},{1,9},{9,17},{17,25},{25,1},{2,10},{10... | collective-permute-start | bytes 786440 | tf_op jit(solution)/shard_map/ppermute | solution.py:179
  226.3 15.1 %collective-permute-start.31 = (bf16[128,1024]{1,0:T(8,128)(2,1)S(1)}, bf16[128,1024]{1,0:T(8,128)(2,1)S(1)}, u32[]{:S(2)}, u32[]{:S(2)}) collective-permute-start(bf16[128,1024]{1,0:T(8,128)(2,1)S(1)} %collective-permute-done.29.refs_10_), channel_id=1, source_target_pairs={{0,8},{8,16},{16,24},{24,0},{1,9},{9,17},{17,25},{25,1},{2,10},{10... | collective-permute-start | bytes 786440 | tf_op jit(solution)/shard_map/ppermute | solution.py:179
  235.8 10.4 %collective-permute-start.34 = (bf16[128,1024]{1,0:T(8,128)(2,1)S(1)}, bf16[128,1024]{1,0:T(8,128)(2,1)S(1)}, u32[]{:S(2)}, u32[]{:S(2)}) collective-permute-start(bf16[128,1024]{1,0:T(8,128)(2,1)S(1)} %collective-permute-done.32.refs_13_), channel_id=1, source_target_pairs={{0,8},{8,16},{16,24},{24,0},{1,9},{9,17},{17,25},{25,1},{2,10},{10... | collective-permute-start | bytes 786440 | tf_op jit(solution)/shard_map/ppermute | solution.py:179
  288.8 10.3 %collective-permute-start.43 = (bf16[128,896]{1,0:T(8,128)(2,1)S(1)}, bf16[128,896]{1,0:T(8,128)(2,1)S(1)}, u32[]{:S(2)}, u32[]{:S(2)}) collective-permute-start(bf16[128,896]{1,0:T(8,128)(2,1)S(1)} %convolution_convert_fusion.4.refs_16_), channel_id=1, source_target_pairs={{0,8},{8,16},{16,24},{24,0},{1,9},{9,17},{17,25},{25,1},{2,10},{10... | collective-permute-start | bytes 688136 | tf_op jit(solution)/shard_map/ppermute | solution.py:179
  288.9 14.3 %collective-permute-start.40 = (bf16[128,896]{1,0:T(8,128)(2,1)S(1)}, bf16[128,896]{1,0:T(8,128)(2,1)S(1)}, u32[]{:S(2)}, u32[]{:S(2)}) collective-permute-start(bf16[128,896]{1,0:T(8,128)(2,1)S(1)} %convolution_convert_fusion.5), channel_id=1, source_target_pairs={{0,8},{8,16},{16,24},{24,0},{1,9},{9,17},{17,25},{25,1},{2,10},{10... | collective-permute-start | bytes 688136 | tf_op jit(solution)/shard_map/ppermute | solution.py:179
  325.3 24.9 %collective-permute-start.49 = (bf16[128,1792]{1,0:T(8,128)(2,1)S(1)}, bf16[128,1792]{1,0:T(8,128)(2,1)S(1)}, u32[]{:S(2)}, u32[]{:S(2)}) collective-permute-start(bf16[128,1792]{1,0:T(8,128)(2,1)S(1)} %get-tuple-element.53.refs_8_), channel_id=1, source_target_pairs={{0,8},{8,16},{16,24},{24,0},{1,9},{9,17},{17,25},{25,1},{2,10},{10... | collective-permute-start | bytes 1376264 | tf_op jit(solution)/shard_map/ppermute | solution.py:179
  327.8 19.8 %collective-permute-start.46 = (bf16[128,1792]{1,0:T(8,128)(2,1)S(1)}, bf16[128,1792]{1,0:T(8,128)(2,1)S(1)}, u32[]{:S(2)}, u32[]{:S(2)}) collective-permute-start(bf16[128,1792]{1,0:T(8,128)(2,1)S(1)} %get-tuple-element.54.refs_8_), channel_id=1, source_target_pairs={{0,8},{8,16},{16,24},{24,0},{1,9},{9,17},{17,25},{25,1},{2,10},{10... | collective-permute-start | bytes 1376264 | tf_op jit(solution)/shard_map/ppermute | solution.py:179
  347.6 15.3 %collective-permute-start.47 = (bf16[128,1792]{1,0:T(8,128)(2,1)S(1)}, bf16[128,1792]{1,0:T(8,128)(2,1)S(1)}, u32[]{:S(2)}, u32[]{:S(2)}) collective-permute-start(bf16[128,1792]{1,0:T(8,128)(2,1)S(1)} %collective-permute-done.46.refs_9_), channel_id=1, source_target_pairs={{0,8},{8,16},{16,24},{24,0},{1,9},{9,17},{17,25},{25,1},{2,10},{10... | collective-permute-start | bytes 1376264 | tf_op jit(solution)/shard_map/ppermute | solution.py:179
  350.1 22.6 %collective-permute-start.50 = (bf16[128,1792]{1,0:T(8,128)(2,1)S(1)}, bf16[128,1792]{1,0:T(8,128)(2,1)S(1)}, u32[]{:S(2)}, u32[]{:S(2)}) collective-permute-start(bf16[128,1792]{1,0:T(8,128)(2,1)S(1)} %collective-permute-done.49.refs_9_), channel_id=1, source_target_pairs={{0,8},{8,16},{16,24},{24,0},{1,9},{9,17},{17,25},{25,1},{2,10},{10... | collective-permute-start | bytes 1376264 | tf_op jit(solution)/shard_map/ppermute | solution.py:179
  362.9 19.7 %collective-permute-start.48 = (bf16[128,1792]{1,0:T(8,128)(2,1)S(1)}, bf16[128,1792]{1,0:T(8,128)(2,1)S(1)}, u32[]{:S(2)}, u32[]{:S(2)}) collective-permute-start(bf16[128,1792]{1,0:T(8,128)(2,1)S(1)} %collective-permute-done.47.refs_10_), channel_id=1, source_target_pairs={{0,8},{8,16},{16,24},{24,0},{1,9},{9,17},{17,25},{25,1},{2,10},{10... | collective-permute-start | bytes 1376264 | tf_op jit(solution)/shard_map/ppermute | solution.py:179
  372.7 16.0 %collective-permute-start.51 = (bf16[128,1792]{1,0:T(8,128)(2,1)S(1)}, bf16[128,1792]{1,0:T(8,128)(2,1)S(1)}, u32[]{:S(2)}, u32[]{:S(2)}) collective-permute-start(bf16[128,1792]{1,0:T(8,128)(2,1)S(1)} %collective-permute-done.50.refs_10_), channel_id=1, source_target_pairs={{0,8},{8,16},{16,24},{24,0},{1,9},{9,17},{17,25},{25,1},{2,10},{10... | collective-permute-start | bytes 1376264 | tf_op jit(solution)/shard_map/ppermute | solution.py:179
  402.3 10.0 %collective-permute-start.53 = (bf16[128,2048]{1,0:T(8,128)(2,1)S(1)}, bf16[128,2048]{1,0:T(8,128)(2,1)S(1)}, u32[]{:S(2)}, u32[]{:S(2)}) collective-permute-start(bf16[128,2048]{1,0:T(8,128)(2,1)S(1)} %slice.400.refs_12_), channel_id=1, source_target_pairs={{0,4},{1,3},{2,6},{3,1},{4,0},{5,7},{6,2},{7,5},{8,12},{9,11},{10,... | collective-permute-start | bytes 1572872 | tf_op jit(solution)/shard_map/ppermute | solution.py:136
  (70 other events, 647.6 us)
